TPU v7x, 32 devices: a whole 2x2x4 slice. The times are simulated.
32 devices in a mesh: expert: 16 (over z, x, core), mp: 2 (over y).
Axes of the slice: x: 2, y: 2, z: 4, core: 2. Of those that a mesh axis runs over, the one named last changes fastest.
Arguments:
- routes: int32 [4096], P('expert'), may hold values from 0 to 15
- slots: int32 [4096], P('expert'), may hold values from -1 to 19, as said below
- gate: float32 [4096], P('expert'), may hold values from 0.2 to 1
- grad_out: bfloat16 [4096, 4096], P('expert', 'mp'), may hold values from -6 to 6
- saved_inputs: bfloat16 [16, 320, 4096], P('expert'), may hold values from -6 to 6
- w_in: bfloat16 [16, 4096, 5120], P('expert', None, 'mp'), may hold values from -0.09375 to 0.09375
- w_out: bfloat16 [16, 5120, 4096], P('expert', 'mp'), may hold values from -0.078125 to 0.078125
- dense_partial: float32 [16, 256, 4096], P('expert', None, 'mp'), may hold values from -6 to 6
Outputs:
- grad_in: bfloat16 [4096, 4096], P('expert', 'mp')
- dense_sum: float32 [256, 4096], P(None, 'mp')
Inputs may be any that keep to these rules, and one draw needn't show every extreme that they name: Within each group, the tokens routed to one expert take slots 0, 1, 2, ... in token order; the k-th such token has slot k - 1 if k <= 20, else -1.
All inputs are finite; a program needn't handle non-finite values.
Results may differ from a plain program's by a relative error of at most 0.0058.
Values may be sent and summed in bfloat16 or wider, within the bound.
No kernel may reach another device: no remote copies, remote signals or barrier semaphores. Data moves between devices by JAX's collectives and lax.ppermute only.
A program may use at most 128 MiB of HBM per device.

v0:
```python
import math

import jax
import jax.numpy as jnp
from jax import lax
from jax.sharding import PartitionSpec as P

gelu_scale = math.sqrt(2.0 / math.pi)
cubic_coef = 0.044715


def slope_of(preact):
    inner = gelu_scale * (preact + cubic_coef * preact * preact * preact)
    tanh_val = jnp.tanh(inner)
    return 0.5 * (1.0 + tanh_val) + 0.5 * preact * (1.0 - tanh_val * tanh_val) * gelu_scale * (
        1.0 + 3.0 * cubic_coef * preact * preact
    )


def on_device(routes, slots, gate, grad_out, saved_inputs, w_in, w_out, dense_partial):
    groups = lax.axis_size("expert")
    slot_rows = saved_inputs.shape[1]
    capacity = slot_rows // groups
    features = grad_out.shape[1]
    tok_count = grad_out.shape[0]
    dense_sum = lax.psum(dense_partial[0], "expert")
    scaled = (gate[:, None] * grad_out.astype(jnp.float32)).astype(jnp.bfloat16)
    target = jnp.where(slots >= 0, routes * capacity + slots, -1)
    slot_table = (
        lax.broadcasted_iota(jnp.int32, (groups * capacity, tok_count), 0) == target[None, :]
    ).astype(jnp.bfloat16)
    outgoing = jnp.dot(slot_table, scaled, preferred_element_type=jnp.float32).astype(jnp.bfloat16)
    outgoing = outgoing.reshape(groups, capacity, features)
    incoming = lax.all_to_all(outgoing, "expert", split_axis=0, concat_axis=0, tiled=True).reshape(
        slot_rows, features
    )
    preact = jnp.dot(saved_inputs[0], w_in[0], preferred_element_type=jnp.float32)
    slopes = slope_of(preact)
    out_rows = w_out[0]
    upstream = lax.dot_general(
        lax.all_gather(incoming, "mp", axis=1, tiled=True),
        out_rows,
        (((1,), (1,)), ((), ())),
        preferred_element_type=jnp.float32,
    )
    hidden_grad = (upstream * slopes).astype(jnp.bfloat16)
    in_rows = w_in[0]
    reduced = lax.psum_scatter(
        lax.dot_general(
            in_rows, hidden_grad, (((1,), (1,)), ((), ())), preferred_element_type=jnp.float32
        ),
        "mp",
        scatter_dimension=0,
        tiled=True,
    )
    outbound = reduced.astype(jnp.bfloat16).reshape(features, groups, capacity)
    returned = lax.all_to_all(outbound, "expert", split_axis=1, concat_axis=1, tiled=True)
    flattened = returned.reshape(features, groups * capacity)
    grad_in = jnp.dot(flattened, slot_table, preferred_element_type=jnp.float32).T.astype(
        jnp.bfloat16
    )
    return (grad_in, dense_sum)


def solution(mesh):
    in_specs = (
        P("expert"),
        P("expert"),
        P("expert"),
        P("expert", "mp"),
        P("expert", None, None),
        P("expert", None, "mp"),
        P("expert", "mp", None),
        P("expert", None, "mp"),
    )
    out_specs = (P("expert", "mp"), P(None, "mp"))
    return jax.shard_map(
        on_device, mesh=mesh, in_specs=in_specs, out_specs=out_specs, check_vma=False
    )
```

profile of v0, /device:TPU:9, one launch (start us, length us, event | category | flops | bytes accessed | tf_op | source)
XLA Modules:
  0.0 325.2 jit_solution(10927059319903911736)
XLA Ops:
  8.0 0.0 copy-start
  8.0 0.0 all-gather.2.cloned.1.call-start
  8.1 0.9 compare_select_fusion
  8.9 2.9 convolution_convert_fusion
  11.8 3.2 reshape.18
  15.0 43.3 %all_to_all.10 = bf16[16,20,2048]{2,1,0:T(8,128)(2,1)} all-to-all(bf16[16,20,2048]{2,1,0:T(8,128)(2,1)} %reshape.18), channel_id=1, replica_groups=mesh['expert'=16,'mp'=2] {'expert'}, dimensions={0} | all-to-all | bytes 2621440 | tf_op jit(solution)/shard_map/all_to_all | solution.py:34
  58.3 3.3 %reshape.19 = bf16[320,2048]{1,0:T(8,128)(2,1)} reshape(bf16[16,20,2048]{2,1,0:T(8,128)(2,1)} %all_to_all.10) | data formatting | bytes 2621440 | tf_op jit(solution)/shard_map/reshape | solution.py:34
  61.6 0.0 all-gather.2.cloned.1.call-update
  61.6 0.0 reduce-scatter.2.cloned.1.call-start
  61.7 0.0 copy-done
  61.7 12.8 %fusion.2 = f32[320,2560]{1,0:T(8,128)} fusion(bf16[1,4096,2560]{2,1,0:T(8,128)(2,1)} %param.13, bf16[1,320,4096]{2,1,0:T(8,128)(2,1)S(1)} %copy-done), kind=kOutput, calls=%fused_computation.2 | convolution fusion | flops 6710886400 | bytes 26869760 | tf_op jit(solution)/shard_map/dot_general | solution.py:37
  74.5 25.4 %all-gather.2.cloned.1.call-done = bf16[320,4096]{1,0:T(8,128)(2,1)} async-done(((bf16[320,2048]{1,0:T(8,128)(2,1)}), bf16[320,4096]{1,0:T(8,128)(2,1)}) %all-gather.2.cloned.1.call-update) | async-done | bytes 2621456 | tf_op jit(solution)/shard_map/all_gather | solution.py:41
  99.9 24.1 %fusion.6 = f32[4096,320]{0,1:T(8,128)} fusion(bf16[1,4096,2560]{2,1,0:T(8,128)(2,1)} %param.13, bf16[320,4096]{1,0:T(8,128)(2,1)} %all-gather.2.cloned.1.call-done, bf16[1,2560,4096]{2,1,0:T(8,128)(2,1)} %param.14, f32[320,2560]{1,0:T(8,128)} %fusion.2), kind=kOutput, calls=%fused_computation.6 | convolution fusion | flops 13437337600 | bytes 53084160 | tf_op jit(solution)/shard_map/dot_general | solution.py:49
  124.0 0.0 reduce-scatter.2.cloned.1.call-update
  124.0 65.8 %reduce-scatter.2.cloned.1.call-done = f32[2048,320]{0,1:T(8,128)} async-done(((f32[4096,320]{0,1:T(8,128)}), f32[2048,320]{0,1:T(8,128)}) %reduce-scatter.2.cloned.1.call-update) | async-done | bytes 2621456 | tf_op jit(solution)/shard_map/reduce_scatter | solution.py:48
  189.9 1.9 convert_element_type.23
  191.8 1.3 reshape.20
  193.1 6.4 %all-to-all-start.1 = ((bf16[2048,16,20]{0,2,1:T(8,128)(2,1)}), bf16[2048,16,20]{0,2,1:T(8,128)(2,1)}, u32[]{:S(2)}, u32[]{:S(2)}) async-start(bf16[2048,16,20]{0,2,1:T(8,128)(2,1)} %reshape.20), calls=%async_computation.2 | async-start | bytes 3145728 | tf_op jit(solution)/shard_map/all_to_all | solution.py:57
  199.5 0.0 all-reduce.2.cloned.1.call-start
  199.5 0.5 all-reduce.2.cloned.1.call-update
  200.0 47.1 %all-to-all-done.1 = bf16[2048,16,20]{0,2,1:T(8,128)(2,1)} async-done(((bf16[2048,16,20]{0,2,1:T(8,128)(2,1)}), bf16[2048,16,20]{0,2,1:T(8,128)(2,1)}, u32[]{:S(2)}, u32[]{:S(2)}) %all-to-all-start.1) | async-done | bytes 1310752 | tf_op jit(solution)/shard_map/all_to_all | solution.py:57
  247.1 0.0 copy-start.1
  247.1 3.4 %reshape.21 = bf16[2048,320]{0,1:T(8,128)(2,1)} reshape(bf16[2048,16,20]{0,2,1:T(8,128)(2,1)} %all-to-all-done.1) | data formatting | bytes 2621440 | tf_op jit(solution)/shard_map/reshape | solution.py:58
  250.6 3.0 convolution_convert_fusion.1
  253.6 61.0 %all-reduce.2.cloned.1.call-done = f32[256,2048]{1,0:T(8,128)} async-done(((f32[256,2048]{1,0:T(8,128)}), f32[256,2048]{1,0:T(8,128)}) %all-reduce.2.cloned.1.call-update) | async-done | bytes 2097168 | tf_op jit(solution)/shard_map/psum | solution.py:26
  314.7 3.1 copy.12
  317.8 0.0 copy-done.1
Async XLA Ops:
  8.0 53.7 %copy-start = (bf16[1,320,4096]{2,1,0:T(8,128)(2,1)S(1)}, bf16[1,320,4096]{2,1,0:T(8,128)(2,1)}, u32[]{:S(2)}) copy-start(bf16[1,320,4096]{2,1,0:T(8,128)(2,1)} %param.12) | copy-start | bytes 7864324
  8.0 91.9 %all-gather.2.cloned.1.call-start = ((), (), s32[]{:S(2)}) async-start(), calls=%async_computation.3 | async-start | bytes 3932160 | tf_op jit(solution)/shard_map/all_gather | solution.py:41
  61.6 128.3 %reduce-scatter.2.cloned.1.call-start = ((), (), s32[]{:S(2)}) async-start(), calls=%async_computation.4 | async-start | bytes 7864320 | tf_op jit(solution)/shard_map/reduce_scatter | solution.py:48
  193.1 54.0 %all-to-all-start.1 = ((bf16[2048,16,20]{0,2,1:T(8,128)(2,1)}), bf16[2048,16,20]{0,2,1:T(8,128)(2,1)}, u32[]{:S(2)}, u32[]{:S(2)}) async-start(bf16[2048,16,20]{0,2,1:T(8,128)(2,1)} %reshape.20), calls=%async_computation.2 | async-start | bytes 3145728 | tf_op jit(solution)/shard_map/all_to_all | solution.py:57
  199.5 115.2 %all-reduce.2.cloned.1.call-start = ((), (), s32[]{:S(2)}) async-start(), calls=%async_computation.5 | async-start | bytes 4194304 | tf_op jit(solution)/shard_map/psum | solution.py:26
  247.1 70.7 %copy-start.1 = (bf16[1,320,4096]{2,1,0:T(8,128)(2,1)S(1)}, bf16[1,320,4096]{2,1,0:T(8,128)(2,1)}, u32[]{:S(2)}) copy-start(bf16[1,320,4096]{2,1,0:T(8,128)(2,1)} %param.12) | copy-start | bytes 7864324
Sparse Core Ops, SparseCore 0:
  61.7 38.0 all-gather.1
  124.2 65.6 reduce-scatter.1
Sparse Core Ops, SparseCore 1:
  203.9 110.7 all-reduce.1
where the time goes:
time: 329 us; the launch traced here: 325 us
  waiting for transfers between devices  200 us (61%)
  blocking collectives  43.3 us (13%)
  matrix products  42.9 us (13%)
  between operations  15.5 us (5%)
  local copies, waits for them, and re-layouts  14.3 us (4%)
  starting transfers between devices  6.5 us (2%)
    reduce_scatter x1, waiting for transfers between devices, on_device(): lax.psum_scatter(lax.dot_general(in_rows, hidden_grad, (((1,), (1,)), (()...  65.8 us
    psum x1, waiting for transfers between devices, on_device(): dense_sum = lax.psum(dense_partial[0], 'expert')  61 us
    all_to_all x1, waiting for transfers between devices, on_device(): lax.all_to_all(outbound, 'expert', split_axis=1, concat_axis=1, tiled=True)  47.1 us
    all_to_all x1, blocking collectives, on_device(): lax.all_to_all(outgoing, 'expert', split_axis=0, concat_axis=0, tiled=True)  43.3 us
    all_gather x1, waiting for transfers between devices, on_device(): lax.all_gather(incoming, 'mp', axis=1, tiled=True)  25.4 us
    dot_general x1, matrix products, on_device(): lax.dot_general(in_rows, hidden_grad, (((1,), (1,)), ((), ())), preferred...  24.1 us
    dot_general x1, matrix products, on_device(): jnp.dot(saved_inputs[0], w_in[0], preferred_element_type=jnp.float32)  12.8 us
  transfers between devices with their start and end apart: 4, of which 4 were waited for; matrix products, arithmetic and copies ran while one was open for 6% of the time, Pallas kernels for 0%

commit v1 on v0

v1 whole, which is shorter than its diff:
```python
import math

import jax
import jax.numpy as jnp
from jax import lax
from jax.sharding import PartitionSpec as P

gelu_scale = math.sqrt(2.0 / math.pi)
cubic_coef = 0.044715
BF16 = jnp.bfloat16
F32 = jnp.float32
NT = (((1,), (1,)), ((), ()))


def slope_of(preact):
    inner = gelu_scale * (preact + cubic_coef * preact * preact * preact)
    tanh_val = jnp.tanh(inner)
    return 0.5 * (1.0 + tanh_val) + 0.5 * preact * (1.0 - tanh_val * tanh_val) * gelu_scale * (
        1.0 + 3.0 * cubic_coef * preact * preact
    )


def after(value, *others):
    return lax.optimization_barrier((value,) + others)[0]


def xor_send(value, axis, bit):
    size = lax.axis_size(axis)
    return lax.ppermute(value, axis, [(i, i ^ bit) for i in range(size)])


def halve(mine, axis, bit):
    rows = mine.shape[0] // 2
    upper = (lax.axis_index(axis) & bit) != 0
    kept = jnp.where(upper, mine[rows:], mine[:rows])
    sent = jnp.where(upper, mine[:rows], mine[rows:])
    return kept + xor_send(sent.astype(BF16), axis, bit).astype(F32)


def double(mine, axis, bit):
    upper = (lax.axis_index(axis) & bit) != 0
    other = xor_send(mine, axis, bit)
    return jnp.concatenate([jnp.where(upper, other, mine), jnp.where(upper, mine, other)], axis=0)


def bits_of(size):
    return [1 << i for i in range(size.bit_length() - 1)]


def summed_over(part, axis):
    bits = bits_of(lax.axis_size(axis))
    for bit in bits:
        part = halve(part, axis, bit)
    part = part.astype(BF16)
    for bit in reversed(bits):
        part = double(part, axis, bit)
    return part.astype(F32)


def one_hot(rows, columns):
    return (lax.broadcasted_iota(jnp.int32, (rows, columns.shape[0]), 0) == columns[None, :]).astype(BF16)


def dot(a, b):
    return jnp.dot(a, b, preferred_element_type=F32)


def chunk_widths(features, share):
    unit = 256
    if features % unit or features < 2 * unit:
        return [features]
    first = int(round(features * share / unit)) * unit
    return [first, features - first]


def on_device(routes, slots, gate, grad_out, saved_inputs, w_in, w_out, dense_partial):
    groups = lax.axis_size("expert")
    models = lax.axis_size("mp")
    me = lax.axis_index("mp")
    slot_rows = saved_inputs.shape[1]
    cap = slot_rows // groups
    tok_count, features = grad_out.shape
    pair = models == 2
    fold = 2 if pair and features % 512 == 0 else 1
    rows = fold * slot_rows

    dense_sum = summed_over(dense_partial[0], "expert")

    scaled = (gate[:, None] * grad_out.astype(F32)).astype(BF16)
    columns = jnp.concatenate(
        [jnp.where(slots >= 0, routes * (fold * cap) + h * cap + slots, -1) for h in range(fold)]
    )
    table = one_hot(rows, columns)
    slot = jnp.arange(slot_rows, dtype=jnp.int32)
    spread = [one_hot(rows, (slot // cap) * (fold * cap) + h * cap + slot % cap) for h in range(fold)]

    widths = chunk_widths(features, 0.625) if pair else [features]
    starts = [sum(widths[:i]) for i in range(len(widths))]

    def all_to_all(block):
        wide = block.shape[1]
        block = block.reshape(groups, fold * cap, wide)
        return lax.all_to_all(block, "expert", split_axis=0, concat_axis=0, tiled=True).reshape(rows, wide)

    mine = []
    for start, width in zip(starts, widths):
        part = width // fold
        stacked = jnp.concatenate(
            [scaled[:, start + h * part : start + (h + 1) * part] for h in range(fold)], axis=0
        )
        arrived = all_to_all(dot(table, stacked).astype(BF16))
        mine.append(
            jnp.concatenate(
                [
                    lax.dot_general(t, arrived, (((0,), (0,)), ((), ())), preferred_element_type=F32).astype(BF16)
                    for t in spread
                ],
                axis=1,
            )
        )

    slopes = slope_of(dot(saved_inputs[0], w_in[0]))

    if pair:
        theirs = [xor_send(x, "mp", 1) for x in mine]
        upstream = None
        for start, width, own, other in zip(starts, widths, mine, theirs):
            for who, x in ((me, own), (1 - me, other)):
                w = lax.dynamic_slice_in_dim(w_out[0], who * features + start, width, 1)
                term = lax.dot_general(x, w, NT, preferred_element_type=F32)
                upstream = term if upstream is None else upstream + term
    else:
        upstream = lax.dot_general(
            lax.all_gather(mine[0], "mp", axis=1, tiled=True), w_out[0], NT, preferred_element_type=F32
        )
    hidden = (upstream * slopes).astype(BF16)

    def share_of(who, start, width):
        w = lax.dynamic_slice_in_dim(w_in[0], who * features + start, width, 0)
        return lax.dot_general(hidden, w, NT, preferred_element_type=F32)

    outs = []
    if pair:
        sent = [
            xor_send(share_of(1 - me, start, width).astype(BF16), "mp", 1)
            for start, width in reversed(list(zip(starts, widths)))
        ][::-1]
    for i, (start, width) in reversed(list(enumerate(zip(starts, widths)))):
        part = width // fold
        if pair:
            total = (share_of(me, start, width) + sent[i].astype(F32)).astype(BF16)
        else:
            total = lax.psum_scatter(
                lax.dot_general(hidden, w_in[0], NT, preferred_element_type=F32),
                "mp",
                scatter_dimension=1,
                tiled=True,
            ).astype(BF16)
        folded = sum(dot(t, total[:, h * part : (h + 1) * part]) for h, t in enumerate(spread))
        back = all_to_all(folded.astype(BF16))
        outs = [
            lax.dot_general(
                table[:, h * tok_count : (h + 1) * tok_count],
                back,
                (((0,), (0,)), ((), ())),
                preferred_element_type=F32,
            ).astype(BF16)
            for h in range(fold)
        ] + outs
    return (jnp.concatenate(outs, axis=1), dense_sum)


def solution(mesh):
    in_specs = (
        P("expert"),
        P("expert"),
        P("expert"),
        P("expert", "mp"),
        P("expert", None, None),
        P("expert", None, "mp"),
        P("expert", "mp", None),
        P("expert", None, "mp"),
    )
    out_specs = (P("expert", "mp"), P(None, "mp"))
    return jax.shard_map(
        on_device, mesh=mesh, in_specs=in_specs, out_specs=out_specs, check_vma=False
    )
```

time: 329 us -> 184 us (0.56)
  waiting for transfers between devices: 200 us -> 46.2 us
  blocking collectives: 43.3 us -> 0 us
  starting transfers between devices: 6.5 us -> 42.3 us
  matrix products: 42.9 us -> 75.9 us
  between operations: 15.5 us -> 0.96 us
  other arithmetic: 2.77 us -> 13.7 us
  local copies, waits for them, and re-layouts: 14.3 us -> 3.91 us
    reduce_scatter x1 -> x0, waiting for transfers between devices: 65.8 us -> none  [on_device(): lax.psum_scatter(lax.dot_general(in_rows, hidden_grad, (((1,), (1,)), (()...]
    psum x1 -> x0, waiting for transfers between devices: 61 us -> none  [on_device(): dense_sum = lax.psum(dense_partial[0], 'expert')]
    all_to_all x1 -> x0, blocking collectives: 43.3 us -> none  [on_device(): lax.all_to_all(outgoing, 'expert', split_axis=0, concat_axis=0, tiled=True)]
    dot_general x4 -> x23, matrix products: 42.9 us -> 75.9 us  [the longest x4 27.6 us: on_device(): term = lax.dot_general(x, w, NT, preferred_element_type=F32)]
    all_to_all x1 -> x4, waiting for transfers between devices: 47.1 us -> 17.4 us  [all_to_all(): lax.all_to_all(block, 'expert', split_axis=0, concat_axis=0, tiled=True)]
    ppermute x0 -> x12, waiting for transfers between devices: none -> 28.8 us  [xor_send(): return lax.ppermute(value, axis, [(i, i ^ bit) for i in range(size)])]
    all_gather x1 -> x0, waiting for transfers between devices: 25.4 us -> none  [on_device(): lax.all_gather(incoming, 'mp', axis=1, tiled=True)]
    all_to_all x1 -> x4, starting transfers between devices: 6.38 us -> 25.3 us  [all_to_all(): lax.all_to_all(block, 'expert', split_axis=0, concat_axis=0, tiled=True)]
  transfers between devices with their start and end apart: 4 -> 16, of which waited for: 4 -> 7; matrix products, arithmetic and copies ran while one was open for 6% -> 46% of each run, Pallas kernels for 0% -> 0%
where the time goes in v1:
time: 184 us; the launch traced here: 183 us
  matrix products  75.9 us (41%)
  waiting for transfers between devices  46.2 us (25%)
  starting transfers between devices  42.3 us (23%)
  other arithmetic  13.7 us (7%)
  local copies, waits for them, and re-layouts  3.91 us (2%)
    ppermute x12, waiting for transfers between devices, xor_send(): return lax.ppermute(value, axis, [(i, i ^ bit) for i in range(size)])  28.8 us
    dot_general x4, matrix products, on_device(): term = lax.dot_general(x, w, NT, preferred_element_type=F32)  27.6 us
    all_to_all x4, starting transfers between devices, all_to_all(): lax.all_to_all(block, 'expert', split_axis=0, concat_axis=0, tiled=True)  25.3 us
    dot_general x4, matrix products, share_of(): return lax.dot_general(hidden, w, NT, preferred_element_type=F32)  19.7 us
    dot_general x7, matrix products, dot(): return jnp.dot(a, b, preferred_element_type=F32)  19.4 us
    all_to_all x4, waiting for transfers between devices, all_to_all(): lax.all_to_all(block, 'expert', split_axis=0, concat_axis=0, tiled=True)  17.4 us
    ppermute x12, starting transfers between devices, xor_send(): return lax.ppermute(value, axis, [(i, i ^ bit) for i in range(size)])  17 us
    dot_general x4, matrix products, on_device(): lax.dot_general(table[:, h * tok_count:(h + 1) * tok_count], back, (((0,)...  4.91 us
  transfers between devices with their start and end apart: 16, of which 7 were waited for; matrix products, arithmetic and copies ran while one was open for 46% of the time, Pallas kernels for 0%

profile of v1, /device:TPU:9, one launch (start us, length us, event | category | flops | bytes accessed | tf_op | source)
XLA Modules:
  0.0 182.9 jit_solution(9490660489738342247)
XLA Ops:
  0.7 1.8 fusion.61
  7.7 6.0 %all-to-all-start.1 = ((bf16[16,40,384]{2,1,0:T(8,128)(2,1)}), bf16[16,40,384]{2,1,0:T(8,128)(2,1)}, u32[]{:S(2)}, u32[]{:S(2)}) async-start(bf16[16,40,384]{2,1,0:T(8,128)(2,1)} %bitcast.78), calls=%async_computation.1 | async-start | bytes 983040 | tf_op jit(solution)/shard_map/all_to_all | solution.py:103
  13.7 1.9 %bitcast_add_fusion = f32[128,2048]{1,0:T(8,128)S(1)} fusion(bf16[128,2048]{1,0:T(8,128)(2,1)} %collective-permute-done.4, f32[1,256,2048]{2,1,0:T(8,128)} %param.15, pred[]{:T(512)S(6)} %ne.100), kind=kLoop, calls=%fused_computation.59 | loop fusion | flops 786432 | bytes 3670017 | tf_op jit(solution)/shard_map/add | solution.py:37
  17.8 12.8 %fusion = f32[320,2560]{1,0:T(8,128)} fusion(bf16[1,4096,2560]{2,1,0:T(8,128)(2,1)} %param.13, bf16[1,320,4096]{2,1,0:T(8,128)(2,1)S(1)} %copy-done), kind=kOutput, calls=%fused_computation | convolution fusion | flops 6710886400 | bytes 26869760 | tf_op jit(solution)/shard_map/dot_general | solution.py:65
  33.4 1.6 convolution_convert_fusion
  35.0 2.5 %collective-permute-done.6 = bf16[32,2048]{1,0:T(8,128)(2,1)S(1)} collective-permute-done((bf16[32,2048]{1,0:T(8,128)(2,1)S(1)}, bf16[32,2048]{1,0:T(8,128)(2,1)S(1)}, u32[]{:S(2)}, u32[]{:S(2)}) %collective-permute-start.6) | collective-permute-done | bytes 131104 | tf_op jit(solution)/shard_map/ppermute | solution.py:29
  37.6 2.2 %collective-permute-start.7 = (bf16[16,2048]{1,0:T(8,128)(2,1)S(1)}, bf16[16,2048]{1,0:T(8,128)(2,1)S(1)}, u32[]{:S(2)}, u32[]{:S(2)}) collective-permute-start(bf16[16,2048]{1,0:T(8,128)(2,1)S(1)} %select_convert_fusion.3), channel_id=1, source_target_pairs={{0,16},{2,18},{4,20},{6,22},{8,24},{10,26},{12,28},{14,30},{16,0},... | collective-permute-start | bytes 196616 | tf_op jit(solution)/shard_map/ppermute | solution.py:29
  39.8 5.4 %all-to-all-start = ((bf16[16,40,640]{2,1,0:T(8,128)(2,1)}), bf16[16,40,640]{2,1,0:T(8,128)(2,1)S(1)}, u32[]{:S(2)}, u32[]{:S(2)}) async-start(bf16[16,40,640]{2,1,0:T(8,128)(2,1)} %bitcast), calls=%async_computation | async-start | bytes 1638400 | tf_op jit(solution)/shard_map/all_to_all | solution.py:103
  45.2 1.6 convolution_convert_fusion.6
  46.7 1.6 convolution_convert_fusion.7
  48.4 2.2 %collective-permute-start.8 = (bf16[16,2048]{1,0:T(8,128)(2,1)S(1)}, bf16[16,2048]{1,0:T(8,128)(2,1)S(1)}, u32[]{:S(2)}, u32[]{:S(2)}) collective-permute-start(bf16[16,2048]{1,0:T(8,128)(2,1)S(1)} %add_convert_fusion.3), channel_id=1, source_target_pairs={{0,16},{2,18},{4,20},{6,22},{8,24},{10,26},{12,28},{14,30},{16,0},... | collective-permute-start | bytes 196616 | tf_op jit(solution)/shard_map/ppermute | solution.py:29
  51.9 13.9 %collective-permute-done.8 = bf16[16,2048]{1,0:T(8,128)(2,1)S(1)} collective-permute-done((bf16[16,2048]{1,0:T(8,128)(2,1)S(1)}, bf16[16,2048]{1,0:T(8,128)(2,1)S(1)}, u32[]{:S(2)}, u32[]{:S(2)}) %collective-permute-start.8) | collective-permute-done | bytes 65568 | tf_op jit(solution)/shard_map/ppermute | solution.py:29
  65.9 3.2 %collective-permute-start.9 = (bf16[32,2048]{1,0:T(8,128)(2,1)S(1)}, bf16[32,2048]{1,0:T(8,128)(2,1)S(1)}, u32[]{:S(2)}, u32[]{:S(2)}) collective-permute-start(bf16[32,2048]{1,0:T(8,128)(2,1)S(1)} %pad_maximum_fusion.5), channel_id=1, source_target_pairs={{0,8},{2,10},{4,12},{6,14},{8,0},{10,2},{12,4},{14,6},{16,24},{18,... | collective-permute-start | bytes 393224 | tf_op jit(solution)/shard_map/ppermute | solution.py:29
  69.0 5.3 %fusion.35 = f32[320,2560]{1,0:T(8,128)} fusion(bf16[1,2560,4096]{2,1,0:T(8,128)(2,1)} %param.14, s32[]{:T(128)S(6)} %select_n.180, bf16[320,384]{1,0:T(8,128)(2,1)S(1)} %convolution_convert_fusion.6, bf16[320,384]{1,0:T(8,128)(2,1)S(1)} %convolution_convert_fusion.7), kind=kOutput, calls=%fused_computation.27 | convolution fusion | flops 1259274240 | bytes 7700484 | tf_op jit(solution)/shard_map/dot_general | solution.py:130
  75.7 5.3 %fusion.33 = f32[320,2560]{1,0:T(8,128)} fusion(bf16[320,768]{1,0:T(8,128)(2,1)S(1)} %collective-permute-done.1, bf16[1,2560,4096]{2,1,0:T(8,128)(2,1)} %param.14, s32[]{:T(128)S(6)} %select_n.181), kind=kOutput, calls=%fused_computation.25 | convolution fusion | flops 1258291200 | bytes 7700484 | tf_op jit(solution)/shard_map/dot_general | solution.py:130
  84.6 1.7 collective-permute-start.11
  86.3 7.7 %fusion.8 = f32[320,2560]{1,0:T(8,128)} fusion(bf16[1,2560,4096]{2,1,0:T(8,128)(2,1)} %param.14, s32[]{:T(128)S(6)} %select_n.178, bf16[320,640]{1,0:T(8,128)(2,1)S(1)} %convolution_convert_fusion.2, bf16[320,640]{1,0:T(8,128)(2,1)S(1)} %convolution_convert_fusion.3), kind=kOutput, calls=%fused_computation.8 | convolution fusion | flops 2098790400 | bytes 10649604 | tf_op jit(solution)/shard_map/dot_general | solution.py:130
  94.0 6.7 %collective-permute-done = bf16[320,1280]{1,0:T(8,128)(2,1)S(1)} collective-permute-done((bf16[320,1280]{1,0:T(8,128)(2,1)S(1)}, bf16[320,1280]{1,0:T(8,128)(2,1)S(1)}, u32[]{:S(2)}, u32[]{:S(2)}) %collective-permute-start) | collective-permute-done | bytes 819232 | tf_op jit(solution)/shard_map/ppermute | solution.py:29
  100.7 9.2 %fusion.26 = bf16[320,2560]{1,0:T(8,128)(2,1)S(1)} fusion(f32[320,2560]{1,0:T(8,128)S(1)} %copy-done.7, f32[320,2560]{1,0:T(8,128)S(1)} %copy-done.9, f32[320,2560]{1,0:T(8,128)} %fusion.8, bf16[320,1280]{1,0:T(8,128)(2,1)S(1)} %collective-permute-done, bf16[1,2560,4096]{2,1,0:T(8,128)(2,1)} %param.14, s32[]{:T(128)S(6)} %select_n.179, ...), kind=kOutput, calls=%fused_computation.20 | convolution fusion | flops 2115174400 | bytes 22118404 | tf_op jit(solution)/shard_map/dot_general | solution.py:130
  109.9 4.2 %fusion.51 = bf16[320,768]{1,0:T(8,128)(2,1)S(1)} fusion(bf16[320,2560]{1,0:T(8,128)(2,1)S(1)} %fusion.26, bf16[1,4096,2560]{2,1,0:T(8,128)(2,1)} %param.13, s32[]{:T(128)S(6)} %select_n.181), kind=kOutput, calls=%fused_computation.48 | convolution fusion | flops 1258536960 | bytes 6062084 | tf_op jit(solution)/shard_map/dot_general | solution.py:140
  115.4 6.1 %fusion.46 = bf16[320,1280]{1,0:T(8,128)(2,1)} fusion(bf16[320,2560]{1,0:T(8,128)(2,1)S(1)} %fusion.26, bf16[1,4096,2560]{2,1,0:T(8,128)(2,1)} %param.13, s32[]{:T(128)S(6)} %select_n.179), kind=kOutput, calls=%fused_computation.38 | convolution fusion | flops 2097561600 | bytes 9011204 | tf_op jit(solution)/shard_map/dot_general | solution.py:140
  121.7 2.8 %collective-permute-done.3 = bf16[320,768]{1,0:T(8,128)(2,1)S(1)} collective-permute-done((bf16[320,768]{1,0:T(8,128)(2,1)S(1)}, bf16[320,768]{1,0:T(8,128)(2,1)S(1)}, u32[]{:S(2)}, u32[]{:S(2)}) %collective-permute-start.3) | collective-permute-done | bytes 491552 | tf_op jit(solution)/shard_map/ppermute | solution.py:29
  124.5 3.6 %add_convert_fusion.2 = bf16[320,768]{1,0:T(8,128)(2,1)S(1)} fusion(bf16[320,768]{1,0:T(8,128)(2,1)S(1)} %collective-permute-done.3, bf16[320,2560]{1,0:T(8,128)(2,1)S(1)} %fusion.26, bf16[1,4096,2560]{2,1,0:T(8,128)(2,1)} %param.13, s32[]{:T(128)S(6)} %select_n.180), kind=kOutput, calls=%fused_computation.61 | convolution fusion | flops 1259028480 | bytes 6553604 | tf_op jit(solution)/shard_map/dot_general | solution.py:140
  129.8 9.5 %all-to-all-start.3 = ((bf16[16,40,384]{2,1,0:T(8,128)(2,1)}), bf16[16,40,384]{2,1,0:T(8,128)(2,1)S(1)}, u32[]{:S(2)}, u32[]{:S(2)}) async-start(bf16[16,40,384]{2,1,0:T(8,128)(2,1)} %bitcast.16), calls=%async_computation.3 | async-start | bytes 983040 | tf_op jit(solution)/shard_map/all_to_all | solution.py:103
  139.3 2.9 %collective-permute-done.2 = bf16[320,1280]{1,0:T(8,128)(2,1)} collective-permute-done((bf16[320,1280]{1,0:T(8,128)(2,1)}, bf16[320,1280]{1,0:T(8,128)(2,1)}, u32[]{:S(2)}, u32[]{:S(2)}) %collective-permute-start.2) | collective-permute-done | bytes 819232 | tf_op jit(solution)/shard_map/ppermute | solution.py:29
  142.2 5.8 %add_convert_fusion.1 = bf16[320,1280]{1,0:T(8,128)(2,1)S(1)} fusion(bf16[320,1280]{1,0:T(8,128)(2,1)} %collective-permute-done.2, bf16[320,2560]{1,0:T(8,128)(2,1)} %copy-done.8, bf16[1,4096,2560]{2,1,0:T(8,128)(2,1)} %param.13, s32[]{:T(128)S(6)} %select_n.178), kind=kOutput, calls=%fused_computation.42 | convolution fusion | flops 2098380800 | bytes 9830404 | tf_op jit(solution)/shard_map/dot_general | solution.py:140
  148.6 1.5 add_convert_fusion
  150.1 2.6 %all-to-all-done.3 = bf16[16,40,384]{2,1,0:T(8,128)(2,1)S(1)} async-done(((bf16[16,40,384]{2,1,0:T(8,128)(2,1)}), bf16[16,40,384]{2,1,0:T(8,128)(2,1)S(1)}, u32[]{:S(2)}, u32[]{:S(2)}) %all-to-all-start.3) | async-done | bytes 491552 | tf_op jit(solution)/shard_map/all_to_all | solution.py:103
  153.5 4.4 %all-to-all-start.2 = ((bf16[16,40,640]{2,1,0:T(8,128)(2,1)}), bf16[16,40,640]{2,1,0:T(8,128)(2,1)S(1)}, u32[]{:S(2)}, u32[]{:S(2)}) async-start(bf16[16,40,640]{2,1,0:T(8,128)(2,1)} %bitcast.12), calls=%async_computation.2 | async-start | bytes 1638400 | tf_op jit(solution)/shard_map/all_to_all | solution.py:103
  159.5 1.6 maximum_convert_fusion
  163.3 14.8 %all-to-all-done.2 = bf16[16,40,640]{2,1,0:T(8,128)(2,1)S(1)} async-done(((bf16[16,40,640]{2,1,0:T(8,128)(2,1)}), bf16[16,40,640]{2,1,0:T(8,128)(2,1)S(1)}, u32[]{:S(2)}, u32[]{:S(2)}) %all-to-all-start.2) | async-done | bytes 819232 | tf_op jit(solution)/shard_map/all_to_all | solution.py:103
  180.8 2.1 %pad_maximum_fusion = bf16[256,2048]{1,0:T(8,128)(2,1)} fusion(bf16[256,384]{1,0:T(8,128)(2,1)} %convolution_convert_fusion.8, bf16[256,384]{1,0:T(8,128)(2,1)} %convolution_convert_fusion.9, bf16[256,640]{1,0:T(8,128)(2,1)S(1)} %convolution_convert_fusion.4, bf16[256,640]{1,0:T(8,128)(2,1)S(1)} %convolution_convert_fusion.5), kind=kLoop, calls=%fused_computation.57 | loop fusion | flops 4194304 | bytes 2097152 | tf_op jit(solution)/shard_map/concatenate | solution.py:170
  (71 shorter events, 27.7 us)
Async XLA Ops:
  0.6 17.2 %copy-start = (bf16[1,320,4096]{2,1,0:T(8,128)(2,1)S(1)}, bf16[1,320,4096]{2,1,0:T(8,128)(2,1)}, u32[]{:S(2)}) copy-start(bf16[1,320,4096]{2,1,0:T(8,128)(2,1)} %param.12) | copy-start | bytes 7864324
  2.4 11.3 %collective-permute-start.4 = (bf16[128,2048]{1,0:T(8,128)(2,1)S(1)}, bf16[128,2048]{1,0:T(8,128)(2,1)}, u32[]{:S(2)}, u32[]{:S(2)}) collective-permute-start(bf16[128,2048]{1,0:T(8,128)(2,1)S(1)} %fusion.61), channel_id=1, source_target_pairs={{0,2},{2,0},{4,6},{6,4},{8,10},{10,8},{12,14},{14,12},{16,18},{18,... | collective-permute-start | bytes 1572872 | tf_op jit(solution)/shard_map/ppermute | solution.py:29
  5.4 1.0 copy-start.3
  7.7 32.1 %all-to-all-start.1 = ((bf16[16,40,384]{2,1,0:T(8,128)(2,1)}), bf16[16,40,384]{2,1,0:T(8,128)(2,1)}, u32[]{:S(2)}, u32[]{:S(2)}) async-start(bf16[16,40,384]{2,1,0:T(8,128)(2,1)} %bitcast.78), calls=%async_computation.1 | async-start | bytes 983040 | tf_op jit(solution)/shard_map/all_to_all | solution.py:103
  15.6 1.0 copy-start.2
  16.6 15.2 %collective-permute-start.5 = (bf16[64,2048]{1,0:T(8,128)(2,1)S(1)}, bf16[64,2048]{1,0:T(8,128)(2,1)S(1)}, u32[]{:S(2)}, u32[]{:S(2)}) collective-permute-start(bf16[64,2048]{1,0:T(8,128)(2,1)S(1)} %select_convert_fusion.1), channel_id=1, source_target_pairs={{0,4},{2,6},{4,0},{6,2},{8,12},{10,14},{12,8},{14,10},{16,20},{18,... | collective-permute-start | bytes 786440 | tf_op jit(solution)/shard_map/ppermute | solution.py:29
  33.1 4.5 %collective-permute-start.6 = (bf16[32,2048]{1,0:T(8,128)(2,1)S(1)}, bf16[32,2048]{1,0:T(8,128)(2,1)S(1)}, u32[]{:S(2)}, u32[]{:S(2)}) collective-permute-start(bf16[32,2048]{1,0:T(8,128)(2,1)S(1)} %select_convert_fusion.2), channel_id=1, source_target_pairs={{0,8},{2,10},{4,12},{6,14},{8,0},{10,2},{12,4},{14,6},{16,24},{18,... | collective-permute-start | bytes 393224 | tf_op jit(solution)/shard_map/ppermute | solution.py:29
  37.6 10.7 %collective-permute-start.7 = (bf16[16,2048]{1,0:T(8,128)(2,1)S(1)}, bf16[16,2048]{1,0:T(8,128)(2,1)S(1)}, u32[]{:S(2)}, u32[]{:S(2)}) collective-permute-start(bf16[16,2048]{1,0:T(8,128)(2,1)S(1)} %select_convert_fusion.3), channel_id=1, source_target_pairs={{0,16},{2,18},{4,20},{6,22},{8,24},{10,26},{12,28},{14,30},{16,0},... | collective-permute-start | bytes 196616 | tf_op jit(solution)/shard_map/ppermute | solution.py:29
  39.8 41.3 %all-to-all-start = ((bf16[16,40,640]{2,1,0:T(8,128)(2,1)}), bf16[16,40,640]{2,1,0:T(8,128)(2,1)S(1)}, u32[]{:S(2)}, u32[]{:S(2)}) async-start(bf16[16,40,640]{2,1,0:T(8,128)(2,1)} %bitcast), calls=%async_computation | async-start | bytes 1638400 | tf_op jit(solution)/shard_map/all_to_all | solution.py:103
  48.4 17.4 %collective-permute-start.8 = (bf16[16,2048]{1,0:T(8,128)(2,1)S(1)}, bf16[16,2048]{1,0:T(8,128)(2,1)S(1)}, u32[]{:S(2)}, u32[]{:S(2)}) collective-permute-start(bf16[16,2048]{1,0:T(8,128)(2,1)S(1)} %add_convert_fusion.3), channel_id=1, source_target_pairs={{0,16},{2,18},{4,20},{6,22},{8,24},{10,26},{12,28},{14,30},{16,0},... | collective-permute-start | bytes 196616 | tf_op jit(solution)/shard_map/ppermute | solution.py:29
  50.6 25.1 %collective-permute-start.1 = (bf16[320,768]{1,0:T(8,128)(2,1)S(1)}, bf16[320,768]{1,0:T(8,128)(2,1)S(1)}, u32[]{:S(2)}, u32[]{:S(2)}) collective-permute-start(bf16[320,768]{1,0:T(8,128)(2,1)S(1)} %pad_maximum_fusion.3), channel_id=1, source_target_pairs={{0,1},{1,0},{2,3},{3,2},{4,5},{5,4},{6,7},{7,6},{8,9},{9,8},{10,11... | collective-permute-start | bytes 1474568 | tf_op jit(solution)/shard_map/ppermute | solution.py:29
  65.9 8.5 %collective-permute-start.9 = (bf16[32,2048]{1,0:T(8,128)(2,1)S(1)}, bf16[32,2048]{1,0:T(8,128)(2,1)S(1)}, u32[]{:S(2)}, u32[]{:S(2)}) collective-permute-start(bf16[32,2048]{1,0:T(8,128)(2,1)S(1)} %pad_maximum_fusion.5), channel_id=1, source_target_pairs={{0,8},{2,10},{4,12},{6,14},{8,0},{10,2},{12,4},{14,6},{16,24},{18,... | collective-permute-start | bytes 393224 | tf_op jit(solution)/shard_map/ppermute | solution.py:29
  74.4 9.2 %collective-permute-start.10 = (bf16[64,2048]{1,0:T(8,128)(2,1)S(1)}, bf16[64,2048]{1,0:T(8,128)(2,1)S(1)}, u32[]{:S(2)}, u32[]{:S(2)}) collective-permute-start(bf16[64,2048]{1,0:T(8,128)(2,1)S(1)} %pad_maximum_fusion.4), channel_id=1, source_target_pairs={{0,4},{2,6},{4,0},{6,2},{8,12},{10,14},{12,8},{14,10},{16,20},{18,... | collective-permute-start | bytes 786440 | tf_op jit(solution)/shard_map/ppermute | solution.py:29
  82.3 18.4 %collective-permute-start = (bf16[320,1280]{1,0:T(8,128)(2,1)S(1)}, bf16[320,1280]{1,0:T(8,128)(2,1)S(1)}, u32[]{:S(2)}, u32[]{:S(2)}) collective-permute-start(bf16[320,1280]{1,0:T(8,128)(2,1)S(1)} %pad_maximum_fusion.1), channel_id=1, source_target_pairs={{0,1},{1,0},{2,3},{3,2},{4,5},{5,4},{6,7},{7,6},{8,9},{9,8},{10,11... | collective-permute-start | bytes 2457608 | tf_op jit(solution)/shard_map/ppermute | solution.py:29
  84.5 16.1 %copy-start.7 = (f32[320,2560]{1,0:T(8,128)S(1)}, f32[320,2560]{1,0:T(8,128)}, u32[]{:S(2)}) copy-start(f32[320,2560]{1,0:T(8,128)} %fusion.33) | copy-start | bytes 9830404
  84.6 16.1 %copy-start.9 = (f32[320,2560]{1,0:T(8,128)S(1)}, f32[320,2560]{1,0:T(8,128)}, u32[]{:S(2)}) copy-start(f32[320,2560]{1,0:T(8,128)} %fusion.35) | copy-start | bytes 9830404
  84.6 16.1 %copy-start.10 = (f32[320,2560]{1,0:T(8,128)S(1)}, f32[320,2560]{1,0:T(8,128)}, u32[]{:S(2)}) copy-start(f32[320,2560]{1,0:T(8,128)} %fusion) | copy-start | bytes 9830404
  84.6 73.6 %collective-permute-start.11 = (bf16[128,2048]{1,0:T(8,128)(2,1)}, bf16[128,2048]{1,0:T(8,128)(2,1)}, u32[]{:S(2)}, u32[]{:S(2)}) collective-permute-start(bf16[128,2048]{1,0:T(8,128)(2,1)} %pad_maximum_fusion.2), channel_id=1, source_target_pairs={{0,2},{2,0},{4,6},{6,4},{8,10},{10,8},{12,14},{14,12},{16,18},{18,... | collective-permute-start | bytes 1572872 | tf_op jit(solution)/shard_map/ppermute | solution.py:29
  109.9 14.6 %copy-start.8 = (bf16[320,2560]{1,0:T(8,128)(2,1)}, bf16[320,2560]{1,0:T(8,128)(2,1)S(1)}, u32[]{:S(2)}) copy-start(bf16[320,2560]{1,0:T(8,128)(2,1)S(1)} %fusion.26) | copy-start | bytes 4915204
  114.1 10.4 %collective-permute-start.3 = (bf16[320,768]{1,0:T(8,128)(2,1)S(1)}, bf16[320,768]{1,0:T(8,128)(2,1)S(1)}, u32[]{:S(2)}, u32[]{:S(2)}) collective-permute-start(bf16[320,768]{1,0:T(8,128)(2,1)S(1)} %fusion.51), channel_id=1, source_target_pairs={{0,1},{1,0},{2,3},{3,2},{4,5},{5,4},{6,7},{7,6},{8,9},{9,8},{10,11... | collective-permute-start | bytes 1474568 | tf_op jit(solution)/shard_map/ppermute | solution.py:29
  121.5 20.7 %collective-permute-start.2 = (bf16[320,1280]{1,0:T(8,128)(2,1)}, bf16[320,1280]{1,0:T(8,128)(2,1)}, u32[]{:S(2)}, u32[]{:S(2)}) collective-permute-start(bf16[320,1280]{1,0:T(8,128)(2,1)} %fusion.46), channel_id=1, source_target_pairs={{0,1},{1,0},{2,3},{3,2},{4,5},{5,4},{6,7},{7,6},{8,9},{9,8},{10,11... | collective-permute-start | bytes 2457608 | tf_op jit(solution)/shard_map/ppermute | solution.py:29
  129.8 22.9 %all-to-all-start.3 = ((bf16[16,40,384]{2,1,0:T(8,128)(2,1)}), bf16[16,40,384]{2,1,0:T(8,128)(2,1)S(1)}, u32[]{:S(2)}, u32[]{:S(2)}) async-start(bf16[16,40,384]{2,1,0:T(8,128)(2,1)} %bitcast.16), calls=%async_computation.3 | async-start | bytes 983040 | tf_op jit(solution)/shard_map/all_to_all | solution.py:103
  152.7 0.8 copy-start.4
  153.5 24.6 %all-to-all-start.2 = ((bf16[16,40,640]{2,1,0:T(8,128)(2,1)}), bf16[16,40,640]{2,1,0:T(8,128)(2,1)S(1)}, u32[]{:S(2)}, u32[]{:S(2)}) async-start(bf16[16,40,640]{2,1,0:T(8,128)(2,1)} %bitcast.12), calls=%async_computation.2 | async-start | bytes 1638400 | tf_op jit(solution)/shard_map/all_to_all | solution.py:103
  157.9 3.2 %copy-start.5 = (bf16[16,40,384]{2,1,0:T(8,128)(2,1)S(1)}, bf16[16,40,384]{2,1,0:T(8,128)(2,1)}, u32[]{:S(2)}) copy-start(bf16[16,40,384]{2,1,0:T(8,128)(2,1)} %copy-done.4) | copy-start | bytes 1474564
  158.1 4.1 %copy-start.6 = (pred[640,512]{1,0:T(32,128)(4,1)}, pred[640,512]{1,0:T(32,128)(4,1)S(1)}, u32[]{:S(2)}) copy-start(pred[640,512]{1,0:T(32,128)(4,1)S(1)} %iota_compare_fusion) | copy-start | bytes 983044
  161.1 21.8 %copy-start.1 = (bf16[1,320,4096]{2,1,0:T(8,128)(2,1)S(1)}, bf16[1,320,4096]{2,1,0:T(8,128)(2,1)}, u32[]{:S(2)}) copy-start(bf16[1,320,4096]{2,1,0:T(8,128)(2,1)} %param.12) | copy-start | bytes 7864324

commit v2 on v1

--- a/solution.py
+++ b/solution.py
@@ -47,9 +47,11 @@
     return [1 << i for i in range(size.bit_length() - 1)]
 
 
-def summed_over(part, axis):
+def summed_over(part, axis, early, gate):
     bits = bits_of(lax.axis_size(axis))
-    for bit in bits:
+    for i, bit in enumerate(bits):
+        if i == early:
+            part = after(part, gate)
         part = halve(part, axis, bit)
     part = part.astype(BF16)
     for bit in reversed(bits):
@@ -84,8 +86,6 @@
     fold = 2 if pair and features % 512 == 0 else 1
     rows = fold * slot_rows
 
-    dense_sum = summed_over(dense_partial[0], "expert")
-
     scaled = (gate[:, None] * grad_out.astype(F32)).astype(BF16)
     columns = jnp.concatenate(
         [jnp.where(slots >= 0, routes * (fold * cap) + h * cap + slots, -1) for h in range(fold)]
@@ -102,72 +102,75 @@
         block = block.reshape(groups, fold * cap, wide)
         return lax.all_to_all(block, "expert", split_axis=0, concat_axis=0, tiled=True).reshape(rows, wide)
 
-    mine = []
+    def nt_dot(a, b):
+        return lax.dot_general(a, b, NT, preferred_element_type=F32)
+
+    def tn_dot(a, b):
+        return lax.dot_general(a, b, (((0,), (0,)), ((), ())), preferred_element_type=F32)
+
+    outgoing = []
     for start, width in zip(starts, widths):
         part = width // fold
         stacked = jnp.concatenate(
             [scaled[:, start + h * part : start + (h + 1) * part] for h in range(fold)], axis=0
         )
-        arrived = all_to_all(dot(table, stacked).astype(BF16))
-        mine.append(
-            jnp.concatenate(
-                [
-                    lax.dot_general(t, arrived, (((0,), (0,)), ((), ())), preferred_element_type=F32).astype(BF16)
-                    for t in spread
-                ],
-                axis=1,
-            )
-        )
+        outgoing.append(dot(table, stacked).astype(BF16))
 
-    slopes = slope_of(dot(saved_inputs[0], w_in[0]))
+    saved = after(saved_inputs[0], outgoing[0])
+    slopes = lax.optimization_barrier(slope_of(dot(saved, w_in[0])))
+    arrived = [all_to_all(outgoing[0])]
+    for block in outgoing[1:]:
+        arrived.append(all_to_all(after(block, arrived[-1], slopes)))
+    mine = [jnp.concatenate([tn_dot(t, block).astype(BF16) for t in spread], axis=1) for block in arrived]
+    dense_sum = summed_over(after(dense_partial[0], outgoing[0]), "expert", 2, arrived[-1])
 
     if pair:
-        theirs = [xor_send(x, "mp", 1) for x in mine]
         upstream = None
-        for start, width, own, other in zip(starts, widths, mine, theirs):
-            for who, x in ((me, own), (1 - me, other)):
-                w = lax.dynamic_slice_in_dim(w_out[0], who * features + start, width, 1)
-                term = lax.dot_general(x, w, NT, preferred_element_type=F32)
-                upstream = term if upstream is None else upstream + term
+        waiting = []
+        for i, (start, width) in enumerate(zip(starts, widths)):
+            own = mine[i]
+            if upstream is not None:
+                own = after(own, upstream)
+            theirs = xor_send(own, "mp", 1)
+            todo = waiting + [(me, start, width, own)]
+            for who, first, wide, x in todo:
+                w = lax.dynamic_slice_in_dim(w_out[0], who * features + first, wide, 1)
+                term = nt_dot(x, w)
+                upstream = lax.optimization_barrier(term if upstream is None else upstream + term)
+            waiting = [(1 - me, start, width, theirs)]
+        for who, first, wide, x in waiting:
+            w = lax.dynamic_slice_in_dim(w_out[0], who * features + first, wide, 1)
+            upstream = upstream + nt_dot(x, w)
     else:
-        upstream = lax.dot_general(
-            lax.all_gather(mine[0], "mp", axis=1, tiled=True), w_out[0], NT, preferred_element_type=F32
-        )
-    hidden = (upstream * slopes).astype(BF16)
+        upstream = nt_dot(lax.all_gather(mine[0], "mp", axis=1, tiled=True), w_out[0])
+    hidden = lax.optimization_barrier((upstream * slopes).astype(BF16))
 
     def share_of(who, start, width):
-        w = lax.dynamic_slice_in_dim(w_in[0], who * features + start, width, 0)
-        return lax.dot_general(hidden, w, NT, preferred_element_type=F32)
+        return nt_dot(hidden, lax.dynamic_slice_in_dim(w_in[0], who * features + start, width, 0))
 
-    outs = []
+    order = list(reversed(range(len(widths))))
     if pair:
-        sent = [
-            xor_send(share_of(1 - me, start, width).astype(BF16), "mp", 1)
-            for start, width in reversed(list(zip(starts, widths)))
-        ][::-1]
-    for i, (start, width) in reversed(list(enumerate(zip(starts, widths)))):
-        part = width // fold
+        sent = {i: xor_send(share_of(1 - me, starts[i], widths[i]).astype(BF16), "mp", 1) for i in order}
+        kept = {i: lax.optimization_barrier(share_of(me, starts[i], widths[i])) for i in order}
+    outs = {}
+    last = None
+    for i in order:
+        part = widths[i] // fold
         if pair:
-            total = (share_of(me, start, width) + sent[i].astype(F32)).astype(BF16)
+            total = (kept[i] + sent[i].astype(F32)).astype(BF16)
         else:
             total = lax.psum_scatter(
-                lax.dot_general(hidden, w_in[0], NT, preferred_element_type=F32),
-                "mp",
-                scatter_dimension=1,
-                tiled=True,
+                nt_dot(hidden, w_in[0]), "mp", scatter_dimension=1, tiled=True
             ).astype(BF16)
-        folded = sum(dot(t, total[:, h * part : (h + 1) * part]) for h, t in enumerate(spread))
-        back = all_to_all(folded.astype(BF16))
-        outs = [
-            lax.dot_general(
-                table[:, h * tok_count : (h + 1) * tok_count],
-                back,
-                (((0,), (0,)), ((), ())),
-                preferred_element_type=F32,
-            ).astype(BF16)
-            for h in range(fold)
-        ] + outs
-    return (jnp.concatenate(outs, axis=1), dense_sum)
+        folded = sum(dot(t, total[:, h * part : (h + 1) * part]) for h, t in enumerate(spread)).astype(BF16)
+        if last is not None:
+            folded = after(folded, last)
+        last = all_to_all(folded)
+        outs[i] = jnp.concatenate(
+            [tn_dot(table[:, h * tok_count : (h + 1) * tok_count], last).astype(BF16) for h in range(fold)],
+            axis=1,
+        )
+    return (jnp.concatenate([outs[i] for i in sorted(order)], axis=1), dense_sum)
 
 
 def solution(mesh):

time: 184 us -> 166 us (0.902)
  matrix products: 75.9 us -> 61.8 us
  waiting for transfers between devices: 46.2 us -> 35.2 us
  starting transfers between devices: 42.3 us -> 48.6 us
  other arithmetic: 13.7 us -> 16.5 us
    ppermute x12, waiting for transfers between devices: 28.8 us -> 10.9 us  [xor_send(): return lax.ppermute(value, axis, [(i, i ^ bit) for i in range(size)])]
    dot_general x16, matrix products: 56.4 us -> 41.4 us  [the longest x8 34.3 us: nt_dot(): return lax.dot_general(a, b, NT, preferred_element_type=F32)]
    all_to_all x4, waiting for transfers between devices: 17.4 us -> 24.3 us  [all_to_all(): lax.all_to_all(block, 'expert', split_axis=0, concat_axis=0, tiled=True)]
    all_to_all x4, starting transfers between devices: 25.3 us -> 30.4 us  [all_to_all(): lax.all_to_all(block, 'expert', split_axis=0, concat_axis=0, tiled=True)]
  transfers between devices with their start and end apart: 16 -> 16, of which waited for: 7 -> 10; matrix products, arithmetic and copies ran while one was open for 46% -> 43% of each run, Pallas kernels for 0% -> 0%
where the time goes in v2:
time: 166 us; the launch traced here: 165 us
  matrix products  61.8 us (37%)
  starting transfers between devices  48.6 us (29%)
  waiting for transfers between devices  35.2 us (21%)
  other arithmetic  16.5 us (10%)
  local copies, waits for them, and re-layouts  2.18 us (1%)
    dot_general x8, matrix products, nt_dot(): return lax.dot_general(a, b, NT, preferred_element_type=F32)  34.3 us
    all_to_all x4, starting transfers between devices, all_to_all(): lax.all_to_all(block, 'expert', split_axis=0, concat_axis=0, tiled=True)  30.4 us
    all_to_all x4, waiting for transfers between devices, all_to_all(): lax.all_to_all(block, 'expert', split_axis=0, concat_axis=0, tiled=True)  24.3 us
    dot_general x7, matrix products, dot(): return jnp.dot(a, b, preferred_element_type=F32)  20.4 us
    ppermute x12, starting transfers between devices, xor_send(): return lax.ppermute(value, axis, [(i, i ^ bit) for i in range(size)])  18.2 us
    ppermute x12, waiting for transfers between devices, xor_send(): return lax.ppermute(value, axis, [(i, i ^ bit) for i in range(size)])  10.9 us
    dot_general x8, matrix products, tn_dot(): lax.dot_general(a, b, (((0,), (0,)), ((), ())), preferred_element_type=F32)  7.15 us
  transfers between devices with their start and end apart: 16, of which 10 were waited for; matrix products, arithmetic and copies ran while one was open for 43% of the time, Pallas kernels for 0%

profile of v2, /device:TPU:9, one launch (start us, length us, event | category | flops | bytes accessed | tf_op | source)
XLA Modules:
  0.0 165.5 jit_solution(714300856276455268)
XLA Ops:
  0.7 1.6 multiply_convert_fusion
  3.4 1.6 convolution_convert_fusion
  5.0 6.6 %all-to-all-start = ((bf16[16,40,640]{2,1,0:T(8,128)(2,1)}), bf16[16,40,640]{2,1,0:T(8,128)(2,1)S(1)}, u32[]{:S(2)}, u32[]{:S(2)}) async-start(bf16[16,40,640]{2,1,0:T(8,128)(2,1)} %bitcast.66), calls=%async_computation | async-start | bytes 1638400 | tf_op jit(solution)/shard_map/all_to_all | solution.py:103
  11.6 2.4 %select_convert_fusion = bf16[128,2048]{1,0:T(8,128)(2,1)} fusion(f32[256,2048]{1,0:T(8,128)} %bitcast.62, pred[]{:T(512)S(6)} %ne.100), kind=kLoop, calls=%fused_computation.57 | loop fusion | flops 262144 | bytes 1572865 | tf_op jit(solution)/shard_map/convert_element_type | solution.py:37
  14.3 13.5 %fusion.34 = f32[320,2560]{1,0:T(8,128)} fusion(bf16[320,4096]{1,0:T(8,128)(2,1)S(1)} %bitcast.61, bf16[1,4096,2560]{2,1,0:T(8,128)(2,1)} %param.13), kind=kOutput, calls=%fused_computation.35 | convolution fusion | flops 6724812800 | bytes 26869760 | tf_op jit(solution)/shard_map/dot_general | solution.py:67
  30.2 1.9 %convert_add_fusion = f32[128,2048]{1,0:T(8,128)S(1)} fusion(bf16[128,2048]{1,0:T(8,128)(2,1)} %collective-permute-done.4, f32[256,2048]{1,0:T(8,128)} %bitcast.63, pred[]{:T(512)S(6)} %ne.100), kind=kLoop, calls=%fused_computation.56 | loop fusion | flops 786432 | bytes 3670017 | tf_op jit(solution)/shard_map/add | solution.py:37
  36.7 4.3 %collective-permute-done.5 = bf16[64,2048]{1,0:T(8,128)(2,1)} collective-permute-done((bf16[64,2048]{1,0:T(8,128)(2,1)}, bf16[64,2048]{1,0:T(8,128)(2,1)}, u32[]{:S(2)}, u32[]{:S(2)}) %collective-permute-start.5) | collective-permute-done | bytes 262176 | tf_op jit(solution)/shard_map/ppermute | solution.py:29
  42.0 6.6 %all-to-all-start.1 = ((bf16[16,40,384]{2,1,0:T(8,128)(2,1)}), bf16[16,40,384]{2,1,0:T(8,128)(2,1)S(1)}, u32[]{:S(2)}, u32[]{:S(2)}) async-start(bf16[16,40,384]{2,1,0:T(8,128)(2,1)} %bitcast.69), calls=%async_computation.1 | async-start | bytes 983040 | tf_op jit(solution)/shard_map/all_to_all | solution.py:103
  48.6 5.4 %fusion.8 = f32[320,2560]{1,0:T(8,128)S(1)} fusion(bf16[1,2560,4096]{2,1,0:T(8,128)(2,1)} %param.14, s32[]{:T(128)S(6)} %select_n.172, bf16[320,640]{1,0:T(8,128)(2,1)} %copy-done.7, bf16[320,640]{1,0:T(8,128)(2,1)} %copy-done.8), kind=kOutput, calls=%fused_computation.8 | convolution fusion | flops 2098790400 | bytes 10649604 | tf_op jit(solution)/shard_map/dot_general | solution.py:106
  54.8 6.9 %fusion.14 = f32[320,2560]{1,0:T(8,128)} fusion(f32[320,2560]{1,0:T(8,128)S(1)} %fusion.8, bf16[320,1280]{1,0:T(8,128)(2,1)S(1)} %collective-permute-done, bf16[1,2560,4096]{2,1,0:T(8,128)(2,1)} %param.14, s32[]{:T(128)S(6)} %select_n.173), kind=kOutput, calls=%fused_computation.16 | convolution fusion | flops 2097971200 | bytes 13926404 | tf_op jit(solution)/shard_map/dot_general | solution.py:106
  62.8 3.2 %collective-permute-done.6 = bf16[32,2048]{1,0:T(8,128)(2,1)S(1)} collective-permute-done((bf16[32,2048]{1,0:T(8,128)(2,1)S(1)}, bf16[32,2048]{1,0:T(8,128)(2,1)S(1)}, u32[]{:S(2)}, u32[]{:S(2)}) %collective-permute-start.6) | collective-permute-done | bytes 131104 | tf_op jit(solution)/shard_map/ppermute | solution.py:29
  66.0 1.8 %collective-permute-start.7 = (bf16[16,2048]{1,0:T(8,128)(2,1)S(1)}, bf16[16,2048]{1,0:T(8,128)(2,1)S(1)}, u32[]{:S(2)}, u32[]{:S(2)}) collective-permute-start(bf16[16,2048]{1,0:T(8,128)(2,1)S(1)} %select_convert_fusion.3), channel_id=1, source_target_pairs={{0,16},{2,18},{4,20},{6,22},{8,24},{10,26},{12,28},{14,30},{16,0},... | collective-permute-start | bytes 196616 | tf_op jit(solution)/shard_map/ppermute | solution.py:29
  68.4 1.7 %collective-permute-done.7 = bf16[16,2048]{1,0:T(8,128)(2,1)S(1)} collective-permute-done((bf16[16,2048]{1,0:T(8,128)(2,1)S(1)}, bf16[16,2048]{1,0:T(8,128)(2,1)S(1)}, u32[]{:S(2)}, u32[]{:S(2)}) %collective-permute-start.7) | collective-permute-done | bytes 65568 | tf_op jit(solution)/shard_map/ppermute | solution.py:29
  70.1 2.5 %collective-permute-start.8 = (bf16[16,2048]{1,0:T(8,128)(2,1)S(1)}, bf16[16,2048]{1,0:T(8,128)(2,1)S(1)}, u32[]{:S(2)}, u32[]{:S(2)}) collective-permute-start(bf16[16,2048]{1,0:T(8,128)(2,1)S(1)} %add_convert_fusion.3), channel_id=1, source_target_pairs={{0,16},{2,18},{4,20},{6,22},{8,24},{10,26},{12,28},{14,30},{16,0},... | collective-permute-start | bytes 196616 | tf_op jit(solution)/shard_map/ppermute | solution.py:29
  74.7 3.7 %fusion.24 = f32[320,2560]{1,0:T(8,128)S(1)} fusion(bf16[320,768]{1,0:T(8,128)(2,1)S(1)} %pad_maximum_fusion.3, bf16[1,2560,4096]{2,1,0:T(8,128)(2,1)} %param.14, s32[]{:T(128)S(6)} %select_n.174), kind=kOutput, calls=%fused_computation.25 | convolution fusion | flops 1258291200 | bytes 7700484 | tf_op jit(solution)/shard_map/dot_general | solution.py:106
  79.3 3.0 %collective-permute-start.10 = (bf16[64,2048]{1,0:T(8,128)(2,1)S(1)}, bf16[64,2048]{1,0:T(8,128)(2,1)S(1)}, u32[]{:S(2)}, u32[]{:S(2)}) collective-permute-start(bf16[64,2048]{1,0:T(8,128)(2,1)S(1)} %pad_maximum_fusion.4), channel_id=1, source_target_pairs={{0,4},{2,6},{4,0},{6,2},{8,12},{10,14},{12,8},{14,10},{16,20},{18,... | collective-permute-start | bytes 786440 | tf_op jit(solution)/shard_map/ppermute | solution.py:29
  82.3 4.4 %fusion.18 = bf16[320,2560]{1,0:T(8,128)(2,1)S(1)} fusion(f32[320,2560]{1,0:T(8,128)S(1)} %copy-done.2, f32[320,2560]{1,0:T(8,128)S(1)} %add.179, bf16[320,768]{1,0:T(8,128)(2,1)S(1)} %collective-permute-done.1, bf16[1,2560,4096]{2,1,0:T(8,128)(2,1)} %param.14, s32[]{:T(128)S(6)} %select_n.175), kind=kOutput, calls=%fused_computation.19 | convolution fusion | flops 1260748800 | bytes 12615684 | tf_op jit(solution)/shard_map/dot_general | solution.py:106
  86.7 3.6 %fusion.41 = bf16[320,768]{1,0:T(8,128)(2,1)S(1)} fusion(bf16[320,2560]{1,0:T(8,128)(2,1)S(1)} %fusion.18, bf16[1,4096,2560]{2,1,0:T(8,128)(2,1)} %param.13, s32[]{:T(128)S(6)} %select_n.175), kind=kOutput, calls=%fused_computation.45 | convolution fusion | flops 1258536960 | bytes 6062084 | tf_op jit(solution)/shard_map/dot_general | solution.py:106
  90.3 3.2 %fusion.37 = bf16[320,1280]{1,0:T(8,128)(2,1)} fusion(bf16[320,2560]{1,0:T(8,128)(2,1)S(1)} %fusion.18, bf16[1,4096,2560]{2,1,0:T(8,128)(2,1)S(1)} %bitcast.75, s32[]{:T(128)S(6)} %select_n.173), kind=kOutput, calls=%fused_computation.36 | convolution fusion | flops 2097561600 | bytes 9011204 | tf_op jit(solution)/shard_map/dot_general | solution.py:106
  93.5 3.5 %fusion.4 = f32[320,1280]{1,0:T(8,128)} fusion(bf16[320,2560]{1,0:T(8,128)(2,1)S(1)} %fusion.18, bf16[1,4096,2560]{2,1,0:T(8,128)(2,1)S(1)} %bitcast.75, s32[]{:T(128)S(6)} %select_n.172), kind=kOutput, calls=%fused_computation.4 | convolution fusion | flops 2097152000 | bytes 9830404 | tf_op jit(solution)/shard_map/dot_general | solution.py:106
  98.4 3.6 %fusion.21 = f32[320,768]{1,0:T(8,128)S(1)} fusion(bf16[320,2560]{1,0:T(8,128)(2,1)S(1)} %fusion.18, bf16[1,4096,2560]{2,1,0:T(8,128)(2,1)} %param.13, s32[]{:T(128)S(6)} %select_n.174), kind=kOutput, calls=%fused_computation.22 | convolution fusion | flops 1258291200 | bytes 6553604 | tf_op jit(solution)/shard_map/dot_general | solution.py:106
  103.0 4.7 %collective-permute-start.11 = (bf16[128,2048]{1,0:T(8,128)(2,1)}, bf16[128,2048]{1,0:T(8,128)(2,1)}, u32[]{:S(2)}, u32[]{:S(2)}) collective-permute-start(bf16[128,2048]{1,0:T(8,128)(2,1)} %pad_maximum_fusion.2), channel_id=1, source_target_pairs={{0,2},{2,0},{4,6},{6,4},{8,10},{10,8},{12,14},{14,12},{16,18},{18,... | collective-permute-start | bytes 1572872 | tf_op jit(solution)/shard_map/ppermute | solution.py:29
  109.8 12.8 %all-to-all-start.2 = ((bf16[16,40,384]{2,1,0:T(8,128)(2,1)}), bf16[16,40,384]{2,1,0:T(8,128)(2,1)S(1)}, u32[]{:S(2)}, u32[]{:S(2)}) async-start(bf16[16,40,384]{2,1,0:T(8,128)(2,1)} %bitcast.14), calls=%async_computation.2 | async-start | bytes 983040 | tf_op jit(solution)/shard_map/all_to_all | solution.py:103
  123.1 1.6 add_convert_fusion.1
  125.3 1.5 add_convert_fusion
  126.8 9.2 %all-to-all-done.2 = bf16[16,40,384]{2,1,0:T(8,128)(2,1)S(1)} async-done(((bf16[16,40,384]{2,1,0:T(8,128)(2,1)}), bf16[16,40,384]{2,1,0:T(8,128)(2,1)S(1)}, u32[]{:S(2)}, u32[]{:S(2)}) %all-to-all-start.2) | async-done | bytes 491552 | tf_op jit(solution)/shard_map/all_to_all | solution.py:103
  136.0 4.4 %all-to-all-start.3 = ((bf16[16,40,640]{2,1,0:T(8,128)(2,1)}), bf16[16,40,640]{2,1,0:T(8,128)(2,1)S(1)}, u32[]{:S(2)}, u32[]{:S(2)}) async-start(bf16[16,40,640]{2,1,0:T(8,128)(2,1)} %bitcast.16), calls=%async_computation.3 | async-start | bytes 1638400 | tf_op jit(solution)/shard_map/all_to_all | solution.py:103
  140.7 1.4 broadcast_select_fusion.1
  142.1 1.6 maximum_convert_fusion
  145.9 14.8 %all-to-all-done.3 = bf16[16,40,640]{2,1,0:T(8,128)(2,1)S(1)} async-done(((bf16[16,40,640]{2,1,0:T(8,128)(2,1)}), bf16[16,40,640]{2,1,0:T(8,128)(2,1)S(1)}, u32[]{:S(2)}, u32[]{:S(2)}) %all-to-all-start.3) | async-done | bytes 819232 | tf_op jit(solution)/shard_map/all_to_all | solution.py:103
  162.0 1.4 convolution_convert_fusion.5
  163.3 2.1 %pad_maximum_fusion = bf16[256,2048]{1,0:T(8,128)(2,1)} fusion(bf16[256,384]{1,0:T(8,128)(2,1)} %convolution_convert_fusion.8, bf16[256,384]{1,0:T(8,128)(2,1)} %convolution_convert_fusion.9, bf16[256,640]{1,0:T(8,128)(2,1)S(1)} %convolution_convert_fusion.4, bf16[256,640]{1,0:T(8,128)(2,1)S(1)} %convolution_convert_fusion.5), kind=kLoop, calls=%fused_computation.54 | loop fusion | flops 4194304 | bytes 2097152 | tf_op jit(solution)/shard_map/concatenate | solution.py:173
  (87 shorter events, 24.0 us)
Async XLA Ops:
  0.6 13.7 %copy-start = (bf16[1,320,4096]{2,1,0:T(8,128)(2,1)S(1)}, bf16[1,320,4096]{2,1,0:T(8,128)(2,1)}, u32[]{:S(2)}) copy-start(bf16[1,320,4096]{2,1,0:T(8,128)(2,1)} %param.12) | copy-start | bytes 7864324
  0.6 2.7 %copy-start.10 = (s32[256]{0:T(256)S(1)}, s32[256]{0:T(256)}, u32[]{:S(2)}) copy-start(s32[256]{0:T(256)} %param.9) | copy-start | bytes 3076
  0.7 2.7 %copy-start.11 = (s32[256]{0:T(256)S(1)}, s32[256]{0:T(256)}, u32[]{:S(2)}) copy-start(s32[256]{0:T(256)} %param.8) | copy-start | bytes 3076
  5.0 29.1 %all-to-all-start = ((bf16[16,40,640]{2,1,0:T(8,128)(2,1)}), bf16[16,40,640]{2,1,0:T(8,128)(2,1)S(1)}, u32[]{:S(2)}, u32[]{:S(2)}) async-start(bf16[16,40,640]{2,1,0:T(8,128)(2,1)} %bitcast.66), calls=%async_computation | async-start | bytes 1638400 | tf_op jit(solution)/shard_map/all_to_all | solution.py:103
  14.0 16.3 %collective-permute-start.4 = (bf16[128,2048]{1,0:T(8,128)(2,1)}, bf16[128,2048]{1,0:T(8,128)(2,1)}, u32[]{:S(2)}, u32[]{:S(2)}) collective-permute-start(bf16[128,2048]{1,0:T(8,128)(2,1)} %select_convert_fusion), channel_id=1, source_target_pairs={{0,2},{2,0},{4,6},{6,4},{8,10},{10,8},{12,14},{14,12},{16,18},{18,... | collective-permute-start | bytes 1572872 | tf_op jit(solution)/shard_map/ppermute | solution.py:29
  32.9 8.1 %collective-permute-start.5 = (bf16[64,2048]{1,0:T(8,128)(2,1)}, bf16[64,2048]{1,0:T(8,128)(2,1)}, u32[]{:S(2)}, u32[]{:S(2)}) collective-permute-start(bf16[64,2048]{1,0:T(8,128)(2,1)} %select_convert_fusion.1), channel_id=1, source_target_pairs={{0,4},{2,6},{4,0},{6,2},{8,12},{10,14},{12,8},{14,10},{16,20},{18,... | collective-permute-start | bytes 786440 | tf_op jit(solution)/shard_map/ppermute | solution.py:29
  34.6 2.0 %copy-start.7 = (bf16[320,640]{1,0:T(8,128)(2,1)}, bf16[320,640]{1,0:T(8,128)(2,1)S(1)}, u32[]{:S(2)}) copy-start(bf16[320,640]{1,0:T(8,128)(2,1)S(1)} %convolution_convert_fusion.2) | copy-start | bytes 1228804
  35.3 6.7 %copy-start.8 = (bf16[320,640]{1,0:T(8,128)(2,1)}, bf16[320,640]{1,0:T(8,128)(2,1)S(1)}, u32[]{:S(2)}) copy-start(bf16[320,640]{1,0:T(8,128)(2,1)S(1)} %convolution_convert_fusion.3) | copy-start | bytes 1228804
  35.3 19.4 %collective-permute-start = (bf16[320,1280]{1,0:T(8,128)(2,1)S(1)}, bf16[320,1280]{1,0:T(8,128)(2,1)S(1)}, u32[]{:S(2)}, u32[]{:S(2)}) collective-permute-start(bf16[320,1280]{1,0:T(8,128)(2,1)S(1)} %pad_maximum_fusion.1), channel_id=1, source_target_pairs={{0,1},{1,0},{2,3},{3,2},{4,5},{5,4},{6,7},{7,6},{8,9},{9,8},{10,11... | collective-permute-start | bytes 2457608 | tf_op jit(solution)/shard_map/ppermute | solution.py:29
  42.0 20.1 %all-to-all-start.1 = ((bf16[16,40,384]{2,1,0:T(8,128)(2,1)}), bf16[16,40,384]{2,1,0:T(8,128)(2,1)S(1)}, u32[]{:S(2)}, u32[]{:S(2)}) async-start(bf16[16,40,384]{2,1,0:T(8,128)(2,1)} %bitcast.69), calls=%async_computation.1 | async-start | bytes 983040 | tf_op jit(solution)/shard_map/all_to_all | solution.py:103
  62.1 3.9 %collective-permute-start.6 = (bf16[32,2048]{1,0:T(8,128)(2,1)S(1)}, bf16[32,2048]{1,0:T(8,128)(2,1)S(1)}, u32[]{:S(2)}, u32[]{:S(2)}) collective-permute-start(bf16[32,2048]{1,0:T(8,128)(2,1)S(1)} %select_convert_fusion.2), channel_id=1, source_target_pairs={{0,8},{2,10},{4,12},{6,14},{8,0},{10,2},{12,4},{14,6},{16,24},{18,... | collective-permute-start | bytes 393224 | tf_op jit(solution)/shard_map/ppermute | solution.py:29
  66.0 4.1 %collective-permute-start.7 = (bf16[16,2048]{1,0:T(8,128)(2,1)S(1)}, bf16[16,2048]{1,0:T(8,128)(2,1)S(1)}, u32[]{:S(2)}, u32[]{:S(2)}) collective-permute-start(bf16[16,2048]{1,0:T(8,128)(2,1)S(1)} %select_convert_fusion.3), channel_id=1, source_target_pairs={{0,16},{2,18},{4,20},{6,22},{8,24},{10,26},{12,28},{14,30},{16,0},... | collective-permute-start | bytes 196616 | tf_op jit(solution)/shard_map/ppermute | solution.py:29
  70.1 20.2 %slice-start = ((s8[20971520]{0:T(1024)(128)(4,1)}), s8[4194304]{0:T(1024)(128)(4,1)S(1)}, s32[]{:S(2)}) async-start(s8[20971520]{0:T(1024)(128)(4,1)} %bitcast.74), calls=%async_computation.4 | async-start | bytes 8388608
  70.1 4.1 %collective-permute-start.8 = (bf16[16,2048]{1,0:T(8,128)(2,1)S(1)}, bf16[16,2048]{1,0:T(8,128)(2,1)S(1)}, u32[]{:S(2)}, u32[]{:S(2)}) collective-permute-start(bf16[16,2048]{1,0:T(8,128)(2,1)S(1)} %add_convert_fusion.3), channel_id=1, source_target_pairs={{0,16},{2,18},{4,20},{6,22},{8,24},{10,26},{12,28},{14,30},{16,0},... | collective-permute-start | bytes 196616 | tf_op jit(solution)/shard_map/ppermute | solution.py:29
  72.7 9.6 %collective-permute-start.1 = (bf16[320,768]{1,0:T(8,128)(2,1)S(1)}, bf16[320,768]{1,0:T(8,128)(2,1)S(1)}, u32[]{:S(2)}, u32[]{:S(2)}) collective-permute-start(bf16[320,768]{1,0:T(8,128)(2,1)S(1)} %pad_maximum_fusion.3), channel_id=1, source_target_pairs={{0,1},{1,0},{2,3},{3,2},{4,5},{5,4},{6,7},{7,6},{8,9},{9,8},{10,11... | collective-permute-start | bytes 1474568 | tf_op jit(solution)/shard_map/ppermute | solution.py:29
  74.3 4.1 %copy-start.4 = (f32[320,2560]{1,0:T(8,128)S(1)}, f32[320,2560]{1,0:T(8,128)}, u32[]{:S(2)}) copy-start(f32[320,2560]{1,0:T(8,128)} %fusion.14) | copy-start | bytes 9830404
  74.3 15.9 %slice-start.1 = ((s8[20971520]{0:T(1024)(128)(4,1)}), s8[4194304]{0:T(1024)(128)(4,1)S(1)}, s32[]{:S(2)}) async-start(s8[20971520]{0:T(1024)(128)(4,1)} %bitcast.74), calls=%async_computation.5 | async-start | bytes 8388608
  74.3 4.9 %collective-permute-start.9 = (bf16[32,2048]{1,0:T(8,128)(2,1)S(1)}, bf16[32,2048]{1,0:T(8,128)(2,1)S(1)}, u32[]{:S(2)}, u32[]{:S(2)}) collective-permute-start(bf16[32,2048]{1,0:T(8,128)(2,1)S(1)} %pad_maximum_fusion.5), channel_id=1, source_target_pairs={{0,8},{2,10},{4,12},{6,14},{8,0},{10,2},{12,4},{14,6},{16,24},{18,... | collective-permute-start | bytes 393224 | tf_op jit(solution)/shard_map/ppermute | solution.py:29
  78.4 3.8 %copy-start.2 = (f32[320,2560]{1,0:T(8,128)S(1)}, f32[320,2560]{1,0:T(8,128)}, u32[]{:S(2)}) copy-start(f32[320,2560]{1,0:T(8,128)} %fusion.34) | copy-start | bytes 9830404
  78.4 11.8 %slice-start.2 = ((s8[20971520]{0:T(1024)(128)(4,1)}), s8[4194304]{0:T(1024)(128)(4,1)S(1)}, s32[]{:S(2)}) async-start(s8[20971520]{0:T(1024)(128)(4,1)} %bitcast.74), calls=%async_computation.6 | async-start | bytes 8388608
  79.3 11.0 %slice-start.3 = ((s8[20971520]{0:T(1024)(128)(4,1)}), s8[4194304]{0:T(1024)(128)(4,1)S(1)}, s32[]{:S(2)}) async-start(s8[20971520]{0:T(1024)(128)(4,1)} %bitcast.74), calls=%async_computation.7 | async-start | bytes 8388608
  79.3 11.0 %slice-start.4 = ((s8[20971520]{0:T(1024)(128)(4,1)}), s8[4194304]{0:T(1024)(128)(4,1)S(1)}, s32[]{:S(2)}) async-start(s8[20971520]{0:T(1024)(128)(4,1)} %bitcast.74), calls=%async_computation.8 | async-start | bytes 8388608
  79.3 22.7 %collective-permute-start.10 = (bf16[64,2048]{1,0:T(8,128)(2,1)S(1)}, bf16[64,2048]{1,0:T(8,128)(2,1)S(1)}, u32[]{:S(2)}, u32[]{:S(2)}) collective-permute-start(bf16[64,2048]{1,0:T(8,128)(2,1)S(1)} %pad_maximum_fusion.4), channel_id=1, source_target_pairs={{0,4},{2,6},{4,0},{6,2},{8,12},{10,14},{12,8},{14,10},{16,20},{18,... | collective-permute-start | bytes 786440 | tf_op jit(solution)/shard_map/ppermute | solution.py:29
  97.0 10.7 %collective-permute-start.3 = (bf16[320,768]{1,0:T(8,128)(2,1)S(1)}, bf16[320,768]{1,0:T(8,128)(2,1)S(1)}, u32[]{:S(2)}, u32[]{:S(2)}) collective-permute-start(bf16[320,768]{1,0:T(8,128)(2,1)S(1)} %fusion.41), channel_id=1, source_target_pairs={{0,1},{1,0},{2,3},{3,2},{4,5},{5,4},{6,7},{7,6},{8,9},{9,8},{10,11... | collective-permute-start | bytes 1474568 | tf_op jit(solution)/shard_map/ppermute | solution.py:29
  98.2 24.9 %collective-permute-start.2 = (bf16[320,1280]{1,0:T(8,128)(2,1)}, bf16[320,1280]{1,0:T(8,128)(2,1)S(1)}, u32[]{:S(2)}, u32[]{:S(2)}) collective-permute-start(bf16[320,1280]{1,0:T(8,128)(2,1)} %fusion.37), channel_id=1, source_target_pairs={{0,1},{1,0},{2,3},{3,2},{4,5},{5,4},{6,7},{7,6},{8,9},{9,8},{10,11... | collective-permute-start | bytes 2457608 | tf_op jit(solution)/shard_map/ppermute | solution.py:29
  103.0 37.7 %collective-permute-start.11 = (bf16[128,2048]{1,0:T(8,128)(2,1)}, bf16[128,2048]{1,0:T(8,128)(2,1)}, u32[]{:S(2)}, u32[]{:S(2)}) collective-permute-start(bf16[128,2048]{1,0:T(8,128)(2,1)} %pad_maximum_fusion.2), channel_id=1, source_target_pairs={{0,2},{2,0},{4,6},{6,4},{8,10},{10,8},{12,14},{14,12},{16,18},{18,... | collective-permute-start | bytes 1572872 | tf_op jit(solution)/shard_map/ppermute | solution.py:29
  109.8 26.2 %all-to-all-start.2 = ((bf16[16,40,384]{2,1,0:T(8,128)(2,1)}), bf16[16,40,384]{2,1,0:T(8,128)(2,1)S(1)}, u32[]{:S(2)}, u32[]{:S(2)}) async-start(bf16[16,40,384]{2,1,0:T(8,128)(2,1)} %bitcast.14), calls=%async_computation.2 | async-start | bytes 983040 | tf_op jit(solution)/shard_map/all_to_all | solution.py:103
  136.0 4.7 %copy-start.5 = (bf16[16,40,384]{2,1,0:T(8,128)(2,1)}, bf16[16,40,384]{2,1,0:T(8,128)(2,1)S(1)}, u32[]{:S(2)}) copy-start(bf16[16,40,384]{2,1,0:T(8,128)(2,1)S(1)} %all-to-all-done.2) | copy-start | bytes 1474564
  136.0 24.6 %all-to-all-start.3 = ((bf16[16,40,640]{2,1,0:T(8,128)(2,1)}), bf16[16,40,640]{2,1,0:T(8,128)(2,1)S(1)}, u32[]{:S(2)}, u32[]{:S(2)}) async-start(bf16[16,40,640]{2,1,0:T(8,128)(2,1)} %bitcast.16), calls=%async_computation.3 | async-start | bytes 1638400 | tf_op jit(solution)/shard_map/all_to_all | solution.py:103
  140.6 4.1 %copy-start.9 = (pred[640,512]{1,0:T(32,128)(4,1)}, pred[640,512]{1,0:T(32,128)(4,1)S(1)}, u32[]{:S(2)}) copy-start(pred[640,512]{1,0:T(32,128)(4,1)S(1)} %iota_compare_fusion) | copy-start | bytes 983044
  140.7 3.0 %copy-start.6 = (bf16[16,40,384]{2,1,0:T(8,128)(2,1)S(1)}, bf16[16,40,384]{2,1,0:T(8,128)(2,1)}, u32[]{:S(2)}) copy-start(bf16[16,40,384]{2,1,0:T(8,128)(2,1)} %copy-done.5) | copy-start | bytes 1474564
  143.6 21.8 %copy-start.1 = (bf16[1,320,4096]{2,1,0:T(8,128)(2,1)S(1)}, bf16[1,320,4096]{2,1,0:T(8,128)(2,1)}, u32[]{:S(2)}) copy-start(bf16[1,320,4096]{2,1,0:T(8,128)(2,1)} %param.12) | copy-start | bytes 7864324
  (1 other events, 1.0 us)

commit v3 on v2

--- a/solution.py
+++ b/solution.py
@@ -47,16 +47,26 @@
     return [1 << i for i in range(size.bit_length() - 1)]
 
 
-def summed_over(part, axis, early, gate):
-    bits = bits_of(lax.axis_size(axis))
-    for i, bit in enumerate(bits):
-        if i == early:
-            part = after(part, gate)
-        part = halve(part, axis, bit)
-    part = part.astype(BF16)
-    for bit in reversed(bits):
-        part = double(part, axis, bit)
-    return part.astype(F32)
+class Summed:
+    def __init__(self, part, axis):
+        bits = bits_of(lax.axis_size(axis))
+        self.axis, self.part = axis, part
+        self.steps = [(halve, bit) for bit in bits] + [(double, bit) for bit in reversed(bits)]
+        self.doubling = len(bits)
+
+    def step(self, *others):
+        if not self.steps or (self.doubling == len(self.steps) and self.part.dtype != BF16):
+            self.part = self.part.astype(BF16)
+        if self.steps:
+            run, bit = self.steps.pop(0)
+            self.part = run(after(self.part, *others) if others else self.part, self.axis, bit)
+        return self.part
+
+    def rest(self, *others):
+        while self.steps:
+            self.step(*others)
+            others = ()
+        return self.part.astype(F32)
 
 
 def one_hot(rows, columns):
@@ -116,53 +126,64 @@
         )
         outgoing.append(dot(table, stacked).astype(BF16))
 
-    saved = after(saved_inputs[0], outgoing[0])
+    dense = Summed(dense_partial[0], "expert")
+    saved = saved_inputs[0]
     slopes = lax.optimization_barrier(slope_of(dot(saved, w_in[0])))
     arrived = [all_to_all(outgoing[0])]
     for block in outgoing[1:]:
         arrived.append(all_to_all(after(block, arrived[-1], slopes)))
     mine = [jnp.concatenate([tn_dot(t, block).astype(BF16) for t in spread], axis=1) for block in arrived]
-    dense_sum = summed_over(after(dense_partial[0], outgoing[0]), "expert", 2, arrived[-1])
+
+    def up_share(who, i, x):
+        w = lax.dynamic_slice_in_dim(w_out[0], who * features + starts[i], widths[i], 1)
+        return nt_dot(x, w)
 
     if pair:
-        upstream = None
-        waiting = []
-        for i, (start, width) in enumerate(zip(starts, widths)):
-            own = mine[i]
-            if upstream is not None:
-                own = after(own, upstream)
-            theirs = xor_send(own, "mp", 1)
-            todo = waiting + [(me, start, width, own)]
-            for who, first, wide, x in todo:
-                w = lax.dynamic_slice_in_dim(w_out[0], who * features + first, wide, 1)
-                term = nt_dot(x, w)
-                upstream = lax.optimization_barrier(term if upstream is None else upstream + term)
-            waiting = [(1 - me, start, width, theirs)]
-        for who, first, wide, x in waiting:
-            w = lax.dynamic_slice_in_dim(w_out[0], who * features + first, wide, 1)
-            upstream = upstream + nt_dot(x, w)
+        theirs = [xor_send(own, "mp", 1) for own in mine]
+        upstream = lax.optimization_barrier(up_share(me, 0, mine[0]))
+        dense.step(slopes)
+        for i in range(1, len(widths)):
+            fence = dense.step(arrived[i])
+            upstream = lax.optimization_barrier(upstream + up_share(1 - me, i - 1, after(theirs[i - 1], fence)))
+            upstream = lax.optimization_barrier(upstream + up_share(me, i, mine[i]))
+        upstream = upstream + up_share(1 - me, len(widths) - 1, theirs[-1])
     else:
         upstream = nt_dot(lax.all_gather(mine[0], "mp", axis=1, tiled=True), w_out[0])
     hidden = lax.optimization_barrier((upstream * slopes).astype(BF16))
 
-    def share_of(who, start, width):
-        return nt_dot(hidden, lax.dynamic_slice_in_dim(w_in[0], who * features + start, width, 0))
-
+    widths = chunk_widths(features, 0.625) if pair else [features]
+    starts = [sum(widths[:i]) for i in range(len(widths))]
     order = list(reversed(range(len(widths))))
+
+    def down_share(source, who, i):
+        w = lax.dynamic_slice_in_dim(w_in[0], who * features + starts[i], widths[i], 0)
+        return nt_dot(source, w)
+
     if pair:
-        sent = {i: xor_send(share_of(1 - me, starts[i], widths[i]).astype(BF16), "mp", 1) for i in order}
-        kept = {i: lax.optimization_barrier(share_of(me, starts[i], widths[i])) for i in order}
+        while len(dense.steps) > dense.doubling:
+            dense.step()
+        leaving = {}
+        source = hidden
+        for i in order:
+            leaving[i] = lax.optimization_barrier(down_share(source, 1 - me, i).astype(BF16))
+            source = after(hidden, leaving[i])
+        for _ in range(dense.doubling // 2):
+            dense.step(hidden)
     outs = {}
     last = None
     for i in order:
         part = widths[i] // fold
         if pair:
-            total = (kept[i] + sent[i].astype(F32)).astype(BF16)
+            sent = xor_send(leaving[i] if last is None else after(leaving[i], folded), "mp", 1)
+            kept = lax.optimization_barrier(down_share(source, me, i))
+            total = (kept + sent.astype(F32)).astype(BF16)
         else:
             total = lax.psum_scatter(
                 nt_dot(hidden, w_in[0]), "mp", scatter_dimension=1, tiled=True
             ).astype(BF16)
         folded = sum(dot(t, total[:, h * part : (h + 1) * part]) for h, t in enumerate(spread)).astype(BF16)
+        if pair:
+            source = after(hidden, dense.step(folded))
         if last is not None:
             folded = after(folded, last)
         last = all_to_all(folded)
@@ -170,6 +191,7 @@
             [tn_dot(table[:, h * tok_count : (h + 1) * tok_count], last).astype(BF16) for h in range(fold)],
             axis=1,
         )
+    dense_sum = dense.rest()
     return (jnp.concatenate([outs[i] for i in sorted(order)], axis=1), dense_sum)
 
 

time: 166 us -> 149 us (0.90)
  starting transfers between devices: 48.6 us -> 35.6 us
  other arithmetic: 16.5 us -> 10.2 us
  matrix products: 61.8 us -> 67.6 us
  waiting for transfers between devices: 35.2 us -> 29.7 us
    ppermute x12, starting transfers between devices: 18.2 us -> 10.2 us  [xor_send(): return lax.ppermute(value, axis, [(i, i ^ bit) for i in range(size)])]
    all_to_all x4, starting transfers between devices: 30.4 us -> 25.4 us  [all_to_all(): lax.all_to_all(block, 'expert', split_axis=0, concat_axis=0, tiled=True)]
    all_to_all x4, waiting for transfers between devices: 24.3 us -> 20.6 us  [all_to_all(): lax.all_to_all(block, 'expert', split_axis=0, concat_axis=0, tiled=True)]
    dot_general x8, matrix products: 34.3 us -> 37.9 us  [nt_dot(): return lax.dot_general(a, b, NT, preferred_element_type=F32)]
    dot_general x8, matrix products: 7.15 us -> 9.36 us  [tn_dot(): lax.dot_general(a, b, (((0,), (0,)), ((), ())), preferred_element_type=F32)]
    ppermute x12, waiting for transfers between devices: 10.9 us -> 9.09 us  [xor_send(): return lax.ppermute(value, axis, [(i, i ^ bit) for i in range(size)])]
  transfers between devices with their start and end apart: 16 -> 16, of which waited for: 10 -> 7; matrix products, arithmetic and copies ran while one was open for 43% -> 42% of each run, Pallas kernels for 0% -> 0%
where the time goes in v3:
time: 149 us; the launch traced here: 148 us
  matrix products  67.6 us (45%)
  starting transfers between devices  35.6 us (24%)
  waiting for transfers between devices  29.7 us (20%)
  other arithmetic  10.2 us (7%)
  local copies, waits for them, and re-layouts  3.54 us (2%)
    dot_general x8, matrix products, nt_dot(): return lax.dot_general(a, b, NT, preferred_element_type=F32)  37.9 us
    all_to_all x4, starting transfers between devices, all_to_all(): lax.all_to_all(block, 'expert', split_axis=0, concat_axis=0, tiled=True)  25.4 us
    all_to_all x4, waiting for transfers between devices, all_to_all(): lax.all_to_all(block, 'expert', split_axis=0, concat_axis=0, tiled=True)  20.6 us
    dot_general x7, matrix products, dot(): return jnp.dot(a, b, preferred_element_type=F32)  20.4 us
    ppermute x12, starting transfers between devices, xor_send(): return lax.ppermute(value, axis, [(i, i ^ bit) for i in range(size)])  10.2 us
    dot_general x8, matrix products, tn_dot(): lax.dot_general(a, b, (((0,), (0,)), ((), ())), preferred_element_type=F32)  9.36 us
    ppermute x12, waiting for transfers between devices, xor_send(): return lax.ppermute(value, axis, [(i, i ^ bit) for i in range(size)])  9.09 us
  transfers between devices with their start and end apart: 16, of which 7 were waited for; matrix products, arithmetic and copies ran while one was open for 42% of the time, Pallas kernels for 0%

profile of v3, /device:TPU:9, one launch (start us, length us, event | category | flops | bytes accessed | tf_op | source)
XLA Modules:
  0.0 147.8 jit_solution(11293986990868959342)
XLA Ops:
  0.7 1.6 %multiply_convert_fusion = bf16[256,2048]{1,0:T(8,128)(2,1)S(1)} fusion(bf16[256,2048]{1,0:T(8,128)(2,1)} %param.11, f32[256]{0:T(256)} %param.10), kind=kLoop, calls=%fused_computation.38 | loop fusion | flops 1572864 | bytes 2098176 | tf_op jit(solution)/shard_map/convert_element_type | solution.py:99
  3.4 1.6 %convolution_convert_fusion = bf16[640,640]{1,0:T(8,128)(2,1)} fusion(bf16[256,640]{1,0:T(8,128)(2,1)S(1)} %get-tuple-element.33, bf16[256,640]{1,0:T(8,128)(2,1)S(1)} %get-tuple-element.32, s32[512]{0:T(512)S(1)} %pad_add_fusion), kind=kOutput, calls=%fused_computation.41 | convolution fusion | flops 421478400 | bytes 1476608 | tf_op jit(solution)/shard_map/dot_general | solution.py:77
  5.0 6.6 %all-to-all-start = ((bf16[16,40,640]{2,1,0:T(8,128)(2,1)}), bf16[16,40,640]{2,1,0:T(8,128)(2,1)S(1)}, u32[]{:S(2)}, u32[]{:S(2)}) async-start(bf16[16,40,640]{2,1,0:T(8,128)(2,1)} %bitcast.65), calls=%async_computation | async-start | bytes 1638400 | tf_op jit(solution)/shard_map/all_to_all | solution.py:113
  11.6 13.5 %fusion.34 = f32[320,2560]{1,0:T(8,128)} fusion(bf16[1,4096,2560]{2,1,0:T(8,128)(2,1)} %param.13, bf16[1,320,4096]{2,1,0:T(8,128)(2,1)S(1)} %copy-done), kind=kOutput, calls=%fused_computation.35 | convolution fusion | flops 6724812800 | bytes 26869760 | tf_op jit(solution)/shard_map/dot_general | solution.py:77
  25.1 1.6 %select_convert_fusion = bf16[128,2048]{1,0:T(8,128)(2,1)S(1)} fusion(f32[256,2048]{1,0:T(8,128)} %bitcast.61, pred[]{:T(512)S(6)} %ne.101), kind=kLoop, calls=%fused_computation.58 | loop fusion | flops 262144 | bytes 1572865 | tf_op jit(solution)/shard_map/convert_element_type | solution.py:37
  29.6 1.7 %convert_add_fusion = f32[128,2048]{1,0:T(8,128)S(1)} fusion(bf16[128,2048]{1,0:T(8,128)(2,1)S(1)} %collective-permute-done.1, f32[256,2048]{1,0:T(8,128)} %bitcast.62, pred[]{:T(512)S(6)} %ne.101), kind=kLoop, calls=%fused_computation.57 | loop fusion | flops 786432 | bytes 3670017 | tf_op jit(solution)/shard_map/add | solution.py:37
  31.8 5.4 %all-to-all-start.1 = ((bf16[16,40,384]{2,1,0:T(8,128)(2,1)}), bf16[16,40,384]{2,1,0:T(8,128)(2,1)S(1)}, u32[]{:S(2)}, u32[]{:S(2)}) async-start(bf16[16,40,384]{2,1,0:T(8,128)(2,1)} %bitcast.6), calls=%async_computation.1 | async-start | bytes 983040 | tf_op jit(solution)/shard_map/all_to_all | solution.py:113
  39.7 6.9 %fusion.8 = f32[320,2560]{1,0:T(8,128)} fusion(bf16[1,2560,4096]{2,1,0:T(8,128)(2,1)} %param.14, s32[]{:T(128)S(6)} %select_n.172, bf16[320,640]{1,0:T(8,128)(2,1)S(1)} %convolution_convert_fusion.2, bf16[320,640]{1,0:T(8,128)(2,1)S(1)} %convolution_convert_fusion.3), kind=kOutput, calls=%fused_computation.8 | convolution fusion | flops 2098790400 | bytes 10649604 | tf_op jit(solution)/shard_map/dot_general | solution.py:116
  46.6 4.0 %all-to-all-done.1 = bf16[16,40,384]{2,1,0:T(8,128)(2,1)S(1)} async-done(((bf16[16,40,384]{2,1,0:T(8,128)(2,1)}), bf16[16,40,384]{2,1,0:T(8,128)(2,1)S(1)}, u32[]{:S(2)}, u32[]{:S(2)}) %all-to-all-start.1) | async-done | bytes 491552 | tf_op jit(solution)/shard_map/all_to_all | solution.py:113
  52.7 1.3 collective-permute-start.3
  54.0 5.2 %collective-permute-done.2 = bf16[64,2048]{1,0:T(8,128)(2,1)S(1)} collective-permute-done((bf16[64,2048]{1,0:T(8,128)(2,1)S(1)}, bf16[64,2048]{1,0:T(8,128)(2,1)S(1)}, u32[]{:S(2)}, u32[]{:S(2)}) %collective-permute-start.2) | collective-permute-done | bytes 262176 | tf_op jit(solution)/shard_map/ppermute | solution.py:29
  59.4 3.8 %fusion.24 = f32[320,2560]{1,0:T(8,128)S(1)} fusion(bf16[1,2560,4096]{2,1,0:T(8,128)(2,1)} %param.14, s32[]{:T(128)S(6)} %select_n.180, bf16[320,384]{1,0:T(8,128)(2,1)S(1)} %convolution_convert_fusion.6, bf16[320,384]{1,0:T(8,128)(2,1)S(1)} %convolution_convert_fusion.7), kind=kOutput, calls=%fused_computation.25 | convolution fusion | flops 1259274240 | bytes 7700484 | tf_op jit(solution)/shard_map/dot_general | solution.py:116
  64.4 5.2 %fusion.14 = f32[320,2560]{1,0:T(8,128)S(1)} fusion(f32[320,2560]{1,0:T(8,128)S(1)} %copy-done.7, bf16[320,1280]{1,0:T(8,128)(2,1)S(1)} %collective-permute-done, bf16[1,2560,4096]{2,1,0:T(8,128)(2,1)} %param.14, s32[]{:T(128)S(6)} %select_n.179), kind=kOutput, calls=%fused_computation.16 | convolution fusion | flops 2097971200 | bytes 13926404 | tf_op jit(solution)/shard_map/dot_general | solution.py:116
  70.1 1.4 copy-done.2
  71.5 3.6 %fusion.18 = bf16[320,2560]{1,0:T(8,128)(2,1)S(1)} fusion(f32[320,2560]{1,0:T(8,128)S(1)} %copy-done.2, f32[320,2560]{1,0:T(8,128)S(1)} %add.181, bf16[320,768]{1,0:T(8,128)(2,1)S(1)} %collective-permute-done.3, bf16[1,2560,4096]{2,1,0:T(8,128)(2,1)} %param.14, s32[]{:T(128)S(6)} %select_n.181), kind=kOutput, calls=%fused_computation.19 | convolution fusion | flops 1260748800 | bytes 12615684 | tf_op jit(solution)/shard_map/dot_general | solution.py:116
  75.1 3.6 %fusion.42 = bf16[320,768]{1,0:T(8,128)(2,1)S(1)} fusion(bf16[320,2560]{1,0:T(8,128)(2,1)S(1)} %fusion.18, bf16[1,4096,2560]{2,1,0:T(8,128)(2,1)} %param.13, s32[]{:T(128)S(6)} %select_n.181), kind=kOutput, calls=%fused_computation.46 | convolution fusion | flops 1258536960 | bytes 6062084 | tf_op jit(solution)/shard_map/dot_general | solution.py:116
  80.0 1.8 %collective-permute-start.6 = (bf16[16,2048]{1,0:T(8,128)(2,1)S(1)}, bf16[16,2048]{1,0:T(8,128)(2,1)S(1)}, u32[]{:S(2)}, u32[]{:S(2)}) collective-permute-start(bf16[16,2048]{1,0:T(8,128)(2,1)S(1)} %add_convert_fusion.3), channel_id=1, source_target_pairs={{0,16},{2,18},{4,20},{6,22},{8,24},{10,26},{12,28},{14,30},{16,0},... | collective-permute-start | bytes 196616 | tf_op jit(solution)/shard_map/ppermute | solution.py:29
  81.8 6.1 %fusion.37 = bf16[320,1280]{1,0:T(8,128)(2,1)} fusion(bf16[320,2560]{1,0:T(8,128)(2,1)S(1)} %fusion.18, bf16[1,4096,2560]{2,1,0:T(8,128)(2,1)} %param.13, s32[]{:T(128)S(6)} %select_n.179), kind=kOutput, calls=%fused_computation.36 | convolution fusion | flops 2097561600 | bytes 9011204 | tf_op jit(solution)/shard_map/dot_general | solution.py:116
  88.8 3.6 %fusion.19 = f32[320,768]{1,0:T(8,128)S(1)} fusion(bf16[320,2560]{1,0:T(8,128)(2,1)S(1)} %fusion.18, bf16[1,4096,2560]{2,1,0:T(8,128)(2,1)} %param.13, s32[]{:T(128)S(6)} %select_n.180), kind=kOutput, calls=%fused_computation.20 | convolution fusion | flops 1258291200 | bytes 6553604 | tf_op jit(solution)/shard_map/dot_general | solution.py:116
  95.7 7.8 %all-to-all-start.2 = ((bf16[16,40,384]{2,1,0:T(8,128)(2,1)}), bf16[16,40,384]{2,1,0:T(8,128)(2,1)}, u32[]{:S(2)}, u32[]{:S(2)}) async-start(bf16[16,40,384]{2,1,0:T(8,128)(2,1)} %bitcast.15), calls=%async_computation.2 | async-start | bytes 983040 | tf_op jit(solution)/shard_map/all_to_all | solution.py:113
  103.6 5.2 %fusion.2 = f32[320,1280]{1,0:T(8,128)S(1)} fusion(bf16[320,2560]{1,0:T(8,128)(2,1)S(1)} %fusion.18, bf16[1,4096,2560]{2,1,0:T(8,128)(2,1)} %param.13, s32[]{:T(128)S(6)} %select_n.172), kind=kOutput, calls=%fused_computation.2 | convolution fusion | flops 2097152000 | bytes 9830404 | tf_op jit(solution)/shard_map/dot_general | solution.py:116
  108.8 3.4 %collective-permute-done.10 = bf16[320,1280]{1,0:T(8,128)(2,1)S(1)} collective-permute-done((bf16[320,1280]{1,0:T(8,128)(2,1)}, bf16[320,1280]{1,0:T(8,128)(2,1)S(1)}, u32[]{:S(2)}, u32[]{:S(2)}) %collective-permute-start.10) | collective-permute-done | bytes 819232 | tf_op jit(solution)/shard_map/ppermute | solution.py:29
  113.0 1.5 %add_convert_fusion = bf16[640,640]{1,0:T(8,128)(2,1)} fusion(f32[640,640]{1,0:T(8,128)S(1)} %fusion.45, s32[320]{0:T(512)S(1)} %get-tuple-element.43, bf16[320,1280]{1,0:T(8,128)(2,1)S(1)} %add_convert_fusion.1), kind=kOutput, calls=%fused_computation.39 | convolution fusion | flops 263168000 | bytes 2869248 | tf_op jit(solution)/shard_map/dot_general | solution.py:77
  114.5 2.6 %all-to-all-done.2 = bf16[16,40,384]{2,1,0:T(8,128)(2,1)} async-done(((bf16[16,40,384]{2,1,0:T(8,128)(2,1)}), bf16[16,40,384]{2,1,0:T(8,128)(2,1)}, u32[]{:S(2)}, u32[]{:S(2)}) %all-to-all-start.2) | async-done | bytes 491552 | tf_op jit(solution)/shard_map/all_to_all | solution.py:113
  117.1 5.6 %all-to-all-start.3 = ((bf16[16,40,640]{2,1,0:T(8,128)(2,1)}), bf16[16,40,640]{2,1,0:T(8,128)(2,1)S(1)}, u32[]{:S(2)}, u32[]{:S(2)}) async-start(bf16[16,40,640]{2,1,0:T(8,128)(2,1)} %bitcast.17), calls=%async_computation.3 | async-start | bytes 1638400 | tf_op jit(solution)/shard_map/all_to_all | solution.py:113
  123.3 2.2 %convolution_convert_fusion.9 = bf16[256,384]{1,0:T(8,128)(2,1)} fusion(bf16[640,384]{1,0:T(8,128)(2,1)} %bitcast.16, pred[640,512]{1,0:T(32,128)(4,1)S(1)} %iota_compare_fusion), kind=kOutput, calls=%fused_computation.54 | convolution fusion | flops 125927424 | bytes 851968 | tf_op jit(solution)/shard_map/dot_general | solution.py:119
  125.5 2.2 %convolution_convert_fusion.8 = bf16[256,384]{1,0:T(8,128)(2,1)} fusion(bf16[640,384]{1,0:T(8,128)(2,1)} %bitcast.16, pred[640,512]{1,0:T(32,128)(4,1)S(1)} %iota_compare_fusion), kind=kOutput, calls=%fused_computation.53 | convolution fusion | flops 125927424 | bytes 851968 | tf_op jit(solution)/shard_map/dot_general | solution.py:119
  127.8 1.6 %maximum_convert_fusion = f32[256,2048]{1,0:T(8,128)} fusion(bf16[128,2048]{1,0:T(8,128)(2,1)S(1)} %get-tuple-element.29, bf16[128,2048]{1,0:T(8,128)(2,1)S(1)} %get-tuple-element.28), kind=kLoop, calls=%fused_computation.56 | loop fusion | flops 2097152 | bytes 3145728 | tf_op jit(solution)/shard_map/convert_element_type | solution.py:69
  129.4 13.6 %all-to-all-done.3 = bf16[16,40,640]{2,1,0:T(8,128)(2,1)S(1)} async-done(((bf16[16,40,640]{2,1,0:T(8,128)(2,1)}), bf16[16,40,640]{2,1,0:T(8,128)(2,1)S(1)}, u32[]{:S(2)}, u32[]{:S(2)}) %all-to-all-start.3) | async-done | bytes 819232 | tf_op jit(solution)/shard_map/all_to_all | solution.py:113
  142.9 1.3 convolution_convert_fusion.5
  144.3 1.3 convolution_convert_fusion.4
  145.6 2.1 %pad_maximum_fusion = bf16[256,2048]{1,0:T(8,128)(2,1)} fusion(bf16[256,384]{1,0:T(8,128)(2,1)} %convolution_convert_fusion.8, bf16[256,384]{1,0:T(8,128)(2,1)} %convolution_convert_fusion.9, bf16[256,640]{1,0:T(8,128)(2,1)S(1)} %convolution_convert_fusion.4, bf16[256,640]{1,0:T(8,128)(2,1)S(1)} %convolution_convert_fusion.5), kind=kLoop, calls=%fused_computation.55 | loop fusion | flops 4194304 | bytes 2097152 | tf_op jit(solution)/shard_map/concatenate | solution.py:195
  (68 shorter events, 17.8 us)
Async XLA Ops:
  0.6 10.9 %copy-start = (bf16[1,320,4096]{2,1,0:T(8,128)(2,1)S(1)}, bf16[1,320,4096]{2,1,0:T(8,128)(2,1)}, u32[]{:S(2)}) copy-start(bf16[1,320,4096]{2,1,0:T(8,128)(2,1)} %param.12) | copy-start | bytes 7864324
  0.6 2.7 %copy-start.6 = (s32[256]{0:T(256)S(1)}, s32[256]{0:T(256)}, u32[]{:S(2)}) copy-start(s32[256]{0:T(256)} %param.8) | copy-start | bytes 3076
  0.7 2.7 %copy-start.5 = (s32[256]{0:T(256)S(1)}, s32[256]{0:T(256)}, u32[]{:S(2)}) copy-start(s32[256]{0:T(256)} %param.9) | copy-start | bytes 3076
  2.3 1.0 copy-start.3
  5.0 26.8 %all-to-all-start = ((bf16[16,40,640]{2,1,0:T(8,128)(2,1)}), bf16[16,40,640]{2,1,0:T(8,128)(2,1)S(1)}, u32[]{:S(2)}, u32[]{:S(2)}) async-start(bf16[16,40,640]{2,1,0:T(8,128)(2,1)} %bitcast.65), calls=%async_computation | async-start | bytes 1638400 | tf_op jit(solution)/shard_map/all_to_all | solution.py:113
  26.7 2.8 %collective-permute-start.1 = (bf16[128,2048]{1,0:T(8,128)(2,1)S(1)}, bf16[128,2048]{1,0:T(8,128)(2,1)S(1)}, u32[]{:S(2)}, u32[]{:S(2)}) collective-permute-start(bf16[128,2048]{1,0:T(8,128)(2,1)S(1)} %select_convert_fusion), channel_id=1, source_target_pairs={{0,2},{2,0},{4,6},{6,4},{8,10},{10,8},{12,14},{14,12},{16,18},{18,... | collective-permute-start | bytes 1572872 | tf_op jit(solution)/shard_map/ppermute | solution.py:29
  31.8 18.8 %all-to-all-start.1 = ((bf16[16,40,384]{2,1,0:T(8,128)(2,1)}), bf16[16,40,384]{2,1,0:T(8,128)(2,1)S(1)}, u32[]{:S(2)}, u32[]{:S(2)}) async-start(bf16[16,40,384]{2,1,0:T(8,128)(2,1)} %bitcast.6), calls=%async_computation.1 | async-start | bytes 983040 | tf_op jit(solution)/shard_map/all_to_all | solution.py:113
  38.4 24.8 %collective-permute-start = (bf16[320,1280]{1,0:T(8,128)(2,1)S(1)}, bf16[320,1280]{1,0:T(8,128)(2,1)S(1)}, u32[]{:S(2)}, u32[]{:S(2)}) collective-permute-start(bf16[320,1280]{1,0:T(8,128)(2,1)S(1)} %pad_maximum_fusion.1), channel_id=1, source_target_pairs={{0,1},{1,0},{2,3},{3,2},{4,5},{5,4},{6,7},{7,6},{8,9},{9,8},{10,11... | collective-permute-start | bytes 2457608 | tf_op jit(solution)/shard_map/ppermute | solution.py:29
  51.2 8.0 %collective-permute-start.2 = (bf16[64,2048]{1,0:T(8,128)(2,1)S(1)}, bf16[64,2048]{1,0:T(8,128)(2,1)S(1)}, u32[]{:S(2)}, u32[]{:S(2)}) collective-permute-start(bf16[64,2048]{1,0:T(8,128)(2,1)S(1)} %select_convert_fusion.1), channel_id=1, source_target_pairs={{0,4},{2,6},{4,0},{6,2},{8,12},{10,14},{12,8},{14,10},{16,20},{18,... | collective-permute-start | bytes 786440 | tf_op jit(solution)/shard_map/ppermute | solution.py:29
  52.7 17.3 %collective-permute-start.3 = (bf16[320,768]{1,0:T(8,128)(2,1)S(1)}, bf16[320,768]{1,0:T(8,128)(2,1)S(1)}, u32[]{:S(2)}, u32[]{:S(2)}) collective-permute-start(bf16[320,768]{1,0:T(8,128)(2,1)S(1)} %pad_maximum_fusion.3), channel_id=1, source_target_pairs={{0,1},{1,0},{2,3},{3,2},{4,5},{5,4},{6,7},{7,6},{8,9},{9,8},{10,11... | collective-permute-start | bytes 1474568 | tf_op jit(solution)/shard_map/ppermute | solution.py:29
  59.3 5.0 %copy-start.7 = (f32[320,2560]{1,0:T(8,128)S(1)}, f32[320,2560]{1,0:T(8,128)}, u32[]{:S(2)}) copy-start(f32[320,2560]{1,0:T(8,128)} %fusion.8) | copy-start | bytes 9830404
  59.3 4.4 %collective-permute-start.4 = (bf16[32,2048]{1,0:T(8,128)(2,1)S(1)}, bf16[32,2048]{1,0:T(8,128)(2,1)S(1)}, u32[]{:S(2)}, u32[]{:S(2)}) collective-permute-start(bf16[32,2048]{1,0:T(8,128)(2,1)S(1)} %select_convert_fusion.2), channel_id=1, source_target_pairs={{0,8},{2,10},{4,12},{6,14},{8,0},{10,2},{12,4},{14,6},{16,24},{18,... | collective-permute-start | bytes 393224 | tf_op jit(solution)/shard_map/ppermute | solution.py:29
  63.7 6.3 %collective-permute-start.5 = (bf16[16,2048]{1,0:T(8,128)(2,1)S(1)}, bf16[16,2048]{1,0:T(8,128)(2,1)S(1)}, u32[]{:S(2)}, u32[]{:S(2)}) collective-permute-start(bf16[16,2048]{1,0:T(8,128)(2,1)S(1)} %select_convert_fusion.3), channel_id=1, source_target_pairs={{0,16},{2,18},{4,20},{6,22},{8,24},{10,26},{12,28},{14,30},{16,0},... | collective-permute-start | bytes 196616 | tf_op jit(solution)/shard_map/ppermute | solution.py:29
  69.6 1.9 %copy-start.2 = (f32[320,2560]{1,0:T(8,128)S(1)}, f32[320,2560]{1,0:T(8,128)}, u32[]{:S(2)}) copy-start(f32[320,2560]{1,0:T(8,128)} %fusion.34) | copy-start | bytes 9830404
  78.7 13.7 %collective-permute-start.8 = (bf16[320,768]{1,0:T(8,128)(2,1)S(1)}, bf16[320,768]{1,0:T(8,128)(2,1)S(1)}, u32[]{:S(2)}, u32[]{:S(2)}) collective-permute-start(bf16[320,768]{1,0:T(8,128)(2,1)S(1)} %fusion.42), channel_id=1, source_target_pairs={{0,1},{1,0},{2,3},{3,2},{4,5},{5,4},{6,7},{7,6},{8,9},{9,8},{10,11... | collective-permute-start | bytes 1474568 | tf_op jit(solution)/shard_map/ppermute | solution.py:29
  80.0 7.9 %collective-permute-start.6 = (bf16[16,2048]{1,0:T(8,128)(2,1)S(1)}, bf16[16,2048]{1,0:T(8,128)(2,1)S(1)}, u32[]{:S(2)}, u32[]{:S(2)}) collective-permute-start(bf16[16,2048]{1,0:T(8,128)(2,1)S(1)} %add_convert_fusion.3), channel_id=1, source_target_pairs={{0,16},{2,18},{4,20},{6,22},{8,24},{10,26},{12,28},{14,30},{16,0},... | collective-permute-start | bytes 196616 | tf_op jit(solution)/shard_map/ppermute | solution.py:29
  87.9 4.5 %collective-permute-start.7 = (bf16[32,2048]{1,0:T(8,128)(2,1)S(1)}, bf16[32,2048]{1,0:T(8,128)(2,1)S(1)}, u32[]{:S(2)}, u32[]{:S(2)}) collective-permute-start(bf16[32,2048]{1,0:T(8,128)(2,1)S(1)} %pad_maximum_fusion.5), channel_id=1, source_target_pairs={{0,8},{2,10},{4,12},{6,14},{8,0},{10,2},{12,4},{14,6},{16,24},{18,... | collective-permute-start | bytes 393224 | tf_op jit(solution)/shard_map/ppermute | solution.py:29
  94.5 9.1 %collective-permute-start.9 = (bf16[64,2048]{1,0:T(8,128)(2,1)S(1)}, bf16[64,2048]{1,0:T(8,128)(2,1)S(1)}, u32[]{:S(2)}, u32[]{:S(2)}) collective-permute-start(bf16[64,2048]{1,0:T(8,128)(2,1)S(1)} %pad_maximum_fusion.4), channel_id=1, source_target_pairs={{0,4},{2,6},{4,0},{6,2},{8,12},{10,14},{12,8},{14,10},{16,20},{18,... | collective-permute-start | bytes 786440 | tf_op jit(solution)/shard_map/ppermute | solution.py:29
  95.4 16.7 %collective-permute-start.10 = (bf16[320,1280]{1,0:T(8,128)(2,1)}, bf16[320,1280]{1,0:T(8,128)(2,1)S(1)}, u32[]{:S(2)}, u32[]{:S(2)}) collective-permute-start(bf16[320,1280]{1,0:T(8,128)(2,1)} %fusion.37), channel_id=1, source_target_pairs={{0,1},{1,0},{2,3},{3,2},{4,5},{5,4},{6,7},{7,6},{8,9},{9,8},{10,11... | collective-permute-start | bytes 2457608 | tf_op jit(solution)/shard_map/ppermute | solution.py:29
  95.7 21.4 %all-to-all-start.2 = ((bf16[16,40,384]{2,1,0:T(8,128)(2,1)}), bf16[16,40,384]{2,1,0:T(8,128)(2,1)}, u32[]{:S(2)}, u32[]{:S(2)}) async-start(bf16[16,40,384]{2,1,0:T(8,128)(2,1)} %bitcast.15), calls=%async_computation.2 | async-start | bytes 983040 | tf_op jit(solution)/shard_map/all_to_all | solution.py:113
  117.1 25.8 %all-to-all-start.3 = ((bf16[16,40,640]{2,1,0:T(8,128)(2,1)}), bf16[16,40,640]{2,1,0:T(8,128)(2,1)S(1)}, u32[]{:S(2)}, u32[]{:S(2)}) async-start(bf16[16,40,640]{2,1,0:T(8,128)(2,1)} %bitcast.17), calls=%async_computation.3 | async-start | bytes 1638400 | tf_op jit(solution)/shard_map/all_to_all | solution.py:113
  122.7 5.0 %collective-permute-start.11 = (bf16[128,2048]{1,0:T(8,128)(2,1)S(1)}, bf16[128,2048]{1,0:T(8,128)(2,1)S(1)}, u32[]{:S(2)}, u32[]{:S(2)}) collective-permute-start(bf16[128,2048]{1,0:T(8,128)(2,1)S(1)} %pad_maximum_fusion.2), channel_id=1, source_target_pairs={{0,2},{2,0},{4,6},{6,4},{8,10},{10,8},{12,14},{14,12},{16,18},{18,... | collective-permute-start | bytes 1572872 | tf_op jit(solution)/shard_map/ppermute | solution.py:29
  123.3 4.5 %copy-start.4 = (pred[640,512]{1,0:T(32,128)(4,1)}, pred[640,512]{1,0:T(32,128)(4,1)S(1)}, u32[]{:S(2)}) copy-start(pred[640,512]{1,0:T(32,128)(4,1)S(1)} %iota_compare_fusion) | copy-start | bytes 983044
  127.8 20.0 %copy-start.1 = (bf16[1,320,4096]{2,1,0:T(8,128)(2,1)S(1)}, bf16[1,320,4096]{2,1,0:T(8,128)(2,1)}, u32[]{:S(2)}) copy-start(bf16[1,320,4096]{2,1,0:T(8,128)(2,1)} %param.12) | copy-start | bytes 7864324

commit v4 on v3

--- a/solution.py
+++ b/solution.py
@@ -3,6 +3,8 @@
 import jax
 import jax.numpy as jnp
 from jax import lax
+from jax.experimental import pallas as pl
+from jax.experimental.pallas import tpu as pltpu
 from jax.sharding import PartitionSpec as P
 
 gelu_scale = math.sqrt(2.0 / math.pi)
@@ -75,6 +77,70 @@
 
 def dot(a, b):
     return jnp.dot(a, b, preferred_element_type=F32)
+
+
+def column_of(row):
+    return jnp.broadcast_to(row.astype(F32), (8, row.shape[1])).T[:, :1]
+
+
+def spread_tokens(gate, columns, grad_out, width, rows):
+    fold, tokens = columns.shape
+    part, steps = width // fold, 2 if rows % 32 == 0 else 1
+    block = rows // steps
+
+    def kernel(gate_ref, columns_ref, grad_ref, out):
+        scaled = (column_of(gate_ref[...]) * grad_ref[...].astype(F32)).astype(BF16)
+        number = lax.broadcasted_iota(jnp.int32, (block, tokens), 0) + pl.program_id(0) * block
+        total = None
+        for h in range(fold):
+            picked = jnp.where(number == columns_ref[h : h + 1, :], 1.0, 0.0).astype(BF16)
+            term = jnp.dot(picked, scaled[:, h * part : (h + 1) * part], preferred_element_type=F32)
+            total = term if total is None else total + term
+        out[...] = total.astype(BF16)
+
+    return pl.pallas_call(
+        kernel,
+        out_shape=jax.ShapeDtypeStruct((rows, part), BF16),
+        grid=(steps,),
+        in_specs=[
+            pl.BlockSpec((1, tokens), lambda i: (0, 0)),
+            pl.BlockSpec((fold, tokens), lambda i: (0, 0)),
+            pl.BlockSpec((tokens, width), lambda i: (0, 0)),
+        ],
+        out_specs=pl.BlockSpec((block, part), lambda i: (i, 0)),
+        compiler_params=pltpu.CompilerParams(vmem_limit_bytes=24 << 20),
+    )(gate.reshape(1, tokens), columns, grad_out)
+
+
+def gather_tokens(columns, block, tail):
+    fold, tokens = columns.shape
+    rows, part = block.shape
+    steps = 2 if tokens % 256 == 0 else 1
+    share = tokens // steps
+    width = fold * part
+
+    def kernel(columns_ref, block_ref, tail_ref, out):
+        for h in range(fold):
+            column = column_of(columns_ref[h : h + 1, :]).astype(jnp.int32)
+            number = lax.broadcasted_iota(jnp.int32, (share, rows), 1)
+            picked = jnp.where(number == column, 1.0, 0.0).astype(BF16)
+            out[:, h * part : (h + 1) * part] = jnp.dot(
+                picked, block_ref[...], preferred_element_type=F32
+            ).astype(BF16)
+        out[:, width:] = tail_ref[...]
+
+    return pl.pallas_call(
+        kernel,
+        out_shape=jax.ShapeDtypeStruct((tokens, width + tail.shape[1]), BF16),
+        grid=(steps,),
+        in_specs=[
+            pl.BlockSpec((fold, share), lambda i: (0, i)),
+            pl.BlockSpec((rows, part), lambda i: (0, 0)),
+            pl.BlockSpec((share, tail.shape[1]), lambda i: (i, 0)),
+        ],
+        out_specs=pl.BlockSpec((share, width + tail.shape[1]), lambda i: (i, 0)),
+        compiler_params=pltpu.CompilerParams(vmem_limit_bytes=24 << 20),
+    )(columns, block, tail)
 
 
 def chunk_widths(features, share):
@@ -121,9 +187,10 @@
     outgoing = []
     for start, width in zip(starts, widths):
         part = width // fold
-        stacked = jnp.concatenate(
-            [scaled[:, start + h * part : start + (h + 1) * part] for h in range(fold)], axis=0
-        )
+        tokens = after(grad_out, *outgoing) if pair and outgoing else grad_out
+        tokens = tokens[:, start : start + width].astype(F32)
+        scaled = (gate[:, None] * tokens).astype(BF16)
+        stacked = jnp.concatenate([scaled[:, h * part : (h + 1) * part] for h in range(fold)], axis=0)
         outgoing.append(dot(table, stacked).astype(BF16))
 
     dense = Summed(dense_partial[0], "expert")
@@ -187,12 +254,16 @@
         if last is not None:
             folded = after(folded, last)
         last = all_to_all(folded)
+        if pair and not i and len(order) > 1:
+            grad_in = gather_tokens(columns.reshape(fold, tok_count), last, outs[1])
+            break
         outs[i] = jnp.concatenate(
             [tn_dot(table[:, h * tok_count : (h + 1) * tok_count], last).astype(BF16) for h in range(fold)],
             axis=1,
         )
-    dense_sum = dense.rest()
-    return (jnp.concatenate([outs[i] for i in sorted(order)], axis=1), dense_sum)
+    else:
+        grad_in = jnp.concatenate([outs[i] for i in sorted(order)], axis=1)
+    return (grad_in, dense.rest())
 
 
 def solution(mesh):

time: 149 us -> 147 us (0.987)
  matrix products: 67.6 us -> 63.5 us
  other arithmetic: 10.2 us -> 13.4 us
  waiting for transfers between devices: 29.7 us -> 27.3 us
  Pallas kernels: 0 us -> 2.01 us
    dot_general x8 -> x6, matrix products: 9.36 us -> 5.23 us  [tn_dot(): lax.dot_general(a, b, (((0,), (0,)), ((), ())), preferred_element_type=F32)]
    select_n x4, other arithmetic: 0.15 us -> 2.28 us  [double(): jnp.where(upper, other, mine)]
    pallas_call x0 -> x1, Pallas kernels: none -> 2.01 us  [gather_tokens(): pl.pallas_call(kernel, out_shape=jax.ShapeDtypeStruct((tokens, width + ta...]
    ppermute x12, waiting for transfers between devices: 9.09 us -> 7.37 us  [xor_send(): return lax.ppermute(value, axis, [(i, i ^ bit) for i in range(size)])]
  transfers between devices with their start and end apart: 16 -> 16, of which waited for: 7 -> 7; matrix products, arithmetic and copies ran while one was open for 42% -> 44% of each run, Pallas kernels for 0% -> 0%
where the time goes in v4:
time: 147 us; the launch traced here: 146 us
  matrix products  63.5 us (43%)
  starting transfers between devices  35.7 us (24%)
  waiting for transfers between devices  27.3 us (19%)
  other arithmetic  13.4 us (9%)
  local copies, waits for them, and re-layouts  2.55 us (2%)
  Pallas kernels  2.01 us (1%)
    dot_general x8, matrix products, nt_dot(): return lax.dot_general(a, b, NT, preferred_element_type=F32)  37.9 us
    all_to_all x4, starting transfers between devices, all_to_all(): lax.all_to_all(block, 'expert', split_axis=0, concat_axis=0, tiled=True)  25.5 us
    dot_general x7, matrix products, dot(): return jnp.dot(a, b, preferred_element_type=F32)  20.4 us
    all_to_all x4, waiting for transfers between devices, all_to_all(): lax.all_to_all(block, 'expert', split_axis=0, concat_axis=0, tiled=True)  20 us
    ppermute x12, starting transfers between devices, xor_send(): return lax.ppermute(value, axis, [(i, i ^ bit) for i in range(size)])  10.3 us
    ppermute x12, waiting for transfers between devices, xor_send(): return lax.ppermute(value, axis, [(i, i ^ bit) for i in range(size)])  7.37 us
    dot_general x6, matrix products, tn_dot(): lax.dot_general(a, b, (((0,), (0,)), ((), ())), preferred_element_type=F32)  5.23 us
  transfers between devices with their start and end apart: 16, of which 7 were waited for; matrix products, arithmetic and copies ran while one was open for 44% of the time, Pallas kernels for 0%

profile of v4, /device:TPU:9, one launch (start us, length us, event | category | flops | bytes accessed | tf_op | source)
XLA Modules:
  0.0 145.5 jit_solution(12880584530160975513)
XLA Ops:
  0.6 1.4 multiply_convert_fusion
  2.8 1.6 %convolution_convert_fusion = bf16[640,640]{1,0:T(8,128)(2,1)} fusion(bf16[256,640]{1,0:T(8,128)(2,1)S(1)} %get-tuple-element.33, bf16[256,640]{1,0:T(8,128)(2,1)S(1)} %get-tuple-element.32, s32[512]{0:T(512)S(1)} %pad_add_fusion), kind=kOutput, calls=%fused_computation.40 | convolution fusion | flops 421478400 | bytes 1476608 | tf_op jit(solution)/shard_map/dot_general | solution.py:79
  4.4 6.6 %all-to-all-start = ((bf16[16,40,640]{2,1,0:T(8,128)(2,1)}), bf16[16,40,640]{2,1,0:T(8,128)(2,1)S(1)}, u32[]{:S(2)}, u32[]{:S(2)}) async-start(bf16[16,40,640]{2,1,0:T(8,128)(2,1)} %bitcast.64), calls=%async_computation | async-start | bytes 1638400 | tf_op jit(solution)/shard_map/all_to_all | solution.py:179
  11.0 13.5 %fusion.34 = f32[320,2560]{1,0:T(8,128)} fusion(bf16[1,4096,2560]{2,1,0:T(8,128)(2,1)} %param.13, bf16[1,320,4096]{2,1,0:T(8,128)(2,1)S(1)} %copy-done), kind=kOutput, calls=%fused_computation.35 | convolution fusion | flops 6724812800 | bytes 26869760 | tf_op jit(solution)/shard_map/dot_general | solution.py:79
  24.5 1.6 %select_convert_fusion = bf16[128,2048]{1,0:T(8,128)(2,1)S(1)} fusion(f32[256,2048]{1,0:T(8,128)} %bitcast.60, pred[]{:T(512)S(6)} %ne.101), kind=kLoop, calls=%fused_computation.55 | loop fusion | flops 262144 | bytes 1572865 | tf_op jit(solution)/shard_map/convert_element_type | solution.py:39
  27.8 1.3 convolution_convert_fusion.1
  29.1 1.7 %convert_add_fusion = f32[128,2048]{1,0:T(8,128)S(1)} fusion(bf16[128,2048]{1,0:T(8,128)(2,1)S(1)} %collective-permute-done.1, f32[256,2048]{1,0:T(8,128)} %bitcast.61, pred[]{:T(512)S(6)} %ne.101), kind=kLoop, calls=%fused_computation.54 | loop fusion | flops 786432 | bytes 3670017 | tf_op jit(solution)/shard_map/add | solution.py:39
  31.2 5.4 %all-to-all-start.1 = ((bf16[16,40,384]{2,1,0:T(8,128)(2,1)}), bf16[16,40,384]{2,1,0:T(8,128)(2,1)S(1)}, u32[]{:S(2)}, u32[]{:S(2)}) async-start(bf16[16,40,384]{2,1,0:T(8,128)(2,1)} %bitcast.6), calls=%async_computation.1 | async-start | bytes 983040 | tf_op jit(solution)/shard_map/all_to_all | solution.py:179
  37.9 1.3 collective-permute-start
  39.2 6.9 %fusion.8 = f32[320,2560]{1,0:T(8,128)} fusion(bf16[1,2560,4096]{2,1,0:T(8,128)(2,1)} %param.14, s32[]{:T(128)S(6)} %select_n.172, bf16[320,640]{1,0:T(8,128)(2,1)S(1)} %convolution_convert_fusion.2, bf16[320,640]{1,0:T(8,128)(2,1)S(1)} %convolution_convert_fusion.3), kind=kOutput, calls=%fused_computation.8 | convolution fusion | flops 2098790400 | bytes 10649604 | tf_op jit(solution)/shard_map/dot_general | solution.py:182
  46.1 4.0 %all-to-all-done.1 = bf16[16,40,384]{2,1,0:T(8,128)(2,1)S(1)} async-done(((bf16[16,40,384]{2,1,0:T(8,128)(2,1)}), bf16[16,40,384]{2,1,0:T(8,128)(2,1)S(1)}, u32[]{:S(2)}, u32[]{:S(2)}) %all-to-all-start.1) | async-done | bytes 491552 | tf_op jit(solution)/shard_map/all_to_all | solution.py:179
  52.3 1.3 collective-permute-start.3
  53.6 5.2 %collective-permute-done.2 = bf16[64,2048]{1,0:T(8,128)(2,1)S(1)} collective-permute-done((bf16[64,2048]{1,0:T(8,128)(2,1)S(1)}, bf16[64,2048]{1,0:T(8,128)(2,1)S(1)}, u32[]{:S(2)}, u32[]{:S(2)}) %collective-permute-start.2) | collective-permute-done | bytes 262176 | tf_op jit(solution)/shard_map/ppermute | solution.py:31
  59.0 3.8 %fusion.24 = f32[320,2560]{1,0:T(8,128)S(1)} fusion(bf16[1,2560,4096]{2,1,0:T(8,128)(2,1)} %param.14, s32[]{:T(128)S(6)} %select_n.180, bf16[320,384]{1,0:T(8,128)(2,1)S(1)} %convolution_convert_fusion.4, bf16[320,384]{1,0:T(8,128)(2,1)S(1)} %convolution_convert_fusion.5), kind=kOutput, calls=%fused_computation.25 | convolution fusion | flops 1259274240 | bytes 7700484 | tf_op jit(solution)/shard_map/dot_general | solution.py:182
  63.9 5.2 %fusion.14 = f32[320,2560]{1,0:T(8,128)S(1)} fusion(f32[320,2560]{1,0:T(8,128)S(1)} %copy-done.5, bf16[320,1280]{1,0:T(8,128)(2,1)S(1)} %collective-permute-done, bf16[1,2560,4096]{2,1,0:T(8,128)(2,1)} %param.14, s32[]{:T(128)S(6)} %select_n.179), kind=kOutput, calls=%fused_computation.16 | convolution fusion | flops 2097971200 | bytes 13926404 | tf_op jit(solution)/shard_map/dot_general | solution.py:182
  69.6 1.4 copy-done.3
  71.0 3.6 %fusion.18 = bf16[320,2560]{1,0:T(8,128)(2,1)S(1)} fusion(f32[320,2560]{1,0:T(8,128)S(1)} %copy-done.3, f32[320,2560]{1,0:T(8,128)S(1)} %add.181, bf16[320,768]{1,0:T(8,128)(2,1)S(1)} %collective-permute-done.3, bf16[1,2560,4096]{2,1,0:T(8,128)(2,1)} %param.14, s32[]{:T(128)S(6)} %select_n.181), kind=kOutput, calls=%fused_computation.19 | convolution fusion | flops 1260748800 | bytes 12615684 | tf_op jit(solution)/shard_map/dot_general | solution.py:182
  74.7 3.6 %fusion.42 = bf16[320,768]{1,0:T(8,128)(2,1)S(1)} fusion(bf16[320,2560]{1,0:T(8,128)(2,1)S(1)} %fusion.18, bf16[1,4096,2560]{2,1,0:T(8,128)(2,1)} %param.13, s32[]{:T(128)S(6)} %select_n.181), kind=kOutput, calls=%fused_computation.46 | convolution fusion | flops 1258536960 | bytes 6062084 | tf_op jit(solution)/shard_map/dot_general | solution.py:182
  79.5 1.8 %collective-permute-start.6 = (bf16[16,2048]{1,0:T(8,128)(2,1)S(1)}, bf16[16,2048]{1,0:T(8,128)(2,1)S(1)}, u32[]{:S(2)}, u32[]{:S(2)}) collective-permute-start(bf16[16,2048]{1,0:T(8,128)(2,1)S(1)} %add_convert_fusion.3), channel_id=1, source_target_pairs={{0,16},{2,18},{4,20},{6,22},{8,24},{10,26},{12,28},{14,30},{16,0},... | collective-permute-start | bytes 196616 | tf_op jit(solution)/shard_map/ppermute | solution.py:31
  81.4 6.1 %fusion.37 = bf16[320,1280]{1,0:T(8,128)(2,1)} fusion(bf16[320,2560]{1,0:T(8,128)(2,1)S(1)} %fusion.18, bf16[1,4096,2560]{2,1,0:T(8,128)(2,1)} %param.13, s32[]{:T(128)S(6)} %select_n.179), kind=kOutput, calls=%fused_computation.36 | convolution fusion | flops 2097561600 | bytes 9011204 | tf_op jit(solution)/shard_map/dot_general | solution.py:182
  88.3 3.6 %fusion.19 = f32[320,768]{1,0:T(8,128)S(1)} fusion(bf16[320,2560]{1,0:T(8,128)(2,1)S(1)} %fusion.18, bf16[1,4096,2560]{2,1,0:T(8,128)(2,1)} %param.13, s32[]{:T(128)S(6)} %select_n.180), kind=kOutput, calls=%fused_computation.20 | convolution fusion | flops 1258291200 | bytes 6553604 | tf_op jit(solution)/shard_map/dot_general | solution.py:182
  95.2 7.8 %all-to-all-start.2 = ((bf16[16,40,384]{2,1,0:T(8,128)(2,1)}), bf16[16,40,384]{2,1,0:T(8,128)(2,1)}, u32[]{:S(2)}, u32[]{:S(2)}) async-start(bf16[16,40,384]{2,1,0:T(8,128)(2,1)} %bitcast.15), calls=%async_computation.2 | async-start | bytes 983040 | tf_op jit(solution)/shard_map/all_to_all | solution.py:179
  104.9 5.2 %fusion.2 = f32[320,1280]{1,0:T(8,128)S(1)} fusion(bf16[320,2560]{1,0:T(8,128)(2,1)S(1)} %fusion.18, bf16[1,4096,2560]{2,1,0:T(8,128)(2,1)} %param.13, s32[]{:T(128)S(6)} %select_n.172), kind=kOutput, calls=%fused_computation.2 | convolution fusion | flops 2097152000 | bytes 9830404 | tf_op jit(solution)/shard_map/dot_general | solution.py:182
  110.1 1.7 %collective-permute-done.10 = bf16[320,1280]{1,0:T(8,128)(2,1)S(1)} collective-permute-done((bf16[320,1280]{1,0:T(8,128)(2,1)}, bf16[320,1280]{1,0:T(8,128)(2,1)S(1)}, u32[]{:S(2)}, u32[]{:S(2)}) %collective-permute-start.10) | collective-permute-done | bytes 819232 | tf_op jit(solution)/shard_map/ppermute | solution.py:31
  112.6 1.5 %add_convert_fusion = bf16[640,640]{1,0:T(8,128)(2,1)} fusion(f32[640,640]{1,0:T(8,128)S(1)} %fusion.45, s32[320]{0:T(512)S(1)} %get-tuple-element.45, bf16[320,1280]{1,0:T(8,128)(2,1)S(1)} %add_convert_fusion.1), kind=kOutput, calls=%fused_computation.38 | convolution fusion | flops 263168000 | bytes 2869248 | tf_op jit(solution)/shard_map/dot_general | solution.py:79
  114.1 2.6 %all-to-all-done.2 = bf16[16,40,384]{2,1,0:T(8,128)(2,1)} async-done(((bf16[16,40,384]{2,1,0:T(8,128)(2,1)}), bf16[16,40,384]{2,1,0:T(8,128)(2,1)}, u32[]{:S(2)}, u32[]{:S(2)}) %all-to-all-start.2) | async-done | bytes 491552 | tf_op jit(solution)/shard_map/all_to_all | solution.py:179
  116.7 5.6 %all-to-all-start.3 = ((bf16[16,40,640]{2,1,0:T(8,128)(2,1)}), bf16[16,40,640]{2,1,0:T(8,128)(2,1)S(1)}, u32[]{:S(2)}, u32[]{:S(2)}) async-start(bf16[16,40,640]{2,1,0:T(8,128)(2,1)} %bitcast.17), calls=%async_computation.3 | async-start | bytes 1638400 | tf_op jit(solution)/shard_map/all_to_all | solution.py:179
  122.9 1.5 %convolution_convert_fusion.6 = bf16[256,384]{1,0:T(8,128)(2,1)S(1)} fusion(bf16[640,384]{1,0:T(8,128)(2,1)} %bitcast.16, pred[640,512]{1,0:T(32,128)(4,1)S(1)} %iota_compare_fusion), kind=kOutput, calls=%fused_computation.51 | convolution fusion | flops 125927424 | bytes 851968 | tf_op jit(solution)/shard_map/dot_general | solution.py:185
  124.4 1.5 %convolution_convert_fusion.7 = bf16[256,384]{1,0:T(8,128)(2,1)S(1)} fusion(bf16[640,384]{1,0:T(8,128)(2,1)} %bitcast.16, pred[640,512]{1,0:T(32,128)(4,1)S(1)} %iota_compare_fusion), kind=kOutput, calls=%fused_computation.52 | convolution fusion | flops 125927424 | bytes 851968 | tf_op jit(solution)/shard_map/dot_general | solution.py:185
  128.0 1.6 %maximum_convert_fusion = f32[256,2048]{1,0:T(8,128)} fusion(bf16[128,2048]{1,0:T(8,128)(2,1)S(1)} %get-tuple-element.31, bf16[128,2048]{1,0:T(8,128)(2,1)S(1)} %get-tuple-element.30), kind=kLoop, calls=%fused_computation.53 | loop fusion | flops 2097152 | bytes 3145728 | tf_op jit(solution)/shard_map/convert_element_type | solution.py:71
  129.5 13.0 %all-to-all-done.3 = bf16[16,40,640]{2,1,0:T(8,128)(2,1)S(1)} async-done(((bf16[16,40,640]{2,1,0:T(8,128)(2,1)}), bf16[16,40,640]{2,1,0:T(8,128)(2,1)S(1)}, u32[]{:S(2)}, u32[]{:S(2)}) %all-to-all-start.3) | async-done | bytes 819232 | tf_op jit(solution)/shard_map/all_to_all | solution.py:179
  143.5 2.0 %shard_map.95 = bf16[256,2048]{1,0:T(8,128)(2,1)} custom-call(s32[2,256]{1,0:T(2,128)S(1)} %reshape.64.columns_ref, bf16[640,640]{1,0:T(8,128)(2,1)S(1)} %bitcast.59, bf16[256,768]{1,0:T(8,128)(2,1)S(1)} %copy-done.2), custom_call_target="tpu_custom_call" | custom-call | tf_op jit(solution)/shard_map/pallas_call | solution.py:132
  (65 shorter events, 19.7 us)
Async XLA Ops:
  0.6 10.4 %copy-start = (bf16[1,320,4096]{2,1,0:T(8,128)(2,1)S(1)}, bf16[1,320,4096]{2,1,0:T(8,128)(2,1)}, u32[]{:S(2)}) copy-start(bf16[1,320,4096]{2,1,0:T(8,128)(2,1)} %param.12) | copy-start | bytes 7864324
  4.4 26.8 %all-to-all-start = ((bf16[16,40,640]{2,1,0:T(8,128)(2,1)}), bf16[16,40,640]{2,1,0:T(8,128)(2,1)S(1)}, u32[]{:S(2)}, u32[]{:S(2)}) async-start(bf16[16,40,640]{2,1,0:T(8,128)(2,1)} %bitcast.64), calls=%async_computation | async-start | bytes 1638400 | tf_op jit(solution)/shard_map/all_to_all | solution.py:179
  11.0 15.6 %copy-start.4 = (f32[256]{0:T(256)S(1)}, f32[256]{0:T(256)}, u32[]{:S(2)}) copy-start(f32[256]{0:T(256)} %param.10) | copy-start | bytes 3076
  26.2 2.9 %collective-permute-start.1 = (bf16[128,2048]{1,0:T(8,128)(2,1)S(1)}, bf16[128,2048]{1,0:T(8,128)(2,1)S(1)}, u32[]{:S(2)}, u32[]{:S(2)}) collective-permute-start(bf16[128,2048]{1,0:T(8,128)(2,1)S(1)} %select_convert_fusion), channel_id=1, source_target_pairs={{0,2},{2,0},{4,6},{6,4},{8,10},{10,8},{12,14},{14,12},{16,18},{18,... | collective-permute-start | bytes 1572872 | tf_op jit(solution)/shard_map/ppermute | solution.py:31
  31.2 18.9 %all-to-all-start.1 = ((bf16[16,40,384]{2,1,0:T(8,128)(2,1)}), bf16[16,40,384]{2,1,0:T(8,128)(2,1)S(1)}, u32[]{:S(2)}, u32[]{:S(2)}) async-start(bf16[16,40,384]{2,1,0:T(8,128)(2,1)} %bitcast.6), calls=%async_computation.1 | async-start | bytes 983040 | tf_op jit(solution)/shard_map/all_to_all | solution.py:179
  37.9 24.8 %collective-permute-start = (bf16[320,1280]{1,0:T(8,128)(2,1)S(1)}, bf16[320,1280]{1,0:T(8,128)(2,1)S(1)}, u32[]{:S(2)}, u32[]{:S(2)}) collective-permute-start(bf16[320,1280]{1,0:T(8,128)(2,1)S(1)} %pad_maximum_fusion), channel_id=1, source_target_pairs={{0,1},{1,0},{2,3},{3,2},{4,5},{5,4},{6,7},{7,6},{8,9},{9,8},{10,11... | collective-permute-start | bytes 2457608 | tf_op jit(solution)/shard_map/ppermute | solution.py:31
  50.7 8.0 %collective-permute-start.2 = (bf16[64,2048]{1,0:T(8,128)(2,1)S(1)}, bf16[64,2048]{1,0:T(8,128)(2,1)S(1)}, u32[]{:S(2)}, u32[]{:S(2)}) collective-permute-start(bf16[64,2048]{1,0:T(8,128)(2,1)S(1)} %select_convert_fusion.1), channel_id=1, source_target_pairs={{0,4},{2,6},{4,0},{6,2},{8,12},{10,14},{12,8},{14,10},{16,20},{18,... | collective-permute-start | bytes 786440 | tf_op jit(solution)/shard_map/ppermute | solution.py:31
  52.3 17.3 %collective-permute-start.3 = (bf16[320,768]{1,0:T(8,128)(2,1)S(1)}, bf16[320,768]{1,0:T(8,128)(2,1)S(1)}, u32[]{:S(2)}, u32[]{:S(2)}) collective-permute-start(bf16[320,768]{1,0:T(8,128)(2,1)S(1)} %pad_maximum_fusion.2), channel_id=1, source_target_pairs={{0,1},{1,0},{2,3},{3,2},{4,5},{5,4},{6,7},{7,6},{8,9},{9,8},{10,11... | collective-permute-start | bytes 1474568 | tf_op jit(solution)/shard_map/ppermute | solution.py:31
  58.9 5.0 %copy-start.5 = (f32[320,2560]{1,0:T(8,128)S(1)}, f32[320,2560]{1,0:T(8,128)}, u32[]{:S(2)}) copy-start(f32[320,2560]{1,0:T(8,128)} %fusion.8) | copy-start | bytes 9830404
  58.9 4.4 %collective-permute-start.4 = (bf16[32,2048]{1,0:T(8,128)(2,1)S(1)}, bf16[32,2048]{1,0:T(8,128)(2,1)S(1)}, u32[]{:S(2)}, u32[]{:S(2)}) collective-permute-start(bf16[32,2048]{1,0:T(8,128)(2,1)S(1)} %select_convert_fusion.2), channel_id=1, source_target_pairs={{0,8},{2,10},{4,12},{6,14},{8,0},{10,2},{12,4},{14,6},{16,24},{18,... | collective-permute-start | bytes 393224 | tf_op jit(solution)/shard_map/ppermute | solution.py:31
  63.3 6.3 %collective-permute-start.5 = (bf16[16,2048]{1,0:T(8,128)(2,1)S(1)}, bf16[16,2048]{1,0:T(8,128)(2,1)S(1)}, u32[]{:S(2)}, u32[]{:S(2)}) collective-permute-start(bf16[16,2048]{1,0:T(8,128)(2,1)S(1)} %select_convert_fusion.3), channel_id=1, source_target_pairs={{0,16},{2,18},{4,20},{6,22},{8,24},{10,26},{12,28},{14,30},{16,0},... | collective-permute-start | bytes 196616 | tf_op jit(solution)/shard_map/ppermute | solution.py:31
  69.1 1.9 %copy-start.3 = (f32[320,2560]{1,0:T(8,128)S(1)}, f32[320,2560]{1,0:T(8,128)}, u32[]{:S(2)}) copy-start(f32[320,2560]{1,0:T(8,128)} %fusion.34) | copy-start | bytes 9830404
  78.3 13.7 %collective-permute-start.8 = (bf16[320,768]{1,0:T(8,128)(2,1)S(1)}, bf16[320,768]{1,0:T(8,128)(2,1)S(1)}, u32[]{:S(2)}, u32[]{:S(2)}) collective-permute-start(bf16[320,768]{1,0:T(8,128)(2,1)S(1)} %fusion.42), channel_id=1, source_target_pairs={{0,1},{1,0},{2,3},{3,2},{4,5},{5,4},{6,7},{7,6},{8,9},{9,8},{10,11... | collective-permute-start | bytes 1474568 | tf_op jit(solution)/shard_map/ppermute | solution.py:31
  79.5 7.9 %collective-permute-start.6 = (bf16[16,2048]{1,0:T(8,128)(2,1)S(1)}, bf16[16,2048]{1,0:T(8,128)(2,1)S(1)}, u32[]{:S(2)}, u32[]{:S(2)}) collective-permute-start(bf16[16,2048]{1,0:T(8,128)(2,1)S(1)} %add_convert_fusion.3), channel_id=1, source_target_pairs={{0,16},{2,18},{4,20},{6,22},{8,24},{10,26},{12,28},{14,30},{16,0},... | collective-permute-start | bytes 196616 | tf_op jit(solution)/shard_map/ppermute | solution.py:31
  87.5 4.5 %collective-permute-start.7 = (bf16[32,2048]{1,0:T(8,128)(2,1)S(1)}, bf16[32,2048]{1,0:T(8,128)(2,1)S(1)}, u32[]{:S(2)}, u32[]{:S(2)}) collective-permute-start(bf16[32,2048]{1,0:T(8,128)(2,1)S(1)} %pad_maximum_fusion.5), channel_id=1, source_target_pairs={{0,8},{2,10},{4,12},{6,14},{8,0},{10,2},{12,4},{14,6},{16,24},{18,... | collective-permute-start | bytes 393224 | tf_op jit(solution)/shard_map/ppermute | solution.py:31
  94.0 9.1 %collective-permute-start.9 = (bf16[64,2048]{1,0:T(8,128)(2,1)S(1)}, bf16[64,2048]{1,0:T(8,128)(2,1)}, u32[]{:S(2)}, u32[]{:S(2)}) collective-permute-start(bf16[64,2048]{1,0:T(8,128)(2,1)S(1)} %pad_maximum_fusion.4), channel_id=1, source_target_pairs={{0,4},{2,6},{4,0},{6,2},{8,12},{10,14},{12,8},{14,10},{16,20},{18,... | collective-permute-start | bytes 786440 | tf_op jit(solution)/shard_map/ppermute | solution.py:31
  95.0 16.7 %collective-permute-start.10 = (bf16[320,1280]{1,0:T(8,128)(2,1)}, bf16[320,1280]{1,0:T(8,128)(2,1)S(1)}, u32[]{:S(2)}, u32[]{:S(2)}) collective-permute-start(bf16[320,1280]{1,0:T(8,128)(2,1)} %fusion.37), channel_id=1, source_target_pairs={{0,1},{1,0},{2,3},{3,2},{4,5},{5,4},{6,7},{7,6},{8,9},{9,8},{10,11... | collective-permute-start | bytes 2457608 | tf_op jit(solution)/shard_map/ppermute | solution.py:31
  95.2 21.4 %all-to-all-start.2 = ((bf16[16,40,384]{2,1,0:T(8,128)(2,1)}), bf16[16,40,384]{2,1,0:T(8,128)(2,1)}, u32[]{:S(2)}, u32[]{:S(2)}) async-start(bf16[16,40,384]{2,1,0:T(8,128)(2,1)} %bitcast.15), calls=%async_computation.2 | async-start | bytes 983040 | tf_op jit(solution)/shard_map/all_to_all | solution.py:179
  116.7 25.8 %all-to-all-start.3 = ((bf16[16,40,640]{2,1,0:T(8,128)(2,1)}), bf16[16,40,640]{2,1,0:T(8,128)(2,1)S(1)}, u32[]{:S(2)}, u32[]{:S(2)}) async-start(bf16[16,40,640]{2,1,0:T(8,128)(2,1)} %bitcast.17), calls=%async_computation.3 | async-start | bytes 1638400 | tf_op jit(solution)/shard_map/all_to_all | solution.py:179
  122.5 4.2 %collective-permute-start.11 = (bf16[128,2048]{1,0:T(8,128)(2,1)}, bf16[128,2048]{1,0:T(8,128)(2,1)S(1)}, u32[]{:S(2)}, u32[]{:S(2)}) collective-permute-start(bf16[128,2048]{1,0:T(8,128)(2,1)} %pad_maximum_fusion.1), channel_id=1, source_target_pairs={{0,2},{2,0},{4,6},{6,4},{8,10},{10,8},{12,14},{14,12},{16,18},{18,... | collective-permute-start | bytes 1572872 | tf_op jit(solution)/shard_map/ppermute | solution.py:31
  125.9 19.6 %copy-start.1 = (bf16[1,320,4096]{2,1,0:T(8,128)(2,1)S(1)}, bf16[1,320,4096]{2,1,0:T(8,128)(2,1)}, u32[]{:S(2)}) copy-start(bf16[1,320,4096]{2,1,0:T(8,128)(2,1)} %param.12) | copy-start | bytes 7864324
  142.5 1.0 copy-start.2

commit v5 on v4

--- a/solution.py
+++ b/solution.py
@@ -195,18 +195,22 @@
 
     dense = Summed(dense_partial[0], "expert")
     saved = saved_inputs[0]
-    slopes = lax.optimization_barrier(slope_of(dot(saved, w_in[0])))
+    slopes = lax.optimization_barrier(slope_of(dot(saved, w_in[0])).astype(BF16))
     arrived = [all_to_all(outgoing[0])]
     for block in outgoing[1:]:
         arrived.append(all_to_all(after(block, arrived[-1], slopes)))
-    mine = [jnp.concatenate([tn_dot(t, block).astype(BF16) for t in spread], axis=1) for block in arrived]
+
+    def unfolded(block):
+        return jnp.concatenate([tn_dot(t, block).astype(BF16) for t in spread], axis=1)
+
+    mine = [unfolded(block) for block in arrived]
 
     def up_share(who, i, x):
         w = lax.dynamic_slice_in_dim(w_out[0], who * features + starts[i], widths[i], 1)
         return nt_dot(x, w)
 
     if pair:
-        theirs = [xor_send(own, "mp", 1) for own in mine]
+        theirs = [unfolded(xor_send(block, "mp", 1)) for block in arrived]
         upstream = lax.optimization_barrier(up_share(me, 0, mine[0]))
         dense.step(slopes)
         for i in range(1, len(widths)):
@@ -216,7 +220,7 @@
         upstream = upstream + up_share(1 - me, len(widths) - 1, theirs[-1])
     else:
         upstream = nt_dot(lax.all_gather(mine[0], "mp", axis=1, tiled=True), w_out[0])
-    hidden = lax.optimization_barrier((upstream * slopes).astype(BF16))
+    hidden = lax.optimization_barrier((upstream * slopes.astype(F32)).astype(BF16))
 
     widths = chunk_widths(features, 0.625) if pair else [features]
     starts = [sum(widths[:i]) for i in range(len(widths))]

time: 147 us -> 143 us (0.973)
  starting transfers between devices: 35.7 us -> 37.5 us
  matrix products: 63.5 us -> 61.8 us
  other arithmetic: 13.4 us -> 11.9 us
    dot_general x8, matrix products: 37.9 us -> 31.9 us  [nt_dot(): return lax.dot_general(a, b, NT, preferred_element_type=F32)]
    dot_general x6 -> x10, matrix products: 5.23 us -> 9.88 us  [tn_dot(): lax.dot_general(a, b, (((0,), (0,)), ((), ())), preferred_element_type=F32)]
    all_to_all x4, waiting for transfers between devices: 20 us -> 18.2 us  [all_to_all(): lax.all_to_all(block, 'expert', split_axis=0, concat_axis=0, tiled=True)]
  transfers between devices with their start and end apart: 16 -> 16, of which waited for: 7 -> 6; matrix products, arithmetic and copies ran while one was open for 44% -> 43% of each run, Pallas kernels for 0% -> 0%
where the time goes in v5:
time: 143 us; the launch traced here: 142 us
  matrix products  61.8 us (43%)
  starting transfers between devices  37.5 us (26%)
  waiting for transfers between devices  26.7 us (19%)
  other arithmetic  11.9 us (8%)
  Pallas kernels  2.02 us (1%)
    dot_general x8, matrix products, nt_dot(): return lax.dot_general(a, b, NT, preferred_element_type=F32)  31.9 us
    all_to_all x4, starting transfers between devices, all_to_all(): lax.all_to_all(block, 'expert', split_axis=0, concat_axis=0, tiled=True)  26 us
    dot_general x7, matrix products, dot(): return jnp.dot(a, b, preferred_element_type=F32)  20 us
    all_to_all x4, waiting for transfers between devices, all_to_all(): lax.all_to_all(block, 'expert', split_axis=0, concat_axis=0, tiled=True)  18.2 us
    ppermute x12, starting transfers between devices, xor_send(): return lax.ppermute(value, axis, [(i, i ^ bit) for i in range(size)])  11.5 us
    dot_general x10, matrix products, tn_dot(): lax.dot_general(a, b, (((0,), (0,)), ((), ())), preferred_element_type=F32)  9.88 us
    ppermute x12, waiting for transfers between devices, xor_send(): return lax.ppermute(value, axis, [(i, i ^ bit) for i in range(size)])  8.46 us
  transfers between devices with their start and end apart: 16, of which 6 were waited for; matrix products, arithmetic and copies ran while one was open for 43% of the time, Pallas kernels for 0%

profile of v5, /device:TPU:9, one launch (start us, length us, event | category | flops | bytes accessed | tf_op | source)
XLA Modules:
  0.0 142.2 jit_solution(3559685619990953976)
XLA Ops:
  0.6 1.4 multiply_convert_fusion
  2.8 1.6 %convolution_convert_fusion = bf16[640,640]{1,0:T(8,128)(2,1)} fusion(bf16[256,640]{1,0:T(8,128)(2,1)S(1)} %get-tuple-element.33, bf16[256,640]{1,0:T(8,128)(2,1)S(1)} %get-tuple-element.32, s32[512]{0:T(512)S(1)} %pad_add_fusion), kind=kOutput, calls=%fused_computation.41 | convolution fusion | flops 421478400 | bytes 1476608 | tf_op jit(solution)/shard_map/dot_general | solution.py:79
  4.4 6.6 %all-to-all-start = ((bf16[16,40,640]{2,1,0:T(8,128)(2,1)}), bf16[16,40,640]{2,1,0:T(8,128)(2,1)S(1)}, u32[]{:S(2)}, u32[]{:S(2)}) async-start(bf16[16,40,640]{2,1,0:T(8,128)(2,1)} %bitcast.68), calls=%async_computation | async-start | bytes 1638400 | tf_op jit(solution)/shard_map/all_to_all | solution.py:179
  11.0 13.3 %fusion.34 = bf16[320,2560]{1,0:T(8,128)(2,1)} fusion(bf16[1,4096,2560]{2,1,0:T(8,128)(2,1)} %param.13, bf16[1,320,4096]{2,1,0:T(8,128)(2,1)S(1)} %copy-done), kind=kOutput, calls=%fused_computation.36 | convolution fusion | flops 6725632000 | bytes 25231360 | tf_op jit(solution)/shard_map/dot_general | solution.py:79
  24.4 1.6 %select_convert_fusion = bf16[128,2048]{1,0:T(8,128)(2,1)S(1)} fusion(f32[256,2048]{1,0:T(8,128)} %bitcast.63, pred[]{:T(512)S(6)} %ne.117), kind=kLoop, calls=%fused_computation.60 | loop fusion | flops 262144 | bytes 1572865 | tf_op jit(solution)/shard_map/convert_element_type | solution.py:39
  27.6 1.3 convolution_convert_fusion.1
  29.0 1.7 %convert_add_fusion = f32[128,2048]{1,0:T(8,128)S(1)} fusion(bf16[128,2048]{1,0:T(8,128)(2,1)S(1)} %collective-permute-done.1, f32[256,2048]{1,0:T(8,128)} %bitcast.64, pred[]{:T(512)S(6)} %ne.117), kind=kLoop, calls=%fused_computation.59 | loop fusion | flops 786432 | bytes 3670017 | tf_op jit(solution)/shard_map/add | solution.py:39
  32.5 5.6 %all-to-all-start.1 = ((bf16[16,40,384]{2,1,0:T(8,128)(2,1)}), bf16[16,40,384]{2,1,0:T(8,128)(2,1)}, u32[]{:S(2)}, u32[]{:S(2)}) async-start(bf16[16,40,384]{2,1,0:T(8,128)(2,1)} %bitcast.6), calls=%async_computation.1 | async-start | bytes 983040 | tf_op jit(solution)/shard_map/all_to_all | solution.py:179
  39.3 6.8 %fusion.8 = f32[320,2560]{1,0:T(8,128)} fusion(bf16[1,2560,4096]{2,1,0:T(8,128)(2,1)} %param.14, s32[]{:T(128)S(6)} %select_n.188, bf16[320,640]{1,0:T(8,128)(2,1)S(1)} %convolution_convert_fusion.4, bf16[320,640]{1,0:T(8,128)(2,1)S(1)} %convolution_convert_fusion.5), kind=kOutput, calls=%fused_computation.8 | convolution fusion | flops 2098790400 | bytes 10649604 | tf_op jit(solution)/shard_map/dot_general | solution.py:182
  46.1 5.2 %collective-permute-done = bf16[640,640]{1,0:T(8,128)(2,1)S(1)} collective-permute-done((bf16[640,640]{1,0:T(8,128)(2,1)S(1)}, bf16[640,640]{1,0:T(8,128)(2,1)S(1)}, u32[]{:S(2)}, u32[]{:S(2)}) %collective-permute-start) | collective-permute-done | bytes 819232 | tf_op jit(solution)/shard_map/ppermute | solution.py:31
  53.3 1.8 %convolution_convert_fusion.8 = bf16[320,384]{1,0:T(8,128)(2,1)S(1)} fusion(bf16[640,384]{1,0:T(8,128)(2,1)} %bitcast.7, s32[320]{0:T(512)S(1)} %get-tuple-element.44), kind=kOutput, calls=%fused_computation.54 | convolution fusion | flops 157614080 | bytes 738560 | tf_op jit(solution)/shard_map/dot_general | solution.py:185
  56.4 1.6 %convolution_convert_fusion.9 = bf16[320,384]{1,0:T(8,128)(2,1)S(1)} fusion(bf16[640,384]{1,0:T(8,128)(2,1)} %bitcast.7, s32[320]{0:T(512)S(1)} %get-tuple-element.45), kind=kOutput, calls=%fused_computation.55 | convolution fusion | flops 157614080 | bytes 738560 | tf_op jit(solution)/shard_map/dot_general | solution.py:185
  58.0 2.0 %collective-permute-done.2 = bf16[64,2048]{1,0:T(8,128)(2,1)S(1)} collective-permute-done((bf16[64,2048]{1,0:T(8,128)(2,1)S(1)}, bf16[64,2048]{1,0:T(8,128)(2,1)S(1)}, u32[]{:S(2)}, u32[]{:S(2)}) %collective-permute-start.2) | collective-permute-done | bytes 262176 | tf_op jit(solution)/shard_map/ppermute | solution.py:31
  60.2 5.3 %fusion.14 = f32[320,2560]{1,0:T(8,128)S(1)} fusion(f32[320,2560]{1,0:T(8,128)S(1)} %copy-done.6, bf16[320,1280]{1,0:T(8,128)(2,1)S(1)} %pad_maximum_fusion, bf16[1,2560,4096]{2,1,0:T(8,128)(2,1)} %param.14, s32[]{:T(128)S(6)} %select_n.195), kind=kOutput, calls=%fused_computation.16 | convolution fusion | flops 2097971200 | bytes 13926404 | tf_op jit(solution)/shard_map/dot_general | solution.py:182
  66.6 3.8 %convolution_add_fusion.1 = f32[320,2560]{1,0:T(8,128)S(1)} fusion(f32[320,2560]{1,0:T(8,128)S(1)} %fusion.14, bf16[1,2560,4096]{2,1,0:T(8,128)(2,1)} %param.14, s32[]{:T(128)S(6)} %select_n.196, bf16[320,384]{1,0:T(8,128)(2,1)S(1)} %convolution_convert_fusion.8, bf16[320,384]{1,0:T(8,128)(2,1)S(1)} %convolution_convert_fusion.9), kind=kOutput, calls=%fused_computation.19 | convolution fusion | flops 1260093440 | bytes 10977284 | tf_op jit(solution)/shard_map/dot_general | solution.py:182
  71.5 3.9 %fusion.18 = bf16[320,2560]{1,0:T(8,128)(2,1)S(1)} fusion(f32[320,2560]{1,0:T(8,128)S(1)} %convolution_add_fusion.1, bf16[1,2560,4096]{2,1,0:T(8,128)(2,1)} %param.14, s32[]{:T(128)S(6)} %select_n.197, bf16[320,2560]{1,0:T(8,128)(2,1)S(1)} %copy-done.4, bf16[320,384]{1,0:T(8,128)(2,1)S(1)} %convolution_convert_fusion.6, ...), kind=kOutput, calls=%fused_computation.20 | convolution fusion | flops 1262551040 | bytes 10977284 | tf_op jit(solution)/shard_map/dot_general | solution.py:182
  75.5 1.5 %fusion.42 = bf16[320,768]{1,0:T(8,128)(2,1)S(1)} fusion(bf16[320,2560]{1,0:T(8,128)(2,1)S(1)} %fusion.18, bf16[1,4096,2560]{2,1,0:T(8,128)(2,1)S(1)} %bitcast.70, s32[]{:T(128)S(6)} %select_n.197), kind=kOutput, calls=%fused_computation.47 | convolution fusion | flops 1258536960 | bytes 6062084 | tf_op jit(solution)/shard_map/dot_general | solution.py:182
  78.2 1.5 %collective-permute-start.6 = (bf16[16,2048]{1,0:T(8,128)(2,1)S(1)}, bf16[16,2048]{1,0:T(8,128)(2,1)S(1)}, u32[]{:S(2)}, u32[]{:S(2)}) collective-permute-start(bf16[16,2048]{1,0:T(8,128)(2,1)S(1)} %add_convert_fusion.3), channel_id=1, source_target_pairs={{0,16},{2,18},{4,20},{6,22},{8,24},{10,26},{12,28},{14,30},{16,0},... | collective-permute-start | bytes 196616 | tf_op jit(solution)/shard_map/ppermute | solution.py:31
  79.7 3.4 %fusion.37 = bf16[320,1280]{1,0:T(8,128)(2,1)} fusion(bf16[320,2560]{1,0:T(8,128)(2,1)S(1)} %fusion.18, bf16[1,4096,2560]{2,1,0:T(8,128)(2,1)S(1)} %bitcast.70, s32[]{:T(128)S(6)} %select_n.195), kind=kOutput, calls=%fused_computation.37 | convolution fusion | flops 2097561600 | bytes 9011204 | tf_op jit(solution)/shard_map/dot_general | solution.py:182
  83.2 1.5 %collective-permute-start.7 = (bf16[32,2048]{1,0:T(8,128)(2,1)S(1)}, bf16[32,2048]{1,0:T(8,128)(2,1)S(1)}, u32[]{:S(2)}, u32[]{:S(2)}) collective-permute-start(bf16[32,2048]{1,0:T(8,128)(2,1)S(1)} %pad_maximum_fusion.4), channel_id=1, source_target_pairs={{0,8},{2,10},{4,12},{6,14},{8,0},{10,2},{12,4},{14,6},{16,24},{18,... | collective-permute-start | bytes 393224 | tf_op jit(solution)/shard_map/ppermute | solution.py:31
  84.7 1.5 %fusion.19 = f32[320,768]{1,0:T(8,128)S(1)} fusion(bf16[320,2560]{1,0:T(8,128)(2,1)S(1)} %fusion.18, bf16[1,4096,2560]{2,1,0:T(8,128)(2,1)S(1)} %bitcast.70, s32[]{:T(128)S(6)} %select_n.196), kind=kOutput, calls=%fused_computation.21 | convolution fusion | flops 1258291200 | bytes 6553604 | tf_op jit(solution)/shard_map/dot_general | solution.py:182
  86.2 1.3 collective-permute-done.7
  91.6 9.4 %all-to-all-start.2 = ((bf16[16,40,384]{2,1,0:T(8,128)(2,1)}), bf16[16,40,384]{2,1,0:T(8,128)(2,1)}, u32[]{:S(2)}, u32[]{:S(2)}) async-start(bf16[16,40,384]{2,1,0:T(8,128)(2,1)} %bitcast.15), calls=%async_computation.2 | async-start | bytes 983040 | tf_op jit(solution)/shard_map/all_to_all | solution.py:179
  101.9 5.7 %fusion.2 = f32[320,1280]{1,0:T(8,128)S(1)} fusion(bf16[320,2560]{1,0:T(8,128)(2,1)} %copy-done.5, bf16[1,4096,2560]{2,1,0:T(8,128)(2,1)} %param.13, s32[]{:T(128)S(6)} %select_n.188), kind=kOutput, calls=%fused_computation.2 | convolution fusion | flops 2097152000 | bytes 9830404 | tf_op jit(solution)/shard_map/dot_general | solution.py:182
  108.4 1.5 %add_convert_fusion = bf16[640,640]{1,0:T(8,128)(2,1)} fusion(f32[640,640]{1,0:T(8,128)S(1)} %fusion.45, s32[320]{0:T(512)S(1)} %get-tuple-element.45, bf16[320,1280]{1,0:T(8,128)(2,1)S(1)} %add_convert_fusion.1), kind=kOutput, calls=%fused_computation.39 | convolution fusion | flops 263168000 | bytes 2869248 | tf_op jit(solution)/shard_map/dot_general | solution.py:79
  109.9 4.7 %all-to-all-done.2 = bf16[16,40,384]{2,1,0:T(8,128)(2,1)} async-done(((bf16[16,40,384]{2,1,0:T(8,128)(2,1)}), bf16[16,40,384]{2,1,0:T(8,128)(2,1)}, u32[]{:S(2)}, u32[]{:S(2)}) %all-to-all-start.2) | async-done | bytes 491552 | tf_op jit(solution)/shard_map/all_to_all | solution.py:179
  114.6 4.4 %all-to-all-start.3 = ((bf16[16,40,640]{2,1,0:T(8,128)(2,1)}), bf16[16,40,640]{2,1,0:T(8,128)(2,1)S(1)}, u32[]{:S(2)}, u32[]{:S(2)}) async-start(bf16[16,40,640]{2,1,0:T(8,128)(2,1)} %bitcast.17), calls=%async_computation.3 | async-start | bytes 1638400 | tf_op jit(solution)/shard_map/all_to_all | solution.py:179
  119.6 1.5 %convolution_convert_fusion.10 = bf16[256,384]{1,0:T(8,128)(2,1)S(1)} fusion(bf16[640,384]{1,0:T(8,128)(2,1)} %bitcast.16, pred[640,512]{1,0:T(32,128)(4,1)S(1)} %iota_compare_fusion), kind=kOutput, calls=%fused_computation.56 | convolution fusion | flops 125927424 | bytes 851968 | tf_op jit(solution)/shard_map/dot_general | solution.py:185
  121.1 1.5 %convolution_convert_fusion.11 = bf16[256,384]{1,0:T(8,128)(2,1)S(1)} fusion(bf16[640,384]{1,0:T(8,128)(2,1)} %bitcast.16, pred[640,512]{1,0:T(32,128)(4,1)S(1)} %iota_compare_fusion), kind=kOutput, calls=%fused_computation.57 | convolution fusion | flops 125927424 | bytes 851968 | tf_op jit(solution)/shard_map/dot_general | solution.py:185
  124.7 1.6 %maximum_convert_fusion = f32[256,2048]{1,0:T(8,128)} fusion(bf16[128,2048]{1,0:T(8,128)(2,1)S(1)} %get-tuple-element.31, bf16[128,2048]{1,0:T(8,128)(2,1)S(1)} %get-tuple-element.30), kind=kLoop, calls=%fused_computation.58 | loop fusion | flops 2097152 | bytes 3145728 | tf_op jit(solution)/shard_map/convert_element_type | solution.py:71
  126.2 13.0 %all-to-all-done.3 = bf16[16,40,640]{2,1,0:T(8,128)(2,1)S(1)} async-done(((bf16[16,40,640]{2,1,0:T(8,128)(2,1)}), bf16[16,40,640]{2,1,0:T(8,128)(2,1)S(1)}, u32[]{:S(2)}, u32[]{:S(2)}) %all-to-all-start.3) | async-done | bytes 819232 | tf_op jit(solution)/shard_map/all_to_all | solution.py:179
  140.2 2.0 %shard_map.95 = bf16[256,2048]{1,0:T(8,128)(2,1)} custom-call(s32[2,256]{1,0:T(2,128)S(1)} %reshape.64.columns_ref, bf16[640,640]{1,0:T(8,128)(2,1)S(1)} %bitcast.62, bf16[256,768]{1,0:T(8,128)(2,1)S(1)} %copy-done.2), custom_call_target="tpu_custom_call" | custom-call | tf_op jit(solution)/shard_map/pallas_call | solution.py:132
  (80 shorter events, 21.6 us)
Async XLA Ops:
  0.6 10.4 %copy-start = (bf16[1,320,4096]{2,1,0:T(8,128)(2,1)S(1)}, bf16[1,320,4096]{2,1,0:T(8,128)(2,1)}, u32[]{:S(2)}) copy-start(bf16[1,320,4096]{2,1,0:T(8,128)(2,1)} %param.12) | copy-start | bytes 7864324
  4.4 26.8 %all-to-all-start = ((bf16[16,40,640]{2,1,0:T(8,128)(2,1)}), bf16[16,40,640]{2,1,0:T(8,128)(2,1)S(1)}, u32[]{:S(2)}, u32[]{:S(2)}) async-start(bf16[16,40,640]{2,1,0:T(8,128)(2,1)} %bitcast.68), calls=%async_computation | async-start | bytes 1638400 | tf_op jit(solution)/shard_map/all_to_all | solution.py:179
  11.0 15.4 %copy-start.3 = (f32[256]{0:T(256)S(1)}, f32[256]{0:T(256)}, u32[]{:S(2)}) copy-start(f32[256]{0:T(256)} %param.10) | copy-start | bytes 3076
  26.0 2.9 %collective-permute-start.1 = (bf16[128,2048]{1,0:T(8,128)(2,1)S(1)}, bf16[128,2048]{1,0:T(8,128)(2,1)S(1)}, u32[]{:S(2)}, u32[]{:S(2)}) collective-permute-start(bf16[128,2048]{1,0:T(8,128)(2,1)S(1)} %select_convert_fusion), channel_id=1, source_target_pairs={{0,2},{2,0},{4,6},{6,4},{8,10},{10,8},{12,14},{14,12},{16,18},{18,... | collective-permute-start | bytes 1572872 | tf_op jit(solution)/shard_map/ppermute | solution.py:31
  31.2 20.1 %collective-permute-start = (bf16[640,640]{1,0:T(8,128)(2,1)S(1)}, bf16[640,640]{1,0:T(8,128)(2,1)S(1)}, u32[]{:S(2)}, u32[]{:S(2)}) collective-permute-start(bf16[640,640]{1,0:T(8,128)(2,1)S(1)} %bitcast.65), channel_id=1, source_target_pairs={{0,1},{1,0},{2,3},{3,2},{4,5},{5,4},{6,7},{7,6},{8,9},{9,8},{10,11... | collective-permute-start | bytes 2457608 | tf_op jit(solution)/shard_map/ppermute | solution.py:31
  32.5 20.1 %all-to-all-start.1 = ((bf16[16,40,384]{2,1,0:T(8,128)(2,1)}), bf16[16,40,384]{2,1,0:T(8,128)(2,1)}, u32[]{:S(2)}, u32[]{:S(2)}) async-start(bf16[16,40,384]{2,1,0:T(8,128)(2,1)} %bitcast.6), calls=%async_computation.1 | async-start | bytes 983040 | tf_op jit(solution)/shard_map/all_to_all | solution.py:179
  52.6 7.6 %copy-start.6 = (f32[320,2560]{1,0:T(8,128)S(1)}, f32[320,2560]{1,0:T(8,128)}, u32[]{:S(2)}) copy-start(f32[320,2560]{1,0:T(8,128)} %fusion.8) | copy-start | bytes 9830404
  52.6 7.3 %collective-permute-start.2 = (bf16[64,2048]{1,0:T(8,128)(2,1)S(1)}, bf16[64,2048]{1,0:T(8,128)(2,1)S(1)}, u32[]{:S(2)}, u32[]{:S(2)}) collective-permute-start(bf16[64,2048]{1,0:T(8,128)(2,1)S(1)} %select_convert_fusion.1), channel_id=1, source_target_pairs={{0,4},{2,6},{4,0},{6,2},{8,12},{10,14},{12,8},{14,10},{16,20},{18,... | collective-permute-start | bytes 786440 | tf_op jit(solution)/shard_map/ppermute | solution.py:31
  55.1 15.3 %collective-permute-start.3 = (bf16[640,384]{1,0:T(8,128)(2,1)}, bf16[640,384]{1,0:T(8,128)(2,1)S(1)}, u32[]{:S(2)}, u32[]{:S(2)}) collective-permute-start(bf16[640,384]{1,0:T(8,128)(2,1)} %bitcast.7), channel_id=1, source_target_pairs={{0,1},{1,0},{2,3},{3,2},{4,5},{5,4},{6,7},{7,6},{8,9},{9,8},{10,11... | collective-permute-start | bytes 1474568 | tf_op jit(solution)/shard_map/ppermute | solution.py:31
  60.1 5.5 %collective-permute-start.4 = (bf16[32,2048]{1,0:T(8,128)(2,1)S(1)}, bf16[32,2048]{1,0:T(8,128)(2,1)S(1)}, u32[]{:S(2)}, u32[]{:S(2)}) collective-permute-start(bf16[32,2048]{1,0:T(8,128)(2,1)S(1)} %select_convert_fusion.2), channel_id=1, source_target_pairs={{0,8},{2,10},{4,12},{6,14},{8,0},{10,2},{12,4},{14,6},{16,24},{18,... | collective-permute-start | bytes 393224 | tf_op jit(solution)/shard_map/ppermute | solution.py:31
  60.2 15.3 %slice-start = ((s8[20971520]{0:T(1024)(128)(4,1)}), s8[4194304]{0:T(1024)(128)(4,1)S(1)}, s32[]{:S(2)}) async-start(s8[20971520]{0:T(1024)(128)(4,1)} %bitcast.69), calls=%async_computation.4 | async-start | bytes 8388608
  60.2 15.3 %slice-start.1 = ((s8[20971520]{0:T(1024)(128)(4,1)}), s8[4194304]{0:T(1024)(128)(4,1)S(1)}, s32[]{:S(2)}) async-start(s8[20971520]{0:T(1024)(128)(4,1)} %bitcast.69), calls=%async_computation.5 | async-start | bytes 8388608
  60.2 15.3 %slice-start.2 = ((s8[20971520]{0:T(1024)(128)(4,1)}), s8[4194304]{0:T(1024)(128)(4,1)S(1)}, s32[]{:S(2)}) async-start(s8[20971520]{0:T(1024)(128)(4,1)} %bitcast.69), calls=%async_computation.6 | async-start | bytes 8388608
  65.6 5.8 %copy-start.4 = (bf16[320,2560]{1,0:T(8,128)(2,1)S(1)}, bf16[320,2560]{1,0:T(8,128)(2,1)}, u32[]{:S(2)}) copy-start(bf16[320,2560]{1,0:T(8,128)(2,1)} %fusion.34) | copy-start | bytes 4915204
  65.7 9.8 %slice-start.3 = ((s8[20971520]{0:T(1024)(128)(4,1)}), s8[4194304]{0:T(1024)(128)(4,1)S(1)}, s32[]{:S(2)}) async-start(s8[20971520]{0:T(1024)(128)(4,1)} %bitcast.69), calls=%async_computation.7 | async-start | bytes 8388608
  65.7 4.7 %collective-permute-start.5 = (bf16[16,2048]{1,0:T(8,128)(2,1)S(1)}, bf16[16,2048]{1,0:T(8,128)(2,1)S(1)}, u32[]{:S(2)}, u32[]{:S(2)}) collective-permute-start(bf16[16,2048]{1,0:T(8,128)(2,1)S(1)} %select_convert_fusion.3), channel_id=1, source_target_pairs={{0,16},{2,18},{4,20},{6,22},{8,24},{10,26},{12,28},{14,30},{16,0},... | collective-permute-start | bytes 196616 | tf_op jit(solution)/shard_map/ppermute | solution.py:31
  71.5 4.0 %slice-start.4 = ((s8[20971520]{0:T(1024)(128)(4,1)}), s8[4194304]{0:T(1024)(128)(4,1)S(1)}, s32[]{:S(2)}) async-start(s8[20971520]{0:T(1024)(128)(4,1)} %bitcast.69), calls=%async_computation.8 | async-start | bytes 8388608
  75.5 9.2 %copy-start.5 = (bf16[320,2560]{1,0:T(8,128)(2,1)}, bf16[320,2560]{1,0:T(8,128)(2,1)S(1)}, u32[]{:S(2)}) copy-start(bf16[320,2560]{1,0:T(8,128)(2,1)S(1)} %fusion.18) | copy-start | bytes 4915204
  77.0 10.5 %collective-permute-start.8 = (bf16[320,768]{1,0:T(8,128)(2,1)S(1)}, bf16[320,768]{1,0:T(8,128)(2,1)S(1)}, u32[]{:S(2)}, u32[]{:S(2)}) collective-permute-start(bf16[320,768]{1,0:T(8,128)(2,1)S(1)} %fusion.42), channel_id=1, source_target_pairs={{0,1},{1,0},{2,3},{3,2},{4,5},{5,4},{6,7},{7,6},{8,9},{9,8},{10,11... | collective-permute-start | bytes 1474568 | tf_op jit(solution)/shard_map/ppermute | solution.py:31
  78.2 4.9 %collective-permute-start.6 = (bf16[16,2048]{1,0:T(8,128)(2,1)S(1)}, bf16[16,2048]{1,0:T(8,128)(2,1)S(1)}, u32[]{:S(2)}, u32[]{:S(2)}) collective-permute-start(bf16[16,2048]{1,0:T(8,128)(2,1)S(1)} %add_convert_fusion.3), channel_id=1, source_target_pairs={{0,16},{2,18},{4,20},{6,22},{8,24},{10,26},{12,28},{14,30},{16,0},... | collective-permute-start | bytes 196616 | tf_op jit(solution)/shard_map/ppermute | solution.py:31
  83.2 4.3 %collective-permute-start.7 = (bf16[32,2048]{1,0:T(8,128)(2,1)S(1)}, bf16[32,2048]{1,0:T(8,128)(2,1)S(1)}, u32[]{:S(2)}, u32[]{:S(2)}) collective-permute-start(bf16[32,2048]{1,0:T(8,128)(2,1)S(1)} %pad_maximum_fusion.4), channel_id=1, source_target_pairs={{0,8},{2,10},{4,12},{6,14},{8,0},{10,2},{12,4},{14,6},{16,24},{18,... | collective-permute-start | bytes 393224 | tf_op jit(solution)/shard_map/ppermute | solution.py:31
  89.3 11.8 %collective-permute-start.9 = (bf16[64,2048]{1,0:T(8,128)(2,1)S(1)}, bf16[64,2048]{1,0:T(8,128)(2,1)S(1)}, u32[]{:S(2)}, u32[]{:S(2)}) collective-permute-start(bf16[64,2048]{1,0:T(8,128)(2,1)S(1)} %pad_maximum_fusion.3), channel_id=1, source_target_pairs={{0,4},{2,6},{4,0},{6,2},{8,12},{10,14},{12,8},{14,10},{16,20},{18,... | collective-permute-start | bytes 786440 | tf_op jit(solution)/shard_map/ppermute | solution.py:31
  90.4 17.2 %collective-permute-start.10 = (bf16[320,1280]{1,0:T(8,128)(2,1)}, bf16[320,1280]{1,0:T(8,128)(2,1)S(1)}, u32[]{:S(2)}, u32[]{:S(2)}) collective-permute-start(bf16[320,1280]{1,0:T(8,128)(2,1)} %fusion.37), channel_id=1, source_target_pairs={{0,1},{1,0},{2,3},{3,2},{4,5},{5,4},{6,7},{7,6},{8,9},{9,8},{10,11... | collective-permute-start | bytes 2457608 | tf_op jit(solution)/shard_map/ppermute | solution.py:31
  91.6 23.0 %all-to-all-start.2 = ((bf16[16,40,384]{2,1,0:T(8,128)(2,1)}), bf16[16,40,384]{2,1,0:T(8,128)(2,1)}, u32[]{:S(2)}, u32[]{:S(2)}) async-start(bf16[16,40,384]{2,1,0:T(8,128)(2,1)} %bitcast.15), calls=%async_computation.2 | async-start | bytes 983040 | tf_op jit(solution)/shard_map/all_to_all | solution.py:179
  114.6 24.6 %all-to-all-start.3 = ((bf16[16,40,640]{2,1,0:T(8,128)(2,1)}), bf16[16,40,640]{2,1,0:T(8,128)(2,1)S(1)}, u32[]{:S(2)}, u32[]{:S(2)}) async-start(bf16[16,40,640]{2,1,0:T(8,128)(2,1)} %bitcast.17), calls=%async_computation.3 | async-start | bytes 1638400 | tf_op jit(solution)/shard_map/all_to_all | solution.py:179
  119.2 4.3 %collective-permute-start.11 = (bf16[128,2048]{1,0:T(8,128)(2,1)}, bf16[128,2048]{1,0:T(8,128)(2,1)S(1)}, u32[]{:S(2)}, u32[]{:S(2)}) collective-permute-start(bf16[128,2048]{1,0:T(8,128)(2,1)} %pad_maximum_fusion.1), channel_id=1, source_target_pairs={{0,2},{2,0},{4,6},{6,4},{8,10},{10,8},{12,14},{14,12},{16,18},{18,... | collective-permute-start | bytes 1572872 | tf_op jit(solution)/shard_map/ppermute | solution.py:31
  122.6 19.6 %copy-start.1 = (bf16[1,320,4096]{2,1,0:T(8,128)(2,1)S(1)}, bf16[1,320,4096]{2,1,0:T(8,128)(2,1)}, u32[]{:S(2)}) copy-start(bf16[1,320,4096]{2,1,0:T(8,128)(2,1)} %param.12) | copy-start | bytes 7864324
  139.2 1.0 copy-start.2

commit v6 on v5

--- a/solution.py
+++ b/solution.py
@@ -195,7 +195,7 @@
 
     dense = Summed(dense_partial[0], "expert")
     saved = saved_inputs[0]
-    slopes = lax.optimization_barrier(slope_of(dot(saved, w_in[0])).astype(BF16))
+    slopes = lax.optimization_barrier(slope_of(dot(saved, w_in[0])))
     arrived = [all_to_all(outgoing[0])]
     for block in outgoing[1:]:
         arrived.append(all_to_all(after(block, arrived[-1], slopes)))
@@ -220,7 +220,7 @@
         upstream = upstream + up_share(1 - me, len(widths) - 1, theirs[-1])
     else:
         upstream = nt_dot(lax.all_gather(mine[0], "mp", axis=1, tiled=True), w_out[0])
-    hidden = lax.optimization_barrier((upstream * slopes.astype(F32)).astype(BF16))
+    hidden = lax.optimization_barrier((upstream * slopes).astype(BF16))
 
     widths = chunk_widths(features, 0.625) if pair else [features]
     starts = [sum(widths[:i]) for i in range(len(widths))]

time: 143 us -> 143 us (level)
  transfers between devices with their start and end apart: 16 -> 16, of which waited for: 6 -> 7; matrix products, arithmetic and copies ran while one was open for 43% -> 44% of each run, Pallas kernels for 0% -> 0%
where the time goes in v6:
time: 143 us; the launch traced here: 142 us
  matrix products  61.4 us (43%)
  starting transfers between devices  37.9 us (27%)
  waiting for transfers between devices  25.9 us (18%)
  other arithmetic  12.9 us (9%)
  Pallas kernels  2.02 us (1%)
    dot_general x8, matrix products, nt_dot(): return lax.dot_general(a, b, NT, preferred_element_type=F32)  31.4 us
    all_to_all x4, starting transfers between devices, all_to_all(): lax.all_to_all(block, 'expert', split_axis=0, concat_axis=0, tiled=True)  26.1 us
    dot_general x7, matrix products, dot(): return jnp.dot(a, b, preferred_element_type=F32)  20.1 us
    all_to_all x4, waiting for transfers between devices, all_to_all(): lax.all_to_all(block, 'expert', split_axis=0, concat_axis=0, tiled=True)  17.6 us
    ppermute x12, starting transfers between devices, xor_send(): return lax.ppermute(value, axis, [(i, i ^ bit) for i in range(size)])  11.8 us
    dot_general x10, matrix products, tn_dot(): lax.dot_general(a, b, (((0,), (0,)), ((), ())), preferred_element_type=F32)  9.86 us
    ppermute x12, waiting for transfers between devices, xor_send(): return lax.ppermute(value, axis, [(i, i ^ bit) for i in range(size)])  8.27 us
  transfers between devices with their start and end apart: 16, of which 7 were waited for; matrix products, arithmetic and copies ran while one was open for 44% of the time, Pallas kernels for 0%

profile of v6, /device:TPU:9, one launch (start us, length us, event | category | flops | bytes accessed | tf_op | source)
XLA Modules:
  0.0 142.4 jit_solution(10696480017747432777)
XLA Ops:
  0.6 1.4 multiply_convert_fusion
  2.8 1.6 %convolution_convert_fusion = bf16[640,640]{1,0:T(8,128)(2,1)} fusion(bf16[256,640]{1,0:T(8,128)(2,1)S(1)} %get-tuple-element.33, bf16[256,640]{1,0:T(8,128)(2,1)S(1)} %get-tuple-element.32, s32[512]{0:T(512)S(1)} %pad_add_fusion), kind=kOutput, calls=%fused_computation.40 | convolution fusion | flops 421478400 | bytes 1476608 | tf_op jit(solution)/shard_map/dot_general | solution.py:79
  4.4 6.6 %all-to-all-start = ((bf16[16,40,640]{2,1,0:T(8,128)(2,1)}), bf16[16,40,640]{2,1,0:T(8,128)(2,1)S(1)}, u32[]{:S(2)}, u32[]{:S(2)}) async-start(bf16[16,40,640]{2,1,0:T(8,128)(2,1)} %bitcast.68), calls=%async_computation | async-start | bytes 1638400 | tf_op jit(solution)/shard_map/all_to_all | solution.py:179
  11.0 13.5 %fusion.33 = f32[320,2560]{1,0:T(8,128)} fusion(bf16[1,4096,2560]{2,1,0:T(8,128)(2,1)} %param.13, bf16[1,320,4096]{2,1,0:T(8,128)(2,1)S(1)} %copy-done), kind=kOutput, calls=%fused_computation.35 | convolution fusion | flops 6724812800 | bytes 26869760 | tf_op jit(solution)/shard_map/dot_general | solution.py:79
  24.5 1.6 %select_convert_fusion = bf16[128,2048]{1,0:T(8,128)(2,1)S(1)} fusion(f32[256,2048]{1,0:T(8,128)} %bitcast.63, pred[]{:T(512)S(6)} %ne.117), kind=kLoop, calls=%fused_computation.59 | loop fusion | flops 262144 | bytes 1572865 | tf_op jit(solution)/shard_map/convert_element_type | solution.py:39
  27.8 1.3 convolution_convert_fusion.1
  29.1 1.7 %convert_add_fusion = f32[128,2048]{1,0:T(8,128)S(1)} fusion(bf16[128,2048]{1,0:T(8,128)(2,1)S(1)} %collective-permute-done.1, f32[256,2048]{1,0:T(8,128)} %bitcast.64, pred[]{:T(512)S(6)} %ne.117), kind=kLoop, calls=%fused_computation.58 | loop fusion | flops 786432 | bytes 3670017 | tf_op jit(solution)/shard_map/add | solution.py:39
  32.5 5.8 %all-to-all-start.1 = ((bf16[16,40,384]{2,1,0:T(8,128)(2,1)}), bf16[16,40,384]{2,1,0:T(8,128)(2,1)}, u32[]{:S(2)}, u32[]{:S(2)}) async-start(bf16[16,40,384]{2,1,0:T(8,128)(2,1)} %bitcast.6), calls=%async_computation.1 | async-start | bytes 983040 | tf_op jit(solution)/shard_map/all_to_all | solution.py:179
  39.4 6.9 %fusion.8 = f32[320,2560]{1,0:T(8,128)} fusion(bf16[1,2560,4096]{2,1,0:T(8,128)(2,1)} %param.14, s32[]{:T(128)S(6)} %select_n.188, bf16[320,640]{1,0:T(8,128)(2,1)S(1)} %convolution_convert_fusion.4, bf16[320,640]{1,0:T(8,128)(2,1)S(1)} %convolution_convert_fusion.5), kind=kOutput, calls=%fused_computation.8 | convolution fusion | flops 2098790400 | bytes 10649604 | tf_op jit(solution)/shard_map/dot_general | solution.py:182
  46.3 4.9 %collective-permute-done = bf16[640,640]{1,0:T(8,128)(2,1)S(1)} collective-permute-done((bf16[640,640]{1,0:T(8,128)(2,1)S(1)}, bf16[640,640]{1,0:T(8,128)(2,1)S(1)}, u32[]{:S(2)}, u32[]{:S(2)}) %collective-permute-start) | collective-permute-done | bytes 819232 | tf_op jit(solution)/shard_map/ppermute | solution.py:31
  53.3 1.8 %convolution_convert_fusion.8 = bf16[320,384]{1,0:T(8,128)(2,1)S(1)} fusion(bf16[640,384]{1,0:T(8,128)(2,1)} %bitcast.7, s32[320]{0:T(512)S(1)} %get-tuple-element.44), kind=kOutput, calls=%fused_computation.53 | convolution fusion | flops 157614080 | bytes 738560 | tf_op jit(solution)/shard_map/dot_general | solution.py:185
  56.4 1.6 %convolution_convert_fusion.9 = bf16[320,384]{1,0:T(8,128)(2,1)S(1)} fusion(bf16[640,384]{1,0:T(8,128)(2,1)} %bitcast.7, s32[320]{0:T(512)S(1)} %get-tuple-element.45), kind=kOutput, calls=%fused_computation.54 | convolution fusion | flops 157614080 | bytes 738560 | tf_op jit(solution)/shard_map/dot_general | solution.py:185
  58.0 1.9 %collective-permute-done.2 = bf16[64,2048]{1,0:T(8,128)(2,1)S(1)} collective-permute-done((bf16[64,2048]{1,0:T(8,128)(2,1)S(1)}, bf16[64,2048]{1,0:T(8,128)(2,1)S(1)}, u32[]{:S(2)}, u32[]{:S(2)}) %collective-permute-start.2) | collective-permute-done | bytes 262176 | tf_op jit(solution)/shard_map/ppermute | solution.py:31
  60.1 5.3 %fusion.14 = f32[320,2560]{1,0:T(8,128)S(1)} fusion(f32[320,2560]{1,0:T(8,128)S(1)} %copy-done.5, bf16[320,1280]{1,0:T(8,128)(2,1)S(1)} %pad_maximum_fusion, bf16[1,2560,4096]{2,1,0:T(8,128)(2,1)} %param.14, s32[]{:T(128)S(6)} %select_n.195), kind=kOutput, calls=%fused_computation.16 | convolution fusion | flops 2097971200 | bytes 13926404 | tf_op jit(solution)/shard_map/dot_general | solution.py:182
  66.7 3.8 %convolution_add_fusion.1 = f32[320,2560]{1,0:T(8,128)S(1)} fusion(f32[320,2560]{1,0:T(8,128)S(1)} %fusion.14, bf16[1,2560,4096]{2,1,0:T(8,128)(2,1)} %param.14, s32[]{:T(128)S(6)} %select_n.196, bf16[320,384]{1,0:T(8,128)(2,1)S(1)} %convolution_convert_fusion.8, bf16[320,384]{1,0:T(8,128)(2,1)S(1)} %convolution_convert_fusion.9), kind=kOutput, calls=%fused_computation.19 | convolution fusion | flops 1260093440 | bytes 10977284 | tf_op jit(solution)/shard_map/dot_general | solution.py:182
  71.7 3.8 %fusion.18 = bf16[320,2560]{1,0:T(8,128)(2,1)S(1)} fusion(f32[320,2560]{1,0:T(8,128)S(1)} %copy-done.3, f32[320,2560]{1,0:T(8,128)S(1)} %convolution_add_fusion.1, bf16[1,2560,4096]{2,1,0:T(8,128)(2,1)} %param.14, s32[]{:T(128)S(6)} %select_n.197, bf16[320,384]{1,0:T(8,128)(2,1)S(1)} %convolution_convert_fusion.6, ...), kind=kOutput, calls=%fused_computation.20 | convolution fusion | flops 1261731840 | bytes 12615684 | tf_op jit(solution)/shard_map/dot_general | solution.py:182
  75.6 1.5 %fusion.41 = bf16[320,768]{1,0:T(8,128)(2,1)S(1)} fusion(bf16[320,2560]{1,0:T(8,128)(2,1)S(1)} %fusion.18, bf16[1,4096,2560]{2,1,0:T(8,128)(2,1)S(1)} %bitcast.70, s32[]{:T(128)S(6)} %select_n.197), kind=kOutput, calls=%fused_computation.46 | convolution fusion | flops 1258536960 | bytes 6062084 | tf_op jit(solution)/shard_map/dot_general | solution.py:182
  79.6 3.4 %fusion.36 = bf16[320,1280]{1,0:T(8,128)(2,1)} fusion(bf16[320,2560]{1,0:T(8,128)(2,1)S(1)} %fusion.18, bf16[1,4096,2560]{2,1,0:T(8,128)(2,1)S(1)} %bitcast.70, s32[]{:T(128)S(6)} %select_n.195), kind=kOutput, calls=%fused_computation.36 | convolution fusion | flops 2097561600 | bytes 9011204 | tf_op jit(solution)/shard_map/dot_general | solution.py:182
  83.0 1.5 %collective-permute-start.7 = (bf16[32,2048]{1,0:T(8,128)(2,1)S(1)}, bf16[32,2048]{1,0:T(8,128)(2,1)S(1)}, u32[]{:S(2)}, u32[]{:S(2)}) collective-permute-start(bf16[32,2048]{1,0:T(8,128)(2,1)S(1)} %pad_maximum_fusion.4), channel_id=1, source_target_pairs={{0,8},{2,10},{4,12},{6,14},{8,0},{10,2},{12,4},{14,6},{16,24},{18,... | collective-permute-start | bytes 393224 | tf_op jit(solution)/shard_map/ppermute | solution.py:31
  84.5 1.5 %fusion.19 = f32[320,768]{1,0:T(8,128)S(1)} fusion(bf16[320,2560]{1,0:T(8,128)(2,1)S(1)} %fusion.18, bf16[1,4096,2560]{2,1,0:T(8,128)(2,1)S(1)} %bitcast.70, s32[]{:T(128)S(6)} %select_n.196), kind=kOutput, calls=%fused_computation.21 | convolution fusion | flops 1258291200 | bytes 6553604 | tf_op jit(solution)/shard_map/dot_general | solution.py:182
  86.0 1.3 collective-permute-done.7
  89.2 1.4 collective-permute-start.9
  91.8 9.4 %all-to-all-start.2 = ((bf16[16,40,384]{2,1,0:T(8,128)(2,1)}), bf16[16,40,384]{2,1,0:T(8,128)(2,1)}, u32[]{:S(2)}, u32[]{:S(2)}) async-start(bf16[16,40,384]{2,1,0:T(8,128)(2,1)} %bitcast.15), calls=%async_computation.2 | async-start | bytes 983040 | tf_op jit(solution)/shard_map/all_to_all | solution.py:179
  103.1 5.2 %fusion.2 = f32[320,1280]{1,0:T(8,128)S(1)} fusion(bf16[320,2560]{1,0:T(8,128)(2,1)S(1)} %fusion.18, bf16[1,4096,2560]{2,1,0:T(8,128)(2,1)} %param.13, s32[]{:T(128)S(6)} %select_n.188), kind=kOutput, calls=%fused_computation.2 | convolution fusion | flops 2097152000 | bytes 9830404 | tf_op jit(solution)/shard_map/dot_general | solution.py:182
  109.1 1.5 %add_convert_fusion = bf16[640,640]{1,0:T(8,128)(2,1)} fusion(f32[640,640]{1,0:T(8,128)S(1)} %fusion.44, s32[320]{0:T(512)S(1)} %get-tuple-element.45, bf16[320,1280]{1,0:T(8,128)(2,1)S(1)} %add_convert_fusion.1), kind=kOutput, calls=%fused_computation.38 | convolution fusion | flops 263168000 | bytes 2869248 | tf_op jit(solution)/shard_map/dot_general | solution.py:79
  110.6 4.2 %all-to-all-done.2 = bf16[16,40,384]{2,1,0:T(8,128)(2,1)} async-done(((bf16[16,40,384]{2,1,0:T(8,128)(2,1)}), bf16[16,40,384]{2,1,0:T(8,128)(2,1)}, u32[]{:S(2)}, u32[]{:S(2)}) %all-to-all-start.2) | async-done | bytes 491552 | tf_op jit(solution)/shard_map/all_to_all | solution.py:179
  114.8 4.4 %all-to-all-start.3 = ((bf16[16,40,640]{2,1,0:T(8,128)(2,1)}), bf16[16,40,640]{2,1,0:T(8,128)(2,1)S(1)}, u32[]{:S(2)}, u32[]{:S(2)}) async-start(bf16[16,40,640]{2,1,0:T(8,128)(2,1)} %bitcast.17), calls=%async_computation.3 | async-start | bytes 1638400 | tf_op jit(solution)/shard_map/all_to_all | solution.py:179
  119.8 1.5 %convolution_convert_fusion.10 = bf16[256,384]{1,0:T(8,128)(2,1)S(1)} fusion(bf16[640,384]{1,0:T(8,128)(2,1)} %bitcast.16, pred[640,512]{1,0:T(32,128)(4,1)S(1)} %iota_compare_fusion), kind=kOutput, calls=%fused_computation.55 | convolution fusion | flops 125927424 | bytes 851968 | tf_op jit(solution)/shard_map/dot_general | solution.py:185
  121.3 1.5 %convolution_convert_fusion.11 = bf16[256,384]{1,0:T(8,128)(2,1)S(1)} fusion(bf16[640,384]{1,0:T(8,128)(2,1)} %bitcast.16, pred[640,512]{1,0:T(32,128)(4,1)S(1)} %iota_compare_fusion), kind=kOutput, calls=%fused_computation.56 | convolution fusion | flops 125927424 | bytes 851968 | tf_op jit(solution)/shard_map/dot_general | solution.py:185
  124.9 1.6 %maximum_convert_fusion = f32[256,2048]{1,0:T(8,128)} fusion(bf16[128,2048]{1,0:T(8,128)(2,1)S(1)} %get-tuple-element.31, bf16[128,2048]{1,0:T(8,128)(2,1)S(1)} %get-tuple-element.30), kind=kLoop, calls=%fused_computation.57 | loop fusion | flops 2097152 | bytes 3145728 | tf_op jit(solution)/shard_map/convert_element_type | solution.py:71
  126.4 13.0 %all-to-all-done.3 = bf16[16,40,640]{2,1,0:T(8,128)(2,1)S(1)} async-done(((bf16[16,40,640]{2,1,0:T(8,128)(2,1)}), bf16[16,40,640]{2,1,0:T(8,128)(2,1)S(1)}, u32[]{:S(2)}, u32[]{:S(2)}) %all-to-all-start.3) | async-done | bytes 819232 | tf_op jit(solution)/shard_map/all_to_all | solution.py:179
  140.4 2.0 %shard_map.95 = bf16[256,2048]{1,0:T(8,128)(2,1)} custom-call(s32[2,256]{1,0:T(2,128)S(1)} %reshape.64.columns_ref, bf16[640,640]{1,0:T(8,128)(2,1)S(1)} %bitcast.62, bf16[256,768]{1,0:T(8,128)(2,1)S(1)} %copy-done.2), custom_call_target="tpu_custom_call" | custom-call | tf_op jit(solution)/shard_map/pallas_call | solution.py:132
  (78 shorter events, 22.9 us)
Async XLA Ops:
  0.6 10.4 %copy-start = (bf16[1,320,4096]{2,1,0:T(8,128)(2,1)S(1)}, bf16[1,320,4096]{2,1,0:T(8,128)(2,1)}, u32[]{:S(2)}) copy-start(bf16[1,320,4096]{2,1,0:T(8,128)(2,1)} %param.12) | copy-start | bytes 7864324
  4.4 26.8 %all-to-all-start = ((bf16[16,40,640]{2,1,0:T(8,128)(2,1)}), bf16[16,40,640]{2,1,0:T(8,128)(2,1)S(1)}, u32[]{:S(2)}, u32[]{:S(2)}) async-start(bf16[16,40,640]{2,1,0:T(8,128)(2,1)} %bitcast.68), calls=%async_computation | async-start | bytes 1638400 | tf_op jit(solution)/shard_map/all_to_all | solution.py:179
  11.0 15.6 %copy-start.4 = (f32[256]{0:T(256)S(1)}, f32[256]{0:T(256)}, u32[]{:S(2)}) copy-start(f32[256]{0:T(256)} %param.10) | copy-start | bytes 3076
  26.2 2.9 %collective-permute-start.1 = (bf16[128,2048]{1,0:T(8,128)(2,1)S(1)}, bf16[128,2048]{1,0:T(8,128)(2,1)S(1)}, u32[]{:S(2)}, u32[]{:S(2)}) collective-permute-start(bf16[128,2048]{1,0:T(8,128)(2,1)S(1)} %select_convert_fusion), channel_id=1, source_target_pairs={{0,2},{2,0},{4,6},{6,4},{8,10},{10,8},{12,14},{14,12},{16,18},{18,... | collective-permute-start | bytes 1572872 | tf_op jit(solution)/shard_map/ppermute | solution.py:31
  31.2 20.0 %collective-permute-start = (bf16[640,640]{1,0:T(8,128)(2,1)S(1)}, bf16[640,640]{1,0:T(8,128)(2,1)S(1)}, u32[]{:S(2)}, u32[]{:S(2)}) collective-permute-start(bf16[640,640]{1,0:T(8,128)(2,1)S(1)} %bitcast.65), channel_id=1, source_target_pairs={{0,1},{1,0},{2,3},{3,2},{4,5},{5,4},{6,7},{7,6},{8,9},{9,8},{10,11... | collective-permute-start | bytes 2457608 | tf_op jit(solution)/shard_map/ppermute | solution.py:31
  32.5 20.1 %all-to-all-start.1 = ((bf16[16,40,384]{2,1,0:T(8,128)(2,1)}), bf16[16,40,384]{2,1,0:T(8,128)(2,1)}, u32[]{:S(2)}, u32[]{:S(2)}) async-start(bf16[16,40,384]{2,1,0:T(8,128)(2,1)} %bitcast.6), calls=%async_computation.1 | async-start | bytes 983040 | tf_op jit(solution)/shard_map/all_to_all | solution.py:179
  52.6 7.6 %copy-start.5 = (f32[320,2560]{1,0:T(8,128)S(1)}, f32[320,2560]{1,0:T(8,128)}, u32[]{:S(2)}) copy-start(f32[320,2560]{1,0:T(8,128)} %fusion.8) | copy-start | bytes 9830404
  52.6 7.3 %collective-permute-start.2 = (bf16[64,2048]{1,0:T(8,128)(2,1)S(1)}, bf16[64,2048]{1,0:T(8,128)(2,1)S(1)}, u32[]{:S(2)}, u32[]{:S(2)}) collective-permute-start(bf16[64,2048]{1,0:T(8,128)(2,1)S(1)} %select_convert_fusion.1), channel_id=1, source_target_pairs={{0,4},{2,6},{4,0},{6,2},{8,12},{10,14},{12,8},{14,10},{16,20},{18,... | collective-permute-start | bytes 786440 | tf_op jit(solution)/shard_map/ppermute | solution.py:31
  55.1 15.4 %collective-permute-start.3 = (bf16[640,384]{1,0:T(8,128)(2,1)}, bf16[640,384]{1,0:T(8,128)(2,1)S(1)}, u32[]{:S(2)}, u32[]{:S(2)}) collective-permute-start(bf16[640,384]{1,0:T(8,128)(2,1)} %bitcast.7), channel_id=1, source_target_pairs={{0,1},{1,0},{2,3},{3,2},{4,5},{5,4},{6,7},{7,6},{8,9},{9,8},{10,11... | collective-permute-start | bytes 1474568 | tf_op jit(solution)/shard_map/ppermute | solution.py:31
  60.0 5.5 %collective-permute-start.4 = (bf16[32,2048]{1,0:T(8,128)(2,1)S(1)}, bf16[32,2048]{1,0:T(8,128)(2,1)S(1)}, u32[]{:S(2)}, u32[]{:S(2)}) collective-permute-start(bf16[32,2048]{1,0:T(8,128)(2,1)S(1)} %select_convert_fusion.2), channel_id=1, source_target_pairs={{0,8},{2,10},{4,12},{6,14},{8,0},{10,2},{12,4},{14,6},{16,24},{18,... | collective-permute-start | bytes 393224 | tf_op jit(solution)/shard_map/ppermute | solution.py:31
  60.1 15.4 %slice-start = ((s8[20971520]{0:T(1024)(128)(4,1)}), s8[4194304]{0:T(1024)(128)(4,1)S(1)}, s32[]{:S(2)}) async-start(s8[20971520]{0:T(1024)(128)(4,1)} %bitcast.69), calls=%async_computation.4 | async-start | bytes 8388608
  60.1 15.4 %slice-start.1 = ((s8[20971520]{0:T(1024)(128)(4,1)}), s8[4194304]{0:T(1024)(128)(4,1)S(1)}, s32[]{:S(2)}) async-start(s8[20971520]{0:T(1024)(128)(4,1)} %bitcast.69), calls=%async_computation.5 | async-start | bytes 8388608
  60.1 15.4 %slice-start.2 = ((s8[20971520]{0:T(1024)(128)(4,1)}), s8[4194304]{0:T(1024)(128)(4,1)S(1)}, s32[]{:S(2)}) async-start(s8[20971520]{0:T(1024)(128)(4,1)} %bitcast.69), calls=%async_computation.6 | async-start | bytes 8388608
  65.6 9.9 %slice-start.3 = ((s8[20971520]{0:T(1024)(128)(4,1)}), s8[4194304]{0:T(1024)(128)(4,1)S(1)}, s32[]{:S(2)}) async-start(s8[20971520]{0:T(1024)(128)(4,1)} %bitcast.69), calls=%async_computation.7 | async-start | bytes 8388608
  65.6 4.9 %collective-permute-start.5 = (bf16[16,2048]{1,0:T(8,128)(2,1)S(1)}, bf16[16,2048]{1,0:T(8,128)(2,1)S(1)}, u32[]{:S(2)}, u32[]{:S(2)}) collective-permute-start(bf16[16,2048]{1,0:T(8,128)(2,1)S(1)} %select_convert_fusion.3), channel_id=1, source_target_pairs={{0,16},{2,18},{4,20},{6,22},{8,24},{10,26},{12,28},{14,30},{16,0},... | collective-permute-start | bytes 196616 | tf_op jit(solution)/shard_map/ppermute | solution.py:31
  66.7 4.9 %copy-start.3 = (f32[320,2560]{1,0:T(8,128)S(1)}, f32[320,2560]{1,0:T(8,128)}, u32[]{:S(2)}) copy-start(f32[320,2560]{1,0:T(8,128)} %fusion.33) | copy-start | bytes 9830404
  71.7 3.9 %slice-start.4 = ((s8[20971520]{0:T(1024)(128)(4,1)}), s8[4194304]{0:T(1024)(128)(4,1)S(1)}, s32[]{:S(2)}) async-start(s8[20971520]{0:T(1024)(128)(4,1)} %bitcast.69), calls=%async_computation.8 | async-start | bytes 8388608
  77.0 10.4 %collective-permute-start.8 = (bf16[320,768]{1,0:T(8,128)(2,1)S(1)}, bf16[320,768]{1,0:T(8,128)(2,1)S(1)}, u32[]{:S(2)}, u32[]{:S(2)}) collective-permute-start(bf16[320,768]{1,0:T(8,128)(2,1)S(1)} %fusion.41), channel_id=1, source_target_pairs={{0,1},{1,0},{2,3},{3,2},{4,5},{5,4},{6,7},{7,6},{8,9},{9,8},{10,11... | collective-permute-start | bytes 1474568 | tf_op jit(solution)/shard_map/ppermute | solution.py:31
  78.3 4.7 %collective-permute-start.6 = (bf16[16,2048]{1,0:T(8,128)(2,1)S(1)}, bf16[16,2048]{1,0:T(8,128)(2,1)S(1)}, u32[]{:S(2)}, u32[]{:S(2)}) collective-permute-start(bf16[16,2048]{1,0:T(8,128)(2,1)S(1)} %add_convert_fusion.3), channel_id=1, source_target_pairs={{0,16},{2,18},{4,20},{6,22},{8,24},{10,26},{12,28},{14,30},{16,0},... | collective-permute-start | bytes 196616 | tf_op jit(solution)/shard_map/ppermute | solution.py:31
  83.0 4.3 %collective-permute-start.7 = (bf16[32,2048]{1,0:T(8,128)(2,1)S(1)}, bf16[32,2048]{1,0:T(8,128)(2,1)S(1)}, u32[]{:S(2)}, u32[]{:S(2)}) collective-permute-start(bf16[32,2048]{1,0:T(8,128)(2,1)S(1)} %pad_maximum_fusion.4), channel_id=1, source_target_pairs={{0,8},{2,10},{4,12},{6,14},{8,0},{10,2},{12,4},{14,6},{16,24},{18,... | collective-permute-start | bytes 393224 | tf_op jit(solution)/shard_map/ppermute | solution.py:31
  89.2 12.0 %collective-permute-start.9 = (bf16[64,2048]{1,0:T(8,128)(2,1)S(1)}, bf16[64,2048]{1,0:T(8,128)(2,1)}, u32[]{:S(2)}, u32[]{:S(2)}) collective-permute-start(bf16[64,2048]{1,0:T(8,128)(2,1)S(1)} %pad_maximum_fusion.3), channel_id=1, source_target_pairs={{0,4},{2,6},{4,0},{6,2},{8,12},{10,14},{12,8},{14,10},{16,20},{18,... | collective-permute-start | bytes 786440 | tf_op jit(solution)/shard_map/ppermute | solution.py:31
  90.6 17.7 %collective-permute-start.10 = (bf16[320,1280]{1,0:T(8,128)(2,1)}, bf16[320,1280]{1,0:T(8,128)(2,1)S(1)}, u32[]{:S(2)}, u32[]{:S(2)}) collective-permute-start(bf16[320,1280]{1,0:T(8,128)(2,1)} %fusion.36), channel_id=1, source_target_pairs={{0,1},{1,0},{2,3},{3,2},{4,5},{5,4},{6,7},{7,6},{8,9},{9,8},{10,11... | collective-permute-start | bytes 2457608 | tf_op jit(solution)/shard_map/ppermute | solution.py:31
  91.8 23.0 %all-to-all-start.2 = ((bf16[16,40,384]{2,1,0:T(8,128)(2,1)}), bf16[16,40,384]{2,1,0:T(8,128)(2,1)}, u32[]{:S(2)}, u32[]{:S(2)}) async-start(bf16[16,40,384]{2,1,0:T(8,128)(2,1)} %bitcast.15), calls=%async_computation.2 | async-start | bytes 983040 | tf_op jit(solution)/shard_map/all_to_all | solution.py:179
  114.8 24.6 %all-to-all-start.3 = ((bf16[16,40,640]{2,1,0:T(8,128)(2,1)}), bf16[16,40,640]{2,1,0:T(8,128)(2,1)S(1)}, u32[]{:S(2)}, u32[]{:S(2)}) async-start(bf16[16,40,640]{2,1,0:T(8,128)(2,1)} %bitcast.17), calls=%async_computation.3 | async-start | bytes 1638400 | tf_op jit(solution)/shard_map/all_to_all | solution.py:179
  119.4 4.2 %collective-permute-start.11 = (bf16[128,2048]{1,0:T(8,128)(2,1)}, bf16[128,2048]{1,0:T(8,128)(2,1)S(1)}, u32[]{:S(2)}, u32[]{:S(2)}) collective-permute-start(bf16[128,2048]{1,0:T(8,128)(2,1)} %pad_maximum_fusion.1), channel_id=1, source_target_pairs={{0,2},{2,0},{4,6},{6,4},{8,10},{10,8},{12,14},{14,12},{16,18},{18,... | collective-permute-start | bytes 1572872 | tf_op jit(solution)/shard_map/ppermute | solution.py:31
  122.8 19.6 %copy-start.1 = (bf16[1,320,4096]{2,1,0:T(8,128)(2,1)S(1)}, bf16[1,320,4096]{2,1,0:T(8,128)(2,1)}, u32[]{:S(2)}) copy-start(bf16[1,320,4096]{2,1,0:T(8,128)(2,1)} %param.12) | copy-start | bytes 7864324
  139.4 1.0 copy-start.2
